TPU v7x, 256 devices: a whole 4x4x8 slice. The times are simulated.
256 devices in a mesh: ctx: 32 (over y, z_hi, x), head: 8 (over z_lo, core).
Axes of the slice: x: 4, y: 4, z: 8 (z_hi: 2, z_lo: 4; z = z_hi * 4 + z_lo), core: 2. Of those that a mesh axis runs over, the one named last changes fastest.
Arguments:
- window_input: bfloat16 [32, 2048, 768], P('head', 'ctx'), may hold values from -256 to 256
- norm_gain: float32 [768], replicated, may hold values from 0.25 to 1.75
- w_query: bfloat16 [768, 512], replicated, may hold values from -1 to 1
- w_key: bfloat16 [768, 512], replicated, may hold values from -1 to 1
- w_value: bfloat16 [768, 768], replicated, may hold values from -0.21875 to 0.21875
- w_out: bfloat16 [768, 768], replicated, may hold values from -0.21875 to 0.21875
- conv_weight: bfloat16 [2, 3, 768, 384], replicated, may hold values from -0.125 to 0.125
- point_weight: bfloat16 [2, 384, 768], replicated, may hold values from -0.3125 to 0.3125
- dilations: int32 [2], replicated, may hold values from 1 to 16, as said below
- tangent_query: bfloat16 [768, 512], replicated, may hold values from -0.21875 to 0.21875
- tangent_key: bfloat16 [768, 512], replicated, may hold values from -0.21875 to 0.21875
- curvature: float32 [32, 2048], P('head', 'ctx'), may hold values from 0.25 to 4
Outputs:
- output_tangent: bfloat16 [32, 2048, 768], P('head', 'ctx')
- input_cotangent: bfloat16 [32, 2048, 768], P('head', 'ctx')
- gv_query: float32 [768, 512], P(('ctx', 'head'))
- gv_key: float32 [768, 512], P(('ctx', 'head'))
Inputs may be any that keep to these rules, and one draw needn't show every extreme that they name: At least one of the two dilations equals 16.
All inputs are finite; a program needn't handle non-finite values.
Results may differ from a plain program's by a relative error of at most 0.015.
The roundings to bfloat16 on the way count: a program that leaves them out, or rounds other values in their place, can miss the bound.
Values may be sent and summed in bfloat16 or wider, within the bound.
A program may use at most 128 MiB of HBM per device.

v0:
```python
import math

import jax
import jax.numpy as jnp
from jax import lax
from jax.sharding import PartitionSpec as P

HEADS = 8
KEY = 64
DMAX = 16


def extended(cells, sides, width):
    for axis, dim in sides:
        count = lax.axis_size(axis)
        ends = count - 1
        head = lax.slice_in_dim(cells, 0, width, axis=dim)
        tail = lax.slice_in_dim(cells, cells.shape[dim] - width, cells.shape[dim], axis=dim)
        cells = jnp.concatenate(
            [
                lax.ppermute(tail, axis, [(i, (i + 1) % count) for i in range(ends)]),
                cells,
                lax.ppermute(head, axis, [((i + 1) % count, i) for i in range(ends)]),
            ],
            axis=dim,
        )
    return cells


def gelu_pair(values):
    return jax.jvp(jax.nn.gelu, (values,), (jnp.ones_like(values),))


def to_items(row_form):
    groups = lax.axis_size("ctx")
    moved = lax.all_to_all(row_form, "head", split_axis=1, concat_axis=0, tiled=True)
    merged = moved.reshape((groups, moved.shape[2], moved.shape[3]))
    final = lax.all_to_all(merged, "ctx", split_axis=0, concat_axis=1, tiled=True)
    return final.reshape((final.shape[1], final.shape[2]))


def to_rows(item_form, seqs_local, head_count):
    widened = item_form.reshape((1, item_form.shape[0], item_form.shape[1]))
    arrived = lax.all_to_all(widened, "ctx", split_axis=1, concat_axis=0, tiled=True)
    members = lax.axis_size("head")
    grouped = arrived.reshape(
        (seqs_local * members, head_count // members, arrived.shape[1], arrived.shape[2])
    )
    return lax.all_to_all(grouped, "head", split_axis=0, concat_axis=1, tiled=True)


def attend_forward(queries, key_rows, value_rows, tangent_queries, tangent_keys):
    length = queries.shape[0]
    val_size = value_rows.shape[1]
    block_size = math.gcd(length, 512)
    score_scale = KEY ** (-0.5)

    def one_block(operands):
        part_queries, part_tangents = operands
        scores = (
            jnp.einsum("qd,kd->qk", part_queries, key_rows, preferred_element_type=jnp.float32)
            * score_scale
        )
        weights = jax.nn.softmax(scores, axis=-1)
        attended = jnp.einsum(
            "qk,kd->qd",
            weights.astype(jnp.bfloat16),
            value_rows,
            preferred_element_type=jnp.float32,
        ).astype(jnp.bfloat16)
        tangent_scores = (
            jnp.einsum("qd,kd->qk", part_tangents, key_rows, preferred_element_type=jnp.float32)
            + jnp.einsum(
                "qd,kd->qk", part_queries, tangent_keys, preferred_element_type=jnp.float32
            )
        ) * score_scale
        tangent_weights = weights * (
            tangent_scores - jnp.sum(weights * tangent_scores, axis=-1, keepdims=True)
        )
        tangent_attended = jnp.einsum(
            "qk,kd->qd",
            tangent_weights.astype(jnp.bfloat16),
            value_rows,
            preferred_element_type=jnp.float32,
        ).astype(jnp.bfloat16)
        return jnp.concatenate([attended, tangent_attended], axis=1)

    blocks = lax.map(
        one_block,
        (
            queries.reshape((length // block_size, block_size, KEY)),
            tangent_queries.reshape((length // block_size, block_size, KEY)),
        ),
    )
    return blocks.reshape((length, 2 * val_size))


def attend_backward(queries, key_rows, value_rows, grad_attended):
    length = queries.shape[0]
    val_size = value_rows.shape[1]
    block_size = math.gcd(length, 512)
    score_scale = KEY ** (-0.5)

    def one_block(carry, operands):
        acc_keys, acc_values = carry
        part_queries, part_grads = operands
        scores = (
            jnp.einsum("qd,kd->qk", part_queries, key_rows, preferred_element_type=jnp.float32)
            * score_scale
        )
        weights = jax.nn.softmax(scores, axis=-1)
        grad_weights = jnp.einsum(
            "qd,kd->qk", part_grads, value_rows, preferred_element_type=jnp.float32
        )
        grad_scores = (
            weights
            * (grad_weights - jnp.sum(weights * grad_weights, axis=-1, keepdims=True))
            * score_scale
        ).astype(jnp.bfloat16)
        grad_queries = jnp.einsum(
            "qk,kd->qd", grad_scores, key_rows, preferred_element_type=jnp.float32
        ).astype(jnp.bfloat16)
        acc_keys = acc_keys + jnp.einsum(
            "qk,qd->kd", grad_scores, part_queries, preferred_element_type=jnp.float32
        )
        acc_values = acc_values + jnp.einsum(
            "qk,qd->kd",
            weights.astype(jnp.bfloat16),
            part_grads,
            preferred_element_type=jnp.float32,
        )
        return ((acc_keys, acc_values), grad_queries)

    initial = (jnp.zeros((length, KEY), jnp.float32), jnp.zeros((length, val_size), jnp.float32))
    (acc_keys, acc_values), grad_queries = lax.scan(
        one_block,
        initial,
        (
            queries.reshape((length // block_size, block_size, KEY)),
            grad_attended.reshape((length // block_size, block_size, val_size)),
        ),
    )
    return jnp.concatenate(
        [
            grad_queries.reshape((length, KEY)),
            acc_keys.astype(jnp.bfloat16),
            acc_values.astype(jnp.bfloat16),
        ],
        axis=1,
    )


def conv_forward(padded, kernels, dilation, bins_local):
    summed = None
    for tap_index in range(3):
        window = lax.dynamic_slice_in_dim(padded, DMAX + (tap_index - 1) * dilation, bins_local, 2)
        contrib = jnp.einsum(
            "sblc,cf->sblf", window, kernels[tap_index], preferred_element_type=jnp.float32
        )
        summed = contrib if summed is None else summed + contrib
    return summed


def conv_backward(padded, kernels, dilation, bins_local):
    summed = None
    for tap_index in range(3):
        window = lax.dynamic_slice_in_dim(padded, DMAX - (tap_index - 1) * dilation, bins_local, 1)
        contrib = jnp.einsum(
            "blf,cf->blc", window, kernels[tap_index], preferred_element_type=jnp.float32
        )
        summed = contrib if summed is None else summed + contrib
    return summed


def per_device(
    window_input,
    norm_gain,
    w_query,
    w_key,
    w_value,
    w_out,
    conv_weight,
    point_weight,
    dilations,
    tangent_query,
    tangent_key,
    curvature,
):
    seqs_local, bins_local, features = window_input.shape
    head_count = HEADS
    val_size = w_value.shape[1] // head_count
    inputs = window_input.astype(jnp.float32)
    spread = jnp.sqrt(jnp.mean(inputs * inputs, axis=-1, keepdims=True) + 1e-06)
    normed = (inputs / spread * norm_gain).astype(jnp.bfloat16)
    joined = jnp.concatenate(
        [
            w_query.reshape((features, head_count, KEY)),
            w_key.reshape((features, head_count, KEY)),
            w_value.reshape((features, head_count, val_size)),
            tangent_query.reshape((features, head_count, KEY)),
            tangent_key.reshape((features, head_count, KEY)),
        ],
        axis=2,
    )
    projected = jnp.einsum(
        "blc,chd->bhld", normed, joined, preferred_element_type=jnp.float32
    ).astype(jnp.bfloat16)
    item_rows = to_items(projected)
    queries = item_rows[:, :KEY]
    key_rows = item_rows[:, KEY : 2 * KEY]
    value_rows = item_rows[:, 2 * KEY : 2 * KEY + val_size]
    tangent_queries = item_rows[:, 2 * KEY + val_size : 3 * KEY + val_size]
    tangent_keys = item_rows[:, 3 * KEY + val_size :]
    attended = to_rows(
        attend_forward(queries, key_rows, value_rows, tangent_queries, tangent_keys),
        seqs_local,
        head_count,
    )
    out_weight = w_out.reshape((head_count, val_size, features))
    mixed = inputs + jnp.einsum(
        "bhlv,hvc->blc", attended[..., :val_size], out_weight, preferred_element_type=jnp.float32
    )
    tangent_mixed = jnp.einsum(
        "bhlv,hvc->blc", attended[..., val_size:], out_weight, preferred_element_type=jnp.float32
    )
    slopes = []
    for layer_index in range(2):
        dilation = dilations[layer_index]
        activated, act_slope = gelu_pair(mixed)
        stacked = jnp.stack(
            [activated.astype(jnp.bfloat16), (act_slope * tangent_mixed).astype(jnp.bfloat16)]
        )
        padded = extended(stacked, (("ctx", 2),), DMAX)
        inner_pair = conv_forward(padded, conv_weight[layer_index], dilation, bins_local)
        hidden_value, hidden_slope = gelu_pair(inner_pair[0])
        hidden_pair = jnp.stack(
            [hidden_value.astype(jnp.bfloat16), (hidden_slope * inner_pair[1]).astype(jnp.bfloat16)]
        )
        pointwise = jnp.einsum(
            "sblf,fc->sblc",
            hidden_pair,
            point_weight[layer_index],
            preferred_element_type=jnp.float32,
        )
        mixed = mixed + pointwise[0]
        tangent_mixed = tangent_mixed + pointwise[1]
        slopes.append((act_slope, hidden_slope, dilation))
    output_tangent = tangent_mixed.astype(jnp.bfloat16)
    gradient = curvature[..., None] * tangent_mixed
    for layer_index in (1, 0):
        act_slope, hidden_slope, dilation = slopes[layer_index]
        grad_inner = (
            jnp.einsum(
                "blc,fc->blf",
                gradient.astype(jnp.bfloat16),
                point_weight[layer_index],
                preferred_element_type=jnp.float32,
            )
            * hidden_slope
        ).astype(jnp.bfloat16)
        grad_pad = extended(grad_inner, (("ctx", 1),), DMAX)
        gradient = (
            gradient
            + conv_backward(grad_pad, conv_weight[layer_index], dilation, bins_local) * act_slope
        )
    grad_attended = jnp.einsum(
        "blc,hvc->bhlv",
        gradient.astype(jnp.bfloat16),
        out_weight,
        preferred_element_type=jnp.float32,
    ).astype(jnp.bfloat16)
    grad_items = to_items(grad_attended)
    grads_rows = to_rows(
        attend_backward(queries, key_rows, value_rows, grad_items), seqs_local, head_count
    )
    pair_grads = grads_rows[..., : 2 * KEY]
    shard_rows = features // lax.axis_size(("ctx", "head"))
    tokens = float(seqs_local * lax.axis_size("head") * bins_local * lax.axis_size("ctx"))
    summed_all = lax.psum(
        jnp.einsum("blc,bhld->chd", normed, pair_grads, preferred_element_type=jnp.float32),
        ("ctx", "head"),
    )
    summed = lax.dynamic_slice_in_dim(
        summed_all, lax.axis_index(("ctx", "head")) * shard_rows, shard_rows, 0
    )
    summed = summed / tokens
    gv_query = summed[:, :, :KEY].reshape((shard_rows, head_count * KEY))
    gv_key = summed[:, :, KEY:].reshape((shard_rows, head_count * KEY))
    grad_normed = jnp.einsum(
        "bhld,chd->blc",
        grads_rows,
        joined[:, :, : 2 * KEY + val_size],
        preferred_element_type=jnp.float32,
    )
    gained = grad_normed * norm_gain
    input_cotangent = (
        gradient
        + gained / spread
        - inputs
        * jnp.sum(gained * inputs, axis=-1, keepdims=True)
        / (features * spread * spread * spread)
    )
    return (output_tangent, input_cotangent.astype(jnp.bfloat16), gv_query, gv_key)


def solution(mesh):
    in_specs = (
        P("head", "ctx", None),
        P(),
        P(),
        P(),
        P(),
        P(),
        P(),
        P(),
        P(),
        P(),
        P(),
        P("head", "ctx"),
    )
    out_specs = (
        P("head", "ctx", None),
        P("head", "ctx", None),
        P(("ctx", "head"), None),
        P(("ctx", "head"), None),
    )
    return jax.shard_map(
        per_device, mesh=mesh, in_specs=in_specs, out_specs=out_specs, check_vma=False
    )
```

profile of v0, /device:TPU:2, one launch (start us, length us, event | category | flops | bytes accessed | tf_op | source)
XLA Modules:
  0.0 797.2 jit_solution(11856558198745252623)
XLA Ops:
  23.1 3.7 fusion.55
  26.8 43.6 %all_to_all.102 = bf16[4,8,64,352]{3,2,0,1:T(8,128)(2,1)} all-to-all(bf16[4,8,64,352]{3,2,0,1:T(8,128)(2,1)S(1)} %fusion.55), channel_id=1, replica_groups=mesh['ctx'=32,'head'=8] {'head'}, dimensions={1} | all-to-all | bytes 2883584 | tf_op jit(solution)/shard_map/all_to_all | solution.py:36
  70.5 12.2 %all-to-all-start.1 = ((bf16[32,64,352]{2,1,0:T(8,128)(2,1)}), bf16[32,64,352]{2,1,0:T(8,128)(2,1)S(1)}, u32[]{:S(2)}, u32[]{:S(2)}) async-start(bf16[32,64,352]{2,1,0:T(8,128)(2,1)} %bitcast.336), calls=%async_computation.1 | async-start | bytes 3145728 | tf_op jit(solution)/shard_map/all_to_all | solution.py:38
  82.6 40.0 %all-to-all-done.1 = bf16[32,64,352]{2,1,0:T(8,128)(2,1)S(1)} async-done(((bf16[32,64,352]{2,1,0:T(8,128)(2,1)}), bf16[32,64,352]{2,1,0:T(8,128)(2,1)S(1)}, u32[]{:S(2)}, u32[]{:S(2)}) %all-to-all-start.1) | async-done | bytes 1441824 | tf_op jit(solution)/shard_map/all_to_all | solution.py:38
  125.2 51.5 %while.25 = (s32[]{:T(128)}, bf16[4,512,192]{1,2,0:T(8,128)(2,1)}, bf16[4,512,64]{2,1,0:T(8,128)(2,1)}, bf16[2048,64]{1,0:T(8,128)(2,1)}, bf16[2048,96]{1,0:T(8,...) while((s32[]{:T(128)}, bf16[4,512,192]{1,2,0:T(8,128)(2,1)}, ...), condition=%wide.region_5.6_spmd, body=%wide.region_1.5_spmd.sunk | while | flops 828865024 | bytes 41638024 | solution.py:88
  129.7 2.9 multiply_reduce_fusion.9
  142.6 2.9 multiply_reduce_fusion.9
  155.5 2.9 multiply_reduce_fusion.9
  168.4 2.9 multiply_reduce_fusion.9
  179.0 6.1 reshape.193
  185.6 12.6 %reduce = bf16[2048,192]{1,0:T(8,128)(2,1)} reduce(bf16[2048,1,192]{2,1,0:T(2,128)(2,1)S(1)} %bitcast.332, bf16[]{:T(256)} %broadcast.251), dimensions={1}, to_apply=%bitcast.258.reduce_sub_computation | reduce | bytes 1572866
  198.2 2.8 reshape.194
  201.0 22.8 %all_to_all.103 = bf16[32,2,6144]{2,1,0:T(2,128)(2,1)} all-to-all(bf16[32,2,6144]{2,1,0:T(2,128)(2,1)S(1)} %reshape.194), channel_id=1, replica_groups=mesh['ctx'=32,'head'=8] {'ctx'}, dimensions={0} | all-to-all | bytes 1572864 | tf_op jit(solution)/shard_map/all_to_all | solution.py:44
  223.7 4.5 reshape.195
  229.4 7.4 all-to-all-start.3
  243.9 19.5 %all-to-all-done.3 = bf16[32,1,64,192]{3,2,1,0:T(8,128)(2,1)S(1)} async-done(((bf16[32,1,64,192]{3,2,1,0:T(8,128)(2,1)}), bf16[32,1,64,192]{3,2,1,0:T(8,128)(2,1)S(1)}, u32[]{:S(2)}, u32[]{:S(2)}) %all-to-all-start.3) | async-done | bytes 786464 | tf_op jit(solution)/shard_map/all_to_all | solution.py:49
  267.9 3.4 collective-permute-start
  280.6 3.9 collective-permute-start.2
  293.3 9.8 %collective-permute-start.4 = (bf16[4,16,384]{2,1,0:T(8,128)(2,1)S(1)}, bf16[4,16,384]{2,1,0:T(8,128)(2,1)S(1)}, u32[]{:S(2)}, u32[]{:S(2)}) collective-permute-start(bf16[4,16,384]{2,1,0:T(8,128)(2,1)S(1)} %get-tuple-element.172), channel_id=1, source_target_pairs={{0,8},{8,16},{16,24},{24,32},{32,40},{40,48},{48,56},{56,64},{64,7... | collective-permute-start | bytes 147464 | tf_op jit(solution)/shard_map/ppermute | solution.py:21
  308.5 12.2 %collective-permute-start.6 = (bf16[4,16,384]{2,1,0:T(8,128)(2,1)S(1)}, bf16[4,16,384]{2,1,0:T(8,128)(2,1)S(1)}, u32[]{:S(2)}, u32[]{:S(2)}) collective-permute-start(bf16[4,16,384]{2,1,0:T(8,128)(2,1)S(1)} %get-tuple-element.170), channel_id=1, source_target_pairs={{0,8},{8,16},{16,24},{24,32},{32,40},{40,48},{48,56},{56,64},{64,7... | collective-permute-start | bytes 147464 | tf_op jit(solution)/shard_map/ppermute | solution.py:21
  324.2 18.7 %all_to_all.104 = bf16[4,8,64,96]{3,2,0,1:T(8,128)(2,1)} all-to-all(bf16[4,8,64,96]{3,2,0,1:T(8,128)(2,1)S(1)} %copy.80), channel_id=1, replica_groups=mesh['ctx'=32,'head'=8] {'head'}, dimensions={1} | all-to-all | bytes 786432 | tf_op jit(solution)/shard_map/all_to_all | solution.py:36
  342.9 25.1 %all-to-all-start.5 = ((bf16[32,64,96]{2,1,0:T(8,128)(2,1)}), bf16[32,64,96]{2,1,0:T(8,128)(2,1)S(1)}, u32[]{:S(2)}, u32[]{:S(2)}) async-start(bf16[32,64,96]{2,1,0:T(8,128)(2,1)} %bitcast.92), calls=%async_computation.5 | async-start | bytes 1048576 | tf_op jit(solution)/shard_map/all_to_all | solution.py:38
  368.3 17.0 %all-to-all-done.5 = bf16[32,64,96]{2,1,0:T(8,128)(2,1)S(1)} async-done(((bf16[32,64,96]{2,1,0:T(8,128)(2,1)}), bf16[32,64,96]{2,1,0:T(8,128)(2,1)S(1)}, u32[]{:S(2)}, u32[]{:S(2)}) %all-to-all-start.5) | async-done | bytes 393248 | tf_op jit(solution)/shard_map/all_to_all | solution.py:38
  385.3 58.8 %while.26 = (s32[]{:T(128)}, f32[2048,64]{0,1:T(8,128)S(1)}, f32[2048,96]{0,1:T(8,128)}, bf16[4,512,64]{1,2,0:T(8,128)(2,1)S(1)}, bf16[4,512,64]{2,1,0:T(8,128)(...) while((s32[]{:T(128)}, f32[2048,64]{0,1:T(8,128)S(1)}, ...), condition=%wide.region_10.11_spmd.clone, body=%wide.region_6.10_spmd.clone.sunk | while | flops 828013056 | bytes 56842404 | solution.py:135
  393.8 4.2 convolution_add_fusion.9
  408.3 4.4 convolution_add_fusion.9
  423.1 4.4 convolution_add_fusion.9
  437.9 4.4 convolution_add_fusion.9
  447.1 11.6 %reduce.1 = bf16[2048,224]{1,0:T(8,128)(2,1)S(1)} reduce(bf16[2048,1,224]{2,1,0:T(2,128)(2,1)S(1)} %bitcast.333, bf16[]{:T(256)} %broadcast.251), dimensions={1}, to_apply=%bitcast.260.reduce_sub_computation | reduce | bytes 1835010
  460.5 28.3 %all_to_all.105 = bf16[32,2,7168]{2,1,0:T(2,128)(2,1)S(1)} all-to-all(bf16[32,2,7168]{2,1,0:T(2,128)(2,1)S(1)} %reshape.196), channel_id=1, replica_groups=mesh['ctx'=32,'head'=8] {'ctx'}, dimensions={0} | all-to-all | bytes 1835008 | tf_op jit(solution)/shard_map/all_to_all | solution.py:44
  491.2 30.5 %all_to_all.106 = bf16[32,1,64,224]{3,2,1,0:T(8,128)(2,1)S(1)} all-to-all(bf16[32,1,64,224]{3,2,1,0:T(8,128)(2,1)S(1)} %bitcast.340), channel_id=1, replica_groups=mesh['ctx'=32,'head'=8] {'head'}, dimensions={0} | all-to-all | bytes 1835008 | tf_op jit(solution)/shard_map/all_to_all | solution.py:49
  529.1 258.6 %all-reduce.2.cloned.1.call-done = f32[768,8,128]{2,0,1:T(8,128)} async-done(((f32[768,8,128]{2,0,1:T(8,128)}), f32[768,8,128]{2,0,1:T(8,128)}) %all-reduce.2.cloned.1.call-update) | async-done | bytes 3145744 | tf_op jit(solution)/shard_map/psum | solution.py:279
  (200 shorter events, 152.1 us)
Async XLA Ops:
  7.2 256.4 %copy-start = (bf16[768,768]{1,0:T(8,128)(2,1)S(1)}, bf16[768,768]{1,0:T(8,128)(2,1)}, u32[]{:S(2)}) copy-start(bf16[768,768]{1,0:T(8,128)(2,1)} %param.21) | copy-start | bytes 3538948
  9.9 8.5 %copy-start.16 = (bf16[4,64,768]{2,1,0:T(8,128)(2,1)S(1)}, bf16[4,64,768]{2,1,0:T(8,128)(2,1)}, u32[]{:S(2)}) copy-start(bf16[4,64,768]{2,1,0:T(8,128)(2,1)} %param.16) | copy-start | bytes 1179652
  11.3 8.7 %copy-start.8 = (bf16[768,512]{0,1:T(8,128)(2,1)}, bf16[768,512]{0,1:T(8,128)(2,1)S(1)}, u32[]{:S(2)}) copy-start(bf16[768,512]{0,1:T(8,128)(2,1)S(1)} %copy.72) | copy-start | bytes 2359300
  13.2 8.0 %copy-start.4 = (bf16[768,768]{0,1:T(8,128)(2,1)}, bf16[768,768]{0,1:T(8,128)(2,1)S(1)}, u32[]{:S(2)}) copy-start(bf16[768,768]{0,1:T(8,128)(2,1)S(1)} %copy.73) | copy-start | bytes 3538948
  18.3 2.9 copy-start.10
  18.3 3.8 copy-start.9
  19.1 4.0 copy-start.21
  19.1 4.0 copy-start.24
  70.5 52.2 %all-to-all-start.1 = ((bf16[32,64,352]{2,1,0:T(8,128)(2,1)}), bf16[32,64,352]{2,1,0:T(8,128)(2,1)S(1)}, u32[]{:S(2)}, u32[]{:S(2)}) async-start(bf16[32,64,352]{2,1,0:T(8,128)(2,1)} %bitcast.336), calls=%async_computation.1 | async-start | bytes 3145728 | tf_op jit(solution)/shard_map/all_to_all | solution.py:38
  223.7 13.1 %copy-start.23 = (s32[2]{0:T(128)S(1)}, s32[2]{0:T(128)}, u32[]{:S(2)}) copy-start(s32[2]{0:T(128)} %param.24) | copy-start | bytes 28
  229.4 34.1 %copy-start.17 = (bf16[4,64,768]{2,1,0:T(8,128)(2,1)S(1)}, bf16[4,64,768]{2,1,0:T(8,128)(2,1)}, u32[]{:S(2)}) copy-start(bf16[4,64,768]{2,1,0:T(8,128)(2,1)} %param.16) | copy-start | bytes 1179652
  229.4 34.0 %all-to-all-start.3 = ((bf16[32,1,64,192]{3,2,1,0:T(8,128)(2,1)}), bf16[32,1,64,192]{3,2,1,0:T(8,128)(2,1)S(1)}, u32[]{:S(2)}, u32[]{:S(2)}) async-start(bf16[32,1,64,192]{3,2,1,0:T(8,128)(2,1)} %bitcast.339), calls=%async_computation.3 | async-start | bytes 2097152 | tf_op jit(solution)/shard_map/all_to_all | solution.py:49
  264.1 7.1 copy-start.3
  265.4 8.3 %collective-permute-start.1 = (bf16[2,4,16,768]{3,2,1,0:T(8,128)(2,1)S(1)}, bf16[2,4,16,768]{3,2,1,0:T(8,128)(2,1)S(1)}, u32[]{:S(2)}, u32[]{:S(2)}) collective-permute-start(bf16[2,4,16,768]{3,2,1,0:T(8,128)(2,1)S(1)} %get-tuple-element.167), channel_id=1, source_target_pairs={{8,0},{16,8},{24,16},{32,24},{40,32},{48,40},{56,48},{64,56},{72,6... | collective-permute-start | bytes 589832 | tf_op jit(solution)/shard_map/ppermute | solution.py:23
  267.9 8.1 %collective-permute-start = (bf16[2,4,16,768]{3,2,1,0:T(8,128)(2,1)S(1)}, bf16[2,4,16,768]{3,2,1,0:T(8,128)(2,1)S(1)}, u32[]{:S(2)}, u32[]{:S(2)}) collective-permute-start(bf16[2,4,16,768]{3,2,1,0:T(8,128)(2,1)S(1)} %get-tuple-element.166), channel_id=1, source_target_pairs={{0,8},{8,16},{16,24},{24,32},{32,40},{40,48},{48,56},{56,64},{64,7... | collective-permute-start | bytes 589832 | tf_op jit(solution)/shard_map/ppermute | solution.py:21
  278.7 7.6 collective-permute-start.3
  280.6 7.6 collective-permute-start.2
  291.4 12.1 %collective-permute-start.5 = (bf16[4,16,384]{2,1,0:T(8,128)(2,1)S(1)}, bf16[4,16,384]{2,1,0:T(8,128)(2,1)S(1)}, u32[]{:S(2)}, u32[]{:S(2)}) collective-permute-start(bf16[4,16,384]{2,1,0:T(8,128)(2,1)S(1)} %get-tuple-element.173), channel_id=1, source_target_pairs={{8,0},{16,8},{24,16},{32,24},{40,32},{48,40},{56,48},{64,56},{72,6... | collective-permute-start | bytes 147464 | tf_op jit(solution)/shard_map/ppermute | solution.py:23
  293.3 11.5 %collective-permute-start.4 = (bf16[4,16,384]{2,1,0:T(8,128)(2,1)S(1)}, bf16[4,16,384]{2,1,0:T(8,128)(2,1)S(1)}, u32[]{:S(2)}, u32[]{:S(2)}) collective-permute-start(bf16[4,16,384]{2,1,0:T(8,128)(2,1)S(1)} %get-tuple-element.172), channel_id=1, source_target_pairs={{0,8},{8,16},{16,24},{24,32},{32,40},{40,48},{48,56},{56,64},{64,7... | collective-permute-start | bytes 147464 | tf_op jit(solution)/shard_map/ppermute | solution.py:21
  306.5 14.5 %collective-permute-start.7 = (bf16[4,16,384]{2,1,0:T(8,128)(2,1)S(1)}, bf16[4,16,384]{2,1,0:T(8,128)(2,1)S(1)}, u32[]{:S(2)}, u32[]{:S(2)}) collective-permute-start(bf16[4,16,384]{2,1,0:T(8,128)(2,1)S(1)} %get-tuple-element.171), channel_id=1, source_target_pairs={{8,0},{16,8},{24,16},{32,24},{40,32},{48,40},{56,48},{64,56},{72,6... | collective-permute-start | bytes 147464 | tf_op jit(solution)/shard_map/ppermute | solution.py:23
  308.5 13.9 %collective-permute-start.6 = (bf16[4,16,384]{2,1,0:T(8,128)(2,1)S(1)}, bf16[4,16,384]{2,1,0:T(8,128)(2,1)S(1)}, u32[]{:S(2)}, u32[]{:S(2)}) collective-permute-start(bf16[4,16,384]{2,1,0:T(8,128)(2,1)S(1)} %get-tuple-element.170), channel_id=1, source_target_pairs={{0,8},{8,16},{16,24},{24,32},{32,40},{40,48},{48,56},{56,64},{64,7... | collective-permute-start | bytes 147464 | tf_op jit(solution)/shard_map/ppermute | solution.py:21
  323.5 19.4 %copy-start.13 = (f32[4,64,768]{2,1,0:T(8,128)}, f32[4,64,768]{2,1,0:T(8,128)S(1)}, u32[]{:S(2)}) copy-start(f32[4,64,768]{2,1,0:T(8,128)S(1)} %fusion.63) | copy-start | bytes 2359300
  342.9 42.4 %all-to-all-start.5 = ((bf16[32,64,96]{2,1,0:T(8,128)(2,1)}), bf16[32,64,96]{2,1,0:T(8,128)(2,1)S(1)}, u32[]{:S(2)}, u32[]{:S(2)}) async-start(bf16[32,64,96]{2,1,0:T(8,128)(2,1)} %bitcast.92), calls=%async_computation.5 | async-start | bytes 1048576 | tf_op jit(solution)/shard_map/all_to_all | solution.py:38
  368.0 419.8 %all-reduce.2.cloned.1.call-start = ((), (), s32[]{:S(2)}) async-start(), calls=%async_computation.8 | async-start | bytes 6291456 | tf_op jit(solution)/shard_map/psum | solution.py:279
  387.2 3.6 copy-start.2
  401.8 3.6 copy-start.2
  416.5 3.6 copy-start.2
  431.3 3.6 copy-start.2
  488.8 33.9 %copy-start.22 = (f32[4,64]{1,0:T(4,128)S(1)}, f32[4,64]{1,0:T(4,128)}, u32[]{:S(2)}) copy-start(f32[4,64]{1,0:T(4,128)} %copy-done.21) | copy-start | bytes 3076
  488.8 33.9 %copy-start.25 = (f32[768]{0:T(1024)S(1)}, f32[768]{0:T(1024)}, u32[]{:S(2)}) copy-start(f32[768]{0:T(1024)} %param.17) | copy-start | bytes 9220
  491.0 31.7 %copy-start.18 = (bf16[4,64,768]{2,1,0:T(8,128)(2,1)S(1)}, bf16[4,64,768]{2,1,0:T(8,128)(2,1)}, u32[]{:S(2)}) copy-start(bf16[4,64,768]{2,1,0:T(8,128)(2,1)} %param.16) | copy-start | bytes 1179652
  525.3 264.8 %copy-start.1 = (bf16[768,768]{1,0:T(8,128)(2,1)S(1)}, bf16[768,768]{1,0:T(8,128)(2,1)}, u32[]{:S(2)}) copy-start(bf16[768,768]{1,0:T(8,128)(2,1)} %param.21) | copy-start | bytes 3538948
  (13 other events, 28.6 us)
Sparse Core Ops, SparseCore 0:
  525.3 262.4 all-reduce.1
where the time goes:
time: 803 us; the launch traced here: 797 us
  waiting for transfers between devices  345 us (43%)
  blocking collectives  144 us (18%)
  matrix products  114 us (14%)
  starting transfers between devices  82.4 us (10%)
  other arithmetic  46 us (6%)
  local copies, waits for them, and re-layouts  44.2 us (6%)
  between operations  21.4 us (3%)
    psum x1, waiting for transfers between devices, per_device(): lax.psum(jnp.einsum('blc,bhld->chd', normed, pair_grads, preferred_elemen...  259 us
    all_to_all x2, blocking collectives, to_items(): lax.all_to_all(row_form, 'head', split_axis=1, concat_axis=0, tiled=True)  62.4 us
    all_to_all x2, waiting for transfers between devices, to_items(): lax.all_to_all(merged, 'ctx', split_axis=0, concat_axis=1, tiled=True)  57 us
    all_to_all x2, blocking collectives, to_rows(): lax.all_to_all(widened, 'ctx', split_axis=1, concat_axis=0, tiled=True)  51.1 us
    all_to_all x2, starting transfers between devices, to_items(): lax.all_to_all(merged, 'ctx', split_axis=0, concat_axis=1, tiled=True)  37.2 us
    all_to_all x1, blocking collectives, to_rows(): lax.all_to_all(grouped, 'head', split_axis=0, concat_axis=1, tiled=True)  30.5 us
    ppermute x4, starting transfers between devices, extended(): lax.ppermute(tail, axis, [(i, (i + 1) % count) for i in range(ends)])  29.3 us
    unnamed x66, local copies, waits for them, and re-layouts  28.5 us
  transfers between devices with their start and end apart: 12, of which 10 were waited for; matrix products, arithmetic and copies ran while one was open for 1% of the time, Pallas kernels for 0%

commit v1 on v0

v1 whole, which is shorter than its diff:
```python
import functools

import jax
import jax.numpy as jnp
from jax import lax
from jax.experimental import pallas as pl
from jax.experimental.pallas import tpu as pltpu
from jax.sharding import PartitionSpec as P

HEADS = 8
KEY = 64
VAL = 96
DMAX = 16
MESH = pl.DeviceIdType.MESH
VMEM_LIMIT = 56 * 2**20
F32 = jnp.float32
BF16 = jnp.bfloat16
BLOCK = 256


def place(ctx, head):
    return ctx // 8, (ctx // 4) % 2 * 4 + head // 2, ctx % 4, head % 2


def device(y, z, x, core):
    return y * 8 + z // 4 * 4 + x, z % 4 * 2 + core


def chunk_of(ctx, head):
    y, _, x, core = place(ctx, head)
    return (x + 4 - y) % 4 * 2 + core


def member(ctx, head, j):
    y, z, _, _ = place(ctx, head)
    return device(y, z, (j // 2 + y) % 4, j % 2)


def home_of(ctx, head, b):
    y, z, _, core = place(ctx, head)
    return device(b, core * 4 + (z % 4 + 2) % 4, (y + b) % 4, z // 4)


def owner_of(ctx, head, x0):
    y, z, x, core = place(ctx, head)
    return device((x + 4 - y) % 4, core * 4 + (z % 4 + 2) % 4, x0, z // 4)


def me():
    return lax.axis_index("ctx"), lax.axis_index("head")


def signal(barrier, target):
    pl.semaphore_signal(barrier, inc=1, device_id=target, device_id_type=MESH)


def remote(src, dst, send, recv, target):
    return pltpu.make_async_remote_copy(
        src_ref=src, dst_ref=dst, send_sem=send, recv_sem=recv, device_id=target, device_id_type=MESH
    )


class Stream:
    def __init__(self, count, dst, src, slot, own):
        self.count, self.dst, self.src, self.slot, self.own = count, dst, src, slot, own


def home_stream():
    ctx, head = me()
    return Stream(4, lambda i: home_of(ctx, head, i), lambda k: owner_of(ctx, head, k), ctx % 4, None)


def owner_stream():
    ctx, head = me()
    return Stream(4, lambda i: owner_of(ctx, head, i), lambda k: home_of(ctx, head, k), ctx // 8, None)


def group_stream():
    ctx, head = me()
    return Stream(
        8, lambda i: member(ctx, head, i), lambda k: member(ctx, head, k), chunk_of(ctx, head), chunk_of(ctx, head)
    )


def plane_stream():
    ctx, head = me()
    y, z, _, _ = place(ctx, head)
    j = chunk_of(ctx, head)

    def at(r):
        y_at = (r // 8 + 3) % 4
        return device(y_at, r % 8, (j // 2 + y_at) % 4, j % 2)

    rank = (y + 1) % 4 * 8 + z
    return Stream(32, at, at, rank, rank)


def rows_stream():
    ctx, head = me()
    y, z, _, _ = place(ctx, head)
    r = (y + 1) % 4 * 8 + z

    def src(k):
        row = ctx // 8
        y_src = (row + 3) % 4
        return device(y_src, ctx % 8, (k // 2 + y_src) % 4, k % 2)

    return Stream(8, lambda i: (r, i), src, chunk_of(ctx, head), None)


def exchange(arrays, kinds, collective_id):
    count = len(arrays)

    def kernel(*refs):
        xs, outs, sems = refs[:count], refs[count : 2 * count], refs[2 * count :]
        streams = [kind() for kind in kinds]
        barrier = pltpu.get_barrier_semaphore()
        total = 0
        for stream in streams:
            first = 0 if stream.own is None else 1
            base = 0 if stream.own is None else stream.own

            def greet(i, carry, stream=stream, base=base):
                signal(barrier, stream.src((base + i) % stream.count))
                return carry

            lax.fori_loop(first, stream.count, greet, 0)
            total += stream.count - first
        pl.semaphore_wait(barrier, total)
        for n, stream in enumerate(streams):
            x_ref, o_ref, send, recv = xs[n], outs[n], sems[2 * n], sems[2 * n + 1]
            first = 0 if stream.own is None else 1
            base = stream.slot if stream.own is None else stream.own

            def start(i, carry, stream=stream, base=base, x_ref=x_ref, o_ref=o_ref, send=send, recv=recv):
                k = (base + i) % stream.count
                remote(x_ref.at[k], o_ref.at[stream.slot], send.at[k], recv.at[stream.slot], stream.dst(k)).start()
                return carry

            lax.fori_loop(first, stream.count, start, 0)
            if first:
                local = pltpu.make_async_copy(x_ref.at[base], o_ref.at[base], send.at[base])
                local.start()
                local.wait()
        for n, stream in enumerate(streams):
            x_ref, o_ref, send, recv = xs[n], outs[n], sems[2 * n], sems[2 * n + 1]
            first = 0 if stream.own is None else 1
            base = stream.slot if stream.own is None else stream.own

            def finish(i, carry, stream=stream, base=base, x_ref=x_ref, o_ref=o_ref, send=send, recv=recv):
                k = (base + i) % stream.count
                remote(x_ref.at[k], o_ref.at[k], send.at[k], recv.at[k], stream.dst(k)).wait()
                return carry

            lax.fori_loop(first, stream.count, finish, 0)

    scratch = []
    for array in arrays:
        scratch += [pltpu.SemaphoreType.DMA((array.shape[0],))] * 2
    return pl.pallas_call(
        kernel,
        out_shape=[jax.ShapeDtypeStruct(a.shape, a.dtype) for a in arrays],
        in_specs=[pl.BlockSpec(memory_space=pl.ANY)] * count,
        out_specs=[pl.BlockSpec(memory_space=pl.ANY)] * count,
        scratch_shapes=scratch,
        compiler_params=pltpu.CompilerParams(collective_id=collective_id, has_side_effects=True),
    )(*arrays)


def gather(rows, collective_id):
    def kernel(x_ref, o_ref, send, recv, fsend, frecv, local):
        ctx, head = me()
        j = chunk_of(ctx, head)
        core = j % 2
        sibling = member(ctx, head, j - core + 1 - core)
        barrier = pltpu.get_barrier_semaphore()
        signal(barrier, sibling)
        for d in range(1, 4):
            signal(barrier, member(ctx, head, (j + 2 * d) % 8))
        pl.semaphore_wait(barrier, 4)
        for d in range(1, 4):
            remote(x_ref, o_ref.at[j], send.at[d], recv.at[d], member(ctx, head, (j + 2 * d) % 8)).start()
        remote(x_ref, o_ref.at[j], send.at[0], recv.at[0], sibling).start()
        own = pltpu.make_async_copy(x_ref, o_ref.at[j], local)
        own.start()
        for d in (1, 3, 2):
            s = (j + 8 - 2 * d) % 8
            remote(x_ref, o_ref.at[s], send.at[d], recv.at[d], sibling).wait_recv()
            remote(o_ref.at[s], o_ref.at[s], fsend.at[d], frecv.at[d], sibling).start()
        own.wait()
        other = j - core + 1 - core
        remote(x_ref, o_ref.at[other], send.at[0], recv.at[0], sibling).wait()
        for d in (1, 3, 2):
            s = (other + 8 - 2 * d) % 8
            remote(o_ref.at[s], o_ref.at[s], fsend.at[d], frecv.at[d], sibling).wait()
            remote(x_ref, o_ref.at[s], send.at[d], recv.at[d], sibling).wait_send()

    return pl.pallas_call(
        kernel,
        out_shape=jax.ShapeDtypeStruct((8,) + rows.shape, rows.dtype),
        in_specs=[pl.BlockSpec(memory_space=pl.ANY)],
        out_specs=pl.BlockSpec(memory_space=pl.ANY),
        scratch_shapes=[pltpu.SemaphoreType.DMA((4,))] * 4 + [pltpu.SemaphoreType.DMA],
        compiler_params=pltpu.CompilerParams(collective_id=collective_id, has_side_effects=True),
    )(rows)


def dot(a, b, contract):
    return lax.dot_general(a, b, ((contract[0], contract[1]), ((), ())), preferred_element_type=F32)


def attend_forward_kernel(qt_ref, q_ref, kt_ref, k_ref, v_ref, o_ref, lse_ref, att_ref):
    scale = KEY**-0.5
    s = dot(q_ref[...], k_ref[...], ((1,), (1,))) * scale
    top = jnp.max(s, axis=1, keepdims=True)
    p = jnp.exp(s - top)
    ext = dot(p.astype(BF16), v_ref[...], ((1,), (0,)))
    total = ext[:, VAL : VAL + 1]
    inv = 1.0 / total
    ts = dot(qt_ref[...], kt_ref[...], ((1,), (1,))) * scale
    mean = jnp.sum(p * ts, axis=1, keepdims=True) / jnp.sum(p, axis=1, keepdims=True)
    tw = p * (ts - mean)
    tan = dot(tw.astype(BF16), v_ref[...], ((1,), (0,))) * inv
    att = ext * inv
    o_ref[...] = jnp.concatenate([att[:, :VAL], tan[:, :VAL]], axis=1).astype(BF16)
    att_ref[...] = att
    lse = jnp.broadcast_to(top + jnp.log(total), (BLOCK, 128))
    lse_ref[...] = lse.T[:8]


def attend_forward(proj):
    length = proj.shape[0]
    q, tq = proj[:, :KEY], proj[:, KEY : 2 * KEY]
    k, tk = proj[:, 2 * KEY : 3 * KEY], proj[:, 3 * KEY : 4 * KEY]
    qt = jnp.concatenate([tq, q], axis=1)
    kt = jnp.concatenate([k, tk], axis=1)
    v = jnp.concatenate([proj[:, 4 * KEY :], jnp.ones((length, 128 - VAL), BF16)], axis=1)
    whole = lambda a: pl.BlockSpec(a.shape, lambda i: (0, 0))
    part = lambda a: pl.BlockSpec((BLOCK, a.shape[1]), lambda i: (i, 0))
    out, lse, att = pl.pallas_call(
        attend_forward_kernel,
        grid=(length // BLOCK,),
        out_shape=[
            jax.ShapeDtypeStruct((length, 2 * VAL), BF16),
            jax.ShapeDtypeStruct((8, length), F32),
            jax.ShapeDtypeStruct((length, 128), F32),
        ],
        in_specs=[part(qt), part(q), whole(kt), whole(k), whole(v)],
        out_specs=[
            pl.BlockSpec((BLOCK, 2 * VAL), lambda i: (i, 0)),
            pl.BlockSpec((8, BLOCK), lambda i: (0, i)),
            pl.BlockSpec((BLOCK, 128), lambda i: (i, 0)),
        ],
        compiler_params=pltpu.CompilerParams(vmem_limit_bytes=VMEM_LIMIT),
    )(qt, q, kt, k, v)
    return out, lse, att, q, k, v


def attend_backward_kernel(q_ref, k_ref, v_ref, g_ref, kT_ref, lse_ref, delta_ref, dqT_ref, dk_ref, dv_ref, acc_ref):
    i = pl.program_id(0)
    scale = KEY**-0.5
    s = dot(k_ref[...], q_ref[...], ((1,), (1,))) * scale
    w = jnp.exp(s - lse_ref[0:1, :])
    dp = dot(v_ref[...], g_ref[...], ((1,), (1,)))
    ds = (w * (dp - delta_ref[0:1, :]) * scale).astype(BF16)
    dk_ref[...] = dot(ds, q_ref[...], ((1,), (0,))).astype(BF16)
    dv_ref[...] = dot(w.astype(BF16), g_ref[...], ((1,), (0,))).astype(BF16)
    dq = dot(kT_ref[...], ds, ((1,), (0,)))

    @pl.when(i == 0)
    def _():
        acc_ref[...] = dq

    @pl.when(i > 0)
    def _():
        acc_ref[...] += dq

    @pl.when(i == pl.num_programs(0) - 1)
    def _():
        dqT_ref[...] = acc_ref[...].astype(BF16)


def attend_backward(q, k, v, grad, lse, att):
    length = q.shape[0]
    delta = jnp.sum(grad.astype(F32) * att[:, :VAL], axis=1)
    delta = jnp.broadcast_to(delta[None, :], (8, length))
    kT = k.T
    v = v[:, :VAL]
    whole = lambda a: pl.BlockSpec(a.shape, lambda i: (0, 0))
    part = lambda a: pl.BlockSpec((BLOCK, a.shape[1]), lambda i: (i, 0))
    dqT, dk, dv = pl.pallas_call(
        attend_backward_kernel,
        grid=(length // BLOCK,),
        out_shape=[
            jax.ShapeDtypeStruct((KEY, length), BF16),
            jax.ShapeDtypeStruct((length, KEY), BF16),
            jax.ShapeDtypeStruct((length, VAL), BF16),
        ],
        in_specs=[
            whole(q),
            part(k),
            part(v),
            whole(grad),
            pl.BlockSpec((KEY, BLOCK), lambda i: (0, i)),
            whole(lse),
            whole(delta),
        ],
        out_specs=[
            pl.BlockSpec((KEY, length), lambda i: (0, 0)),
            pl.BlockSpec((BLOCK, KEY), lambda i: (i, 0)),
            pl.BlockSpec((BLOCK, VAL), lambda i: (i, 0)),
        ],
        scratch_shapes=[pltpu.VMEM((KEY, length), F32)],
        compiler_params=pltpu.CompilerParams(vmem_limit_bytes=VMEM_LIMIT),
    )(q, k, v, grad, kT, lse, delta)
    return dqT.T, dk, dv


def gelu_pair(values):
    return jax.jvp(jax.nn.gelu, (values,), (jnp.ones_like(values),))


def neighbours(step):
    pairs = []
    for ctx in range(32):
        for head in range(8):
            j = chunk_of(ctx, head)
            if 0 <= j + step < 8:
                to = member(ctx, head, j + step)
                pairs.append((ctx * 8 + head, to[0] * 8 + to[1]))
    return pairs


def extended(cells):
    up = lax.ppermute(cells[..., -DMAX:, :], ("ctx", "head"), neighbours(1))
    down = lax.ppermute(cells[..., :DMAX, :], ("ctx", "head"), neighbours(-1))
    return jnp.concatenate([up, cells, down], axis=-2)


def per_device(
    window_input,
    norm_gain,
    w_query,
    w_key,
    w_value,
    w_out,
    conv_weight,
    point_weight,
    dilations,
    tangent_query,
    tangent_key,
    curvature,
):
    features = window_input.shape[2]
    ctx, head = me()
    j = chunk_of(ctx, head)
    curves = jnp.pad(curvature[:, None, :], ((0, 0), (0, 7), (0, 64)))
    x_home, c_home = exchange([window_input, curves], [home_stream, home_stream], 0)
    inputs = x_home.reshape(256, features).astype(F32)
    curve = c_home[:, 0, :64].reshape(256, 1)
    spread = jnp.sqrt(jnp.mean(inputs * inputs, axis=-1, keepdims=True) + 1e-06)
    normed = (inputs / spread * norm_gain).astype(BF16)
    normed_all = gather(normed, 1).reshape(2048, features)

    def columns(weight, size):
        return lax.dynamic_slice_in_dim(weight, j * size, size, 1)

    joined = jnp.concatenate(
        [
            columns(w_query, KEY),
            columns(tangent_query, KEY),
            columns(w_key, KEY),
            columns(tangent_key, KEY),
            columns(w_value, VAL),
        ],
        axis=1,
    )
    proj = jnp.dot(normed_all, joined, preferred_element_type=F32).astype(BF16)
    out, lse, att, q, k, v = attend_forward(proj)
    (attended,) = exchange([out.reshape(8, 256, 2 * VAL)], [group_stream], 2)
    out_weight = w_out.reshape((HEADS, VAL, features))
    mixed = inputs + jnp.einsum("hlv,hvc->lc", attended[..., :VAL], out_weight, preferred_element_type=F32)
    tangent_mixed = jnp.einsum("hlv,hvc->lc", attended[..., VAL:], out_weight, preferred_element_type=F32)
    slopes = []
    for layer in range(2):
        dilation = dilations[layer]
        activated, act_slope = gelu_pair(mixed)
        stacked = jnp.stack([activated.astype(BF16), (act_slope * tangent_mixed).astype(BF16)])
        padded = extended(stacked)
        inner = 0.0
        for tap in range(3):
            window = lax.dynamic_slice_in_dim(padded, DMAX + (tap - 1) * dilation, 256, 1)
            inner = inner + jnp.einsum("slc,cf->slf", window, conv_weight[layer, tap], preferred_element_type=F32)
        hidden_value, hidden_slope = gelu_pair(inner[0])
        hidden = jnp.stack([hidden_value.astype(BF16), (hidden_slope * inner[1]).astype(BF16)])
        pointwise = jnp.einsum("slf,fc->slc", hidden, point_weight[layer], preferred_element_type=F32)
        mixed = mixed + pointwise[0]
        tangent_mixed = tangent_mixed + pointwise[1]
        slopes.append((act_slope, hidden_slope, dilation))
    output_tangent = tangent_mixed.astype(BF16)
    gradient = curve * tangent_mixed
    for layer in (1, 0):
        act_slope, hidden_slope, dilation = slopes[layer]
        grad_inner = (
            jnp.einsum("lc,fc->lf", gradient.astype(BF16), point_weight[layer], preferred_element_type=F32)
            * hidden_slope
        ).astype(BF16)
        padded = extended(grad_inner)
        grad_act = 0.0
        for tap in range(3):
            window = lax.dynamic_slice_in_dim(padded, DMAX - (tap - 1) * dilation, 256, 0)
            grad_act = grad_act + jnp.einsum("lf,cf->lc", window, conv_weight[layer, tap], preferred_element_type=F32)
        gradient = gradient + grad_act * act_slope
    grad_attended = jnp.einsum("lc,hvc->hlv", gradient.astype(BF16), out_weight, preferred_element_type=F32).astype(
        BF16
    )
    (grad_item,) = exchange([grad_attended], [group_stream], 3)
    dq, dk, dv = attend_backward(q, k, v, grad_item.reshape(2048, VAL), lse, att)
    pair = jnp.concatenate([dq, dk], axis=1)
    part = lax.dot_general(normed_all, pair, (((0,), (0,)), ((), ())), preferred_element_type=F32)
    grads, parts = exchange(
        [jnp.concatenate([pair, dv], axis=1).reshape(8, 256, 2 * KEY + VAL), part.reshape(32, 24, 2 * KEY)],
        [group_stream, plane_stream],
        4,
    )
    summed = jnp.sum(parts, axis=0) / (32.0 * 2048.0)
    joined_grad = jnp.concatenate(
        [
            w_query.reshape(features, HEADS, KEY),
            w_key.reshape(features, HEADS, KEY),
            w_value.reshape(features, HEADS, VAL),
        ],
        axis=2,
    )
    grad_normed = jnp.einsum("hld,chd->lc", grads, joined_grad, preferred_element_type=F32)
    gained = grad_normed * norm_gain
    input_cotangent = (
        gradient
        + gained / spread
        - inputs * jnp.sum(gained * inputs, axis=-1, keepdims=True) / (features * spread * spread * spread)
    ).astype(BF16)
    out_t, out_c, rows = exchange(
        [
            output_tangent.reshape(4, 64, features),
            input_cotangent.reshape(4, 64, features),
            summed.reshape(8, 3, 2 * KEY),
        ],
        [owner_stream, owner_stream, rows_stream],
        5,
    )
    gv_query = rows[:, :, :KEY].transpose(1, 0, 2).reshape(3, HEADS * KEY)
    gv_key = rows[:, :, KEY:].transpose(1, 0, 2).reshape(3, HEADS * KEY)
    return out_t, out_c, gv_query, gv_key


def solution(mesh):
    in_specs = (P("head", "ctx", None),) + (P(),) * 10 + (P("head", "ctx"),)
    out_specs = (
        P("head", "ctx", None),
        P("head", "ctx", None),
        P(("ctx", "head"), None),
        P(("ctx", "head"), None),
    )
    return jax.shard_map(per_device, mesh=mesh, in_specs=in_specs, out_specs=out_specs, check_vma=False)
```

time: 803 us -> 269 us (0.33)
  waiting for transfers between devices: 345 us -> 3.12 us
  Pallas kernels: 0 us -> 161 us
  blocking collectives: 144 us -> 0 us
  matrix products: 114 us -> 26.8 us
  starting transfers between devices: 82.4 us -> 24.2 us
  other arithmetic: 46 us -> 10.2 us
  between operations: 21.4 us -> 7.68 us
  local copies, waits for them, and re-layouts: 44.2 us -> 35.3 us
    psum x1 -> x0, waiting for transfers between devices: 259 us -> none  [per_device(): lax.psum(jnp.einsum('blc,bhld->chd', normed, pair_grads, preferred_elemen...]
    pallas_call x0 -> x8, Pallas kernels: none -> 161 us  [the longest x5 106 us: exchange(): pl.pallas_call(kernel, out_shape=[jax.ShapeDtypeStruct(a.shape, a.dtype)...]
    all_to_all x5 -> x0, blocking collectives: 144 us -> none  [the longest x2 62.4 us: to_items(): lax.all_to_all(row_form, 'head', split_axis=1, concat_axis=0, tiled=True)]
    dot_general x61 -> x21, matrix products: 113 us -> 25.7 us  [the longest x6 7.86 us: per_device(): jnp.einsum('slc,cf->slf', window, conv_weight[layer, tap], preferred_elem...]
    all_to_all x3 -> x0, waiting for transfers between devices: 76.6 us -> none  [the longest x2 57 us: to_items(): lax.all_to_all(merged, 'ctx', split_axis=0, concat_axis=1, tiled=True)]
    all_to_all x3 -> x0, starting transfers between devices: 44.6 us -> none  [the longest x2 37.2 us: to_items(): lax.all_to_all(merged, 'ctx', split_axis=0, concat_axis=1, tiled=True)]
    unnamed x4 -> x0, other arithmetic: 24.2 us -> none
    unnamed x66 -> x32, local copies, waits for them, and re-layouts: 28.5 us -> 11.4 us
  transfers between devices with their start and end apart: 12 -> 8, of which waited for: 10 -> 3; matrix products, arithmetic and copies ran while one was open for 1% -> 6% of each run, Pallas kernels for 0% -> 0%
where the time goes in v1:
time: 269 us; the launch traced here: 268 us
  Pallas kernels  161 us (60%)
  local copies, waits for them, and re-layouts  35.3 us (13%)
  matrix products  26.8 us (10%)
  starting transfers between devices  24.2 us (9%)
  other arithmetic  10.2 us (4%)
  between operations  7.68 us (3%)
  waiting for transfers between devices  3.12 us (1%)
    pallas_call x5, Pallas kernels, exchange(): pl.pallas_call(kernel, out_shape=[jax.ShapeDtypeStruct(a.shape, a.dtype)...  106 us
    pallas_call x1, Pallas kernels, gather(): pl.pallas_call(kernel, out_shape=jax.ShapeDtypeStruct((8,) + rows.shape,...  23.9 us
    pallas_call x1, Pallas kernels, attend_forward(): pl.pallas_call(attend_forward_kernel, grid=(length // BLOCK,), out_shape=...  16.9 us
    ppermute x4, starting transfers between devices, extended(): down = lax.ppermute(cells[..., :DMAX, :], ('ctx', 'head'), neighbours(-1))  14.4 us
    pallas_call x1, Pallas kernels, attend_backward(): pl.pallas_call(attend_backward_kernel, grid=(length // BLOCK,), out_shape...  14.3 us
    unnamed x32, local copies, waits for them, and re-layouts  11.4 us
    ppermute x4, starting transfers between devices, extended(): up = lax.ppermute(cells[..., -DMAX:, :], ('ctx', 'head'), neighbours(1))  9.74 us
    dot_general x6, matrix products, per_device(): jnp.einsum('slc,cf->slf', window, conv_weight[layer, tap], preferred_elem...  7.86 us
  transfers between devices with their start and end apart: 8, of which 3 were waited for; matrix products, arithmetic and copies ran while one was open for 6% of the time, Pallas kernels for 0%

profile of v1, /device:TPU:2, one launch (start us, length us, event | category | flops | bytes accessed | tf_op | source)
XLA Modules:
  0.0 268.0 jit_solution(12272220348471297473)
XLA Ops:
  2.1 18.4 %shard_map.147 = (bf16[4,64,768]{2,1,0:T(8,128)(2,1)}, f32[4,8,128]{2,1,0:T(8,128)}) custom-call(bf16[4,64,768]{2,1,0:T(8,128)(2,1)} %refs_0_.1, f32[4,8,128]{2,1,0:T(8,128)} %pad.5.refs_1_), custom_call_target="tpu_custom_call" | custom-call | tf_op jit(solution)/shard_map/pallas_call | solution.py:160
  21.7 1.9 fusion.55.x_ref
  23.6 23.9 %shard_map.148 = bf16[8,256,768]{2,1,0:T(8,128)(2,1)} custom-call(bf16[256,768]{1,0:T(8,128)(2,1)} %fusion.55.x_ref), custom_call_target="tpu_custom_call" | custom-call | tf_op jit(solution)/shard_map/pallas_call | solution.py:198
  52.2 3.3 %convolution_convert_fusion = bf16[2048,352]{0,1:T(8,128)(2,1)S(1)} fusion(bf16[2048,768]{1,0:T(8,128)(2,1)} %bitcast.183, bf16[768,352]{1,0:T(8,128)(2,1)} %concatenate.34), kind=kOutput, calls=%fused_computation.6 | convolution fusion | flops 1108017152 | bytes 5128192 | tf_op jit(solution)/shard_map/dot_general | solution.py:378
  61.8 16.9 %shard_map.149 = (bf16[2048,192]{1,0:T(8,128)(2,1)}, f32[8,2048]{1,0:T(8,128)}, f32[2048,128]{1,0:T(8,128)}) custom-call(bf16[2048,128]{1,0:T(8,128)(2,1)} %copy.52.qt_ref, bf16[2048,64]{1,0:T(8,128)(2,1)} %copy.53.q_ref, bf16[2048,128]{1,0:T(8,128)(2,1)} %copy.54.kt_ref, bf16[2048,64]{1,0:T(8,128)(2,1)} %copy.55.k_ref, ...), custom_call_target="tpu_custom_call" | custom-call | tf_op jit(solution)/shard_map/pallas_call | solution.py:240
  78.8 15.4 %shard_map.150 = bf16[8,256,192]{2,1,0:T(8,128)(2,1)} custom-call(bf16[8,256,192]{2,1,0:T(8,128)(2,1)} %bitcast.194), custom_call_target="tpu_custom_call" | custom-call | tf_op jit(solution)/shard_map/pallas_call | solution.py:160
  94.2 2.0 convolution_bitcast_fusion.2
  97.3 3.7 %collective-permute-start = (bf16[2,16,768]{2,1,0:T(8,128)(2,1)S(1)}, bf16[2,16,768]{2,1,0:T(8,128)(2,1)S(1)}, u32[]{:S(2)}, u32[]{:S(2)}) collective-permute-start(bf16[2,16,768]{2,1,0:T(8,128)(2,1)S(1)} %get-tuple-element.42), channel_id=1, source_target_pairs={{0,1},{1,8},{2,3},{3,10},{4,5},{5,12},{6,7},{7,14},{8,9},{9,16},{1... | collective-permute-start | bytes 147464 | tf_op jit(solution)/shard_map/ppermute | solution.py:335
  101.0 3.6 %collective-permute-start.1 = (bf16[2,16,768]{2,1,0:T(8,128)(2,1)S(1)}, bf16[2,16,768]{2,1,0:T(8,128)(2,1)S(1)}, u32[]{:S(2)}, u32[]{:S(2)}) collective-permute-start(bf16[2,16,768]{2,1,0:T(8,128)(2,1)S(1)} %get-tuple-element.43), channel_id=1, source_target_pairs={{1,0},{3,2},{5,4},{7,6},{8,1},{9,8},{10,3},{11,10},{12,5},{13,12},... | collective-permute-start | bytes 147464 | tf_op jit(solution)/shard_map/ppermute | solution.py:336
  104.6 2.5 fusion.46
  114.9 2.4 copy.67
  117.3 2.3 copy.65
  119.6 2.3 copy.66
  122.0 4.7 %copy.64 = bf16[768,2048]{1,0:T(8,128)(2,1)} copy(bf16[768,2048]{0,1:T(8,128)(2,1)} %bitcast.184) | data formatting | bytes 6291456 | tf_op jit(solution)/shard_map/dot_general | solution.py:420
  126.8 1.8 fusion.64
  128.9 1.8 fusion.16
  132.5 2.1 collective-permute-start.2
  134.6 3.6 %collective-permute-start.3 = (bf16[2,16,768]{2,1,0:T(8,128)(2,1)S(1)}, bf16[2,16,768]{2,1,0:T(8,128)(2,1)S(1)}, u32[]{:S(2)}, u32[]{:S(2)}) collective-permute-start(bf16[2,16,768]{2,1,0:T(8,128)(2,1)S(1)} %get-tuple-element.39), channel_id=1, source_target_pairs={{1,0},{3,2},{5,4},{7,6},{8,1},{9,8},{10,3},{11,10},{12,5},{13,12},... | collective-permute-start | bytes 147464 | tf_op jit(solution)/shard_map/ppermute | solution.py:336
  143.1 2.0 collective-permute-start.4
  145.1 3.6 %collective-permute-start.5 = (bf16[16,384]{1,0:T(8,128)(2,1)S(1)}, bf16[16,384]{1,0:T(8,128)(2,1)S(1)}, u32[]{:S(2)}, u32[]{:S(2)}) collective-permute-start(bf16[16,384]{1,0:T(8,128)(2,1)S(1)} %get-tuple-element.49), channel_id=1, source_target_pairs={{1,0},{3,2},{5,4},{7,6},{8,1},{9,8},{10,3},{11,10},{12,5},{13,12},... | collective-permute-start | bytes 36872 | tf_op jit(solution)/shard_map/ppermute | solution.py:336
  151.8 2.0 collective-permute-start.6
  153.7 3.6 %collective-permute-start.7 = (bf16[16,384]{1,0:T(8,128)(2,1)S(1)}, bf16[16,384]{1,0:T(8,128)(2,1)S(1)}, u32[]{:S(2)}, u32[]{:S(2)}) collective-permute-start(bf16[16,384]{1,0:T(8,128)(2,1)S(1)} %get-tuple-element.47), channel_id=1, source_target_pairs={{1,0},{3,2},{5,4},{7,6},{8,1},{9,8},{10,3},{11,10},{12,5},{13,12},... | collective-permute-start | bytes 36872 | tf_op jit(solution)/shard_map/ppermute | solution.py:336
  161.4 9.3 %shard_map.151 = bf16[8,256,96]{2,1,0:T(8,128)(2,1)} custom-call(bf16[8,256,96]{2,1,0:T(8,128)(2,1)} %bitcast.190), custom_call_target="tpu_custom_call" | custom-call | tf_op jit(solution)/shard_map/pallas_call | solution.py:160
  170.7 1.7 multiply_reduce_fusion
  173.1 14.3 %shard_map.152 = (bf16[64,2048]{1,0:T(8,128)(2,1)}, bf16[2048,64]{1,0:T(8,128)(2,1)}, bf16[2048,96]{1,0:T(8,128)(2,1)}) custom-call(bf16[2048,64]{1,0:T(8,128)(2,1)} %copy.53.q_ref, bf16[2048,64]{1,0:T(8,128)(2,1)} %copy.55.k_ref, bf16[2048,96]{1,0:T(8,128)(2,1)} %copy-done.2, bf16[2048,96]{1,0:T(8,128)(2,1)} %bitcast.185, ...), custom_call_target="tpu_custom_call" | custom-call | tf_op jit(solution)/shard_map/pallas_call | solution.py:291
  188.6 3.9 %fusion.88.refs_1_ = f32[32,24,128]{2,1,0:T(8,128)} fusion(bf16[32,24,2048]{2,1,0:T(8,128)(2,1)} %bitcast.182, bf16[2048,64]{1,0:T(8,128)(2,1)} %get-tuple-element.23, bf16[2048,64]{1,0:T(8,128)(2,1)S(1)} %bitcast.186), kind=kOutput, calls=%fused_computation.124 | convolution fusion | flops 403701760 | bytes 4063232 | tf_op jit(solution)/shard_map/dot_general | solution.py:420
  192.5 1.5 pad_maximum_fusion
  194.0 35.0 %shard_map.153 = (bf16[8,256,224]{2,1,0:T(8,128)(2,1)}, f32[32,24,128]{2,1,0:T(8,128)}) custom-call(bf16[8,256,224]{2,1,0:T(8,128)(2,1)} %bitcast.188, f32[32,24,128]{2,1,0:T(8,128)} %fusion.88.refs_1_), custom_call_target="tpu_custom_call" | custom-call | tf_op jit(solution)/shard_map/pallas_call | solution.py:160
  230.7 3.0 %fusion.56 = (f32[256]{0:T(256)S(1)}, f32[256,768]{1,0:T(8,128)S(1)}) fusion(bf16[4,64,768]{2,1,0:T(8,128)(2,1)S(1)} %copy-done.3, f32[768]{0:T(1024)S(1)} %copy-done.11, bf16[8,256,224]{2,1,0:T(8,128)(2,1)} %get-tuple-element.25, bf16[768,8,96]{0,2,1:T(8,128)(2,1)} %bitcast.193, bf16[768,8,64]{0,2,1:T(8,128)(2,1)} %bitcast.196, ...), kind=kOutput, calls=%fused_computation.76 | convolution fusion | flops 713686784 | bytes 4853760 | tf_op jit(solution)/shard_map/hld,chd->lc/dot_general | solution.py:435
  234.8 27.4 %shard_map.154 = (bf16[4,64,768]{2,1,0:T(8,128)(2,1)}, bf16[4,64,768]{2,1,0:T(8,128)(2,1)}, f32[8,3,128]{2,1,0:T(4,128)}) custom-call(bf16[4,64,768]{2,1,0:T(8,128)(2,1)} %bitcast.191, bf16[4,64,768]{2,1,0:T(8,128)(2,1)} %bitcast.192, f32[8,3,128]{2,1,0:T(4,128)} %div.52.refs_2_), custom_call_target="tpu_custom_call" | custom-call | tf_op jit(solution)/shard_map/pallas_call | solution.py:160
  264.5 1.8 copy.77
  266.2 1.8 copy.78
  (97 shorter events, 36.7 us)
Async XLA Ops:
  0.6 93.6 %copy-start = (bf16[768,768]{1,0:T(8,128)(2,1)S(1)}, bf16[768,768]{1,0:T(8,128)(2,1)}, u32[]{:S(2)}) copy-start(bf16[768,768]{1,0:T(8,128)(2,1)} %param.17) | copy-start | bytes 3538948
  55.5 2.0 copy-start.7
  57.5 2.1 slice-start
  57.5 2.4 slice-start.1
  59.9 18.9 %copy-start.2 = (bf16[2048,96]{1,0:T(8,128)(2,1)}, bf16[2048,96]{1,0:T(8,128)(2,1)S(1)}, u32[]{:S(2)}) copy-start(bf16[2048,96]{1,0:T(8,128)(2,1)S(1)} %copy.74.v_ref) | copy-start | bytes 1179652
  78.8 17.4 %copy-start.3 = (bf16[4,64,768]{2,1,0:T(8,128)(2,1)S(1)}, bf16[4,64,768]{2,1,0:T(8,128)(2,1)}, u32[]{:S(2)}) copy-start(bf16[4,64,768]{2,1,0:T(8,128)(2,1)} %get-tuple-element.17) | copy-start | bytes 1179652
  94.2 2.0 copy-start.9
  96.8 10.4 %copy-start.4 = (f32[256,768]{1,0:T(8,128)}, f32[256,768]{1,0:T(8,128)S(1)}, u32[]{:S(2)}) copy-start(f32[256,768]{1,0:T(8,128)S(1)} %fusion.20) | copy-start | bytes 2359300
  97.3 10.6 %copy-start.12 = (s32[2]{0:T(128)S(1)}, s32[2]{0:T(128)}, u32[]{:S(2)}) copy-start(s32[2]{0:T(128)} %param.20) | copy-start | bytes 28
  97.3 29.4 %collective-permute-start = (bf16[2,16,768]{2,1,0:T(8,128)(2,1)S(1)}, bf16[2,16,768]{2,1,0:T(8,128)(2,1)S(1)}, u32[]{:S(2)}, u32[]{:S(2)}) collective-permute-start(bf16[2,16,768]{2,1,0:T(8,128)(2,1)S(1)} %get-tuple-element.42), channel_id=1, source_target_pairs={{0,1},{1,8},{2,3},{3,10},{4,5},{5,12},{6,7},{7,14},{8,9},{9,16},{1... | collective-permute-start | bytes 147464 | tf_op jit(solution)/shard_map/ppermute | solution.py:335
  101.0 25.7 %collective-permute-start.1 = (bf16[2,16,768]{2,1,0:T(8,128)(2,1)S(1)}, bf16[2,16,768]{2,1,0:T(8,128)(2,1)S(1)}, u32[]{:S(2)}, u32[]{:S(2)}) collective-permute-start(bf16[2,16,768]{2,1,0:T(8,128)(2,1)S(1)} %get-tuple-element.43), channel_id=1, source_target_pairs={{1,0},{3,2},{5,4},{7,6},{8,1},{9,8},{10,3},{11,10},{12,5},{13,12},... | collective-permute-start | bytes 147464 | tf_op jit(solution)/shard_map/ppermute | solution.py:336
  126.7 2.2 copy-start.1
  128.9 2.1 copy-start.8
  130.7 1.1 copy-start.5
  132.5 6.3 %collective-permute-start.2 = (bf16[2,16,768]{2,1,0:T(8,128)(2,1)S(1)}, bf16[2,16,768]{2,1,0:T(8,128)(2,1)S(1)}, u32[]{:S(2)}, u32[]{:S(2)}) collective-permute-start(bf16[2,16,768]{2,1,0:T(8,128)(2,1)S(1)} %get-tuple-element.38), channel_id=1, source_target_pairs={{0,1},{1,8},{2,3},{3,10},{4,5},{5,12},{6,7},{7,14},{8,9},{9,16},{1... | collective-permute-start | bytes 147464 | tf_op jit(solution)/shard_map/ppermute | solution.py:335
  134.6 5.4 %collective-permute-start.3 = (bf16[2,16,768]{2,1,0:T(8,128)(2,1)S(1)}, bf16[2,16,768]{2,1,0:T(8,128)(2,1)S(1)}, u32[]{:S(2)}, u32[]{:S(2)}) collective-permute-start(bf16[2,16,768]{2,1,0:T(8,128)(2,1)S(1)} %get-tuple-element.39), channel_id=1, source_target_pairs={{1,0},{3,2},{5,4},{7,6},{8,1},{9,8},{10,3},{11,10},{12,5},{13,12},... | collective-permute-start | bytes 147464 | tf_op jit(solution)/shard_map/ppermute | solution.py:336
  143.1 6.0 %collective-permute-start.4 = (bf16[16,384]{1,0:T(8,128)(2,1)S(1)}, bf16[16,384]{1,0:T(8,128)(2,1)S(1)}, u32[]{:S(2)}, u32[]{:S(2)}) collective-permute-start(bf16[16,384]{1,0:T(8,128)(2,1)S(1)} %get-tuple-element.48), channel_id=1, source_target_pairs={{0,1},{1,8},{2,3},{3,10},{4,5},{5,12},{6,7},{7,14},{8,9},{9,16},{1... | collective-permute-start | bytes 36872 | tf_op jit(solution)/shard_map/ppermute | solution.py:335
  145.1 5.0 %collective-permute-start.5 = (bf16[16,384]{1,0:T(8,128)(2,1)S(1)}, bf16[16,384]{1,0:T(8,128)(2,1)S(1)}, u32[]{:S(2)}, u32[]{:S(2)}) collective-permute-start(bf16[16,384]{1,0:T(8,128)(2,1)S(1)} %get-tuple-element.49), channel_id=1, source_target_pairs={{1,0},{3,2},{5,4},{7,6},{8,1},{9,8},{10,3},{11,10},{12,5},{13,12},... | collective-permute-start | bytes 36872 | tf_op jit(solution)/shard_map/ppermute | solution.py:336
  151.8 6.0 %collective-permute-start.6 = (bf16[16,384]{1,0:T(8,128)(2,1)S(1)}, bf16[16,384]{1,0:T(8,128)(2,1)S(1)}, u32[]{:S(2)}, u32[]{:S(2)}) collective-permute-start(bf16[16,384]{1,0:T(8,128)(2,1)S(1)} %get-tuple-element.46), channel_id=1, source_target_pairs={{0,1},{1,8},{2,3},{3,10},{4,5},{5,12},{6,7},{7,14},{8,9},{9,16},{1... | collective-permute-start | bytes 36872 | tf_op jit(solution)/shard_map/ppermute | solution.py:335
  153.7 5.0 %collective-permute-start.7 = (bf16[16,384]{1,0:T(8,128)(2,1)S(1)}, bf16[16,384]{1,0:T(8,128)(2,1)S(1)}, u32[]{:S(2)}, u32[]{:S(2)}) collective-permute-start(bf16[16,384]{1,0:T(8,128)(2,1)S(1)} %get-tuple-element.47), channel_id=1, source_target_pairs={{1,0},{3,2},{5,4},{7,6},{8,1},{9,8},{10,3},{11,10},{12,5},{13,12},... | collective-permute-start | bytes 36872 | tf_op jit(solution)/shard_map/ppermute | solution.py:336
  188.6 3.9 %copy-start.6 = (bf16[2048,64]{1,0:T(8,128)(2,1)S(1)}, bf16[2048,64]{1,0:T(8,128)(2,1)}, u32[]{:S(2)}) copy-start(bf16[2048,64]{1,0:T(8,128)(2,1)} %get-tuple-element.23) | copy-start | bytes 786436
  188.6 3.9 %copy-start.10 = (bf16[2048,96]{1,0:T(8,128)(2,1)S(1)}, bf16[2048,96]{1,0:T(8,128)(2,1)}, u32[]{:S(2)}) copy-start(bf16[2048,96]{1,0:T(8,128)(2,1)} %get-tuple-element.24) | copy-start | bytes 1179652
  192.5 38.2 %copy-start.11 = (f32[768]{0:T(1024)S(1)}, f32[768]{0:T(1024)}, u32[]{:S(2)}) copy-start(f32[768]{0:T(1024)} %param.13) | copy-start | bytes 9220

commit v2 on v1

--- a/solution.py
+++ b/solution.py
@@ -222,7 +222,8 @@
     tw = p * (ts - mean)
     tan = dot(tw.astype(BF16), v_ref[...], ((1,), (0,))) * inv
     att = ext * inv
-    o_ref[...] = jnp.concatenate([att[:, :VAL], tan[:, :VAL]], axis=1).astype(BF16)
+    o_ref[0] = att[:, :VAL].astype(BF16)
+    o_ref[1] = tan[:, :VAL].astype(BF16)
     att_ref[...] = att
     lse = jnp.broadcast_to(top + jnp.log(total), (BLOCK, 128))
     lse_ref[...] = lse.T[:8]
@@ -241,13 +242,13 @@
         attend_forward_kernel,
         grid=(length // BLOCK,),
         out_shape=[
-            jax.ShapeDtypeStruct((length, 2 * VAL), BF16),
+            jax.ShapeDtypeStruct((2, length, VAL), BF16),
             jax.ShapeDtypeStruct((8, length), F32),
             jax.ShapeDtypeStruct((length, 128), F32),
         ],
         in_specs=[part(qt), part(q), whole(kt), whole(k), whole(v)],
         out_specs=[
-            pl.BlockSpec((BLOCK, 2 * VAL), lambda i: (i, 0)),
+            pl.BlockSpec((2, BLOCK, VAL), lambda i: (0, i, 0)),
             pl.BlockSpec((8, BLOCK), lambda i: (0, i)),
             pl.BlockSpec((BLOCK, 128), lambda i: (i, 0)),
         ],
@@ -316,25 +317,310 @@
     return dqT.T, dk, dv
 
 
-def gelu_pair(values):
-    return jax.jvp(jax.nn.gelu, (values,), (jnp.ones_like(values),))
-
-
-def neighbours(step):
-    pairs = []
-    for ctx in range(32):
-        for head in range(8):
-            j = chunk_of(ctx, head)
-            if 0 <= j + step < 8:
-                to = member(ctx, head, j + step)
-                pairs.append((ctx * 8 + head, to[0] * 8 + to[1]))
-    return pairs
-
-
-def extended(cells):
-    up = lax.ppermute(cells[..., -DMAX:, :], ("ctx", "head"), neighbours(1))
-    down = lax.ppermute(cells[..., :DMAX, :], ("ctx", "head"), neighbours(-1))
-    return jnp.concatenate([up, cells, down], axis=-2)
+def gelu_pair(v):
+    root = 0.7978845608028654
+    square = v * v
+    t = jnp.tanh(root * (v + 0.044715 * v * square))
+    half = 0.5 * (1.0 + t)
+    return v * half, half + 0.5 * v * (1.0 - t * t) * (root + (3.0 * 0.044715 * root) * square)
+
+
+def picker(dilation, rows):
+    shape = (2 * rows, rows + 2 * DMAX)
+    row = lax.broadcasted_iota(jnp.int32, shape, 0)
+    column = lax.broadcasted_iota(jnp.int32, shape, 1)
+    wanted = jnp.where(row < rows, row + DMAX - dilation, row - rows + DMAX + dilation)
+    return jnp.where(column == wanted, 1.0, 0.0).astype(BF16)
+
+
+def conv_kernel(
+    dil_ref,
+    att_ref,
+    x_ref,
+    curve_ref,
+    w_out_ref,
+    conv_ref,
+    point_ref,
+    tan_out_ref,
+    grad_out_ref,
+    item_ref,
+    mixed_ref,
+    tan_ref,
+    slope_ref,
+    hslope_ref,
+    pad_ref,
+    gpad_ref,
+    edge_ref,
+    halo_ref,
+    gedge_ref,
+    ghalo_ref,
+    out_ref,
+    ga_ref,
+    h_send,
+    h_recv,
+    o_send,
+    o_recv,
+    g_send,
+    g_recv,
+):
+    ctx, head = me()
+    j = chunk_of(ctx, head)
+    rows = x_ref.shape[0]
+    barrier = pltpu.get_barrier_semaphore()
+
+    def beside(step):
+        return member(ctx, head, (j + step + 8) % 8)
+
+    @pl.when(j > 0)
+    def _():
+        signal(barrier, beside(-1))
+
+    @pl.when(j < 7)
+    def _():
+        signal(barrier, beside(1))
+
+    owners = owner_stream()
+    group = group_stream()
+    for k in range(4):
+        signal(barrier, owners.src(k))
+    for k in range(1, 8):
+        signal(barrier, group.src((j + k) % 8))
+
+    def swap(n, edge, halo, pad, width):
+        lead = pad.shape[:-2]
+        edge[0] = pad[..., DMAX : 2 * DMAX, :]
+        edge[1] = pad[..., rows : rows + DMAX, :]
+        down = remote(edge.at[0], halo.at[1], h_send.at[2 * n], h_recv.at[2 * n], beside(-1))
+        up = remote(edge.at[1], halo.at[0], h_send.at[2 * n + 1], h_recv.at[2 * n + 1], beside(1))
+
+        @pl.when(j > 0)
+        def _():
+            down.start()
+
+        @pl.when(j < 7)
+        def _():
+            up.start()
+
+        def finish():
+            @pl.when(j > 0)
+            def _():
+                up.wait_recv()
+                pad[..., 0:DMAX, :] = halo[0]
+                down.wait_send()
+
+            @pl.when(j == 0)
+            def _():
+                pad[..., 0:DMAX, :] = jnp.zeros(lead + (DMAX, width), BF16)
+
+            @pl.when(j < 7)
+            def _():
+                down.wait_recv()
+                pad[..., rows + DMAX : rows + 2 * DMAX, :] = halo[1]
+                up.wait_send()
+
+            @pl.when(j == 7)
+            def _():
+                pad[..., rows + DMAX : rows + 2 * DMAX, :] = jnp.zeros(lead + (DMAX, width), BF16)
+
+        return finish
+
+    both = jnp.zeros((2 * rows, x_ref.shape[1]), F32)
+    for h in range(HEADS):
+        both = both + dot(
+            att_ref[h].reshape(2 * rows, VAL), w_out_ref[h * VAL : (h + 1) * VAL, :], ((1,), (0,))
+        )
+    mixed_ref[...] = x_ref[...].astype(F32) + both[:rows]
+    tan_ref[...] = both[rows:]
+    ends = jnp.where((j == 0) | (j == 7), 1, 2)
+    pl.semaphore_wait(barrier, 11 + ends)
+    features = x_ref.shape[1]
+    width = conv_ref.shape[3]
+    for layer in range(2):
+        dilation = dil_ref[layer]
+        act, slope = gelu_pair(mixed_ref[...])
+        slope_ref[layer] = slope
+        pad_ref[0, DMAX : DMAX + rows, :] = act.astype(BF16)
+        pad_ref[1, DMAX : DMAX + rows, :] = (slope * tan_ref[...]).astype(BF16)
+        finish = swap(layer, edge_ref.at[layer], halo_ref.at[layer], pad_ref, features)
+
+        inner = dot(
+            pad_ref[:, DMAX : DMAX + rows, :].reshape(2 * rows, features), conv_ref[layer, 1], ((1,), (0,))
+        )
+        finish()
+        pick = picker(dilation, rows)
+        value = dot(pick, pad_ref[0], ((1,), (0,))).astype(BF16)
+        tangent = dot(pick, pad_ref[1], ((1,), (0,))).astype(BF16)
+        for n, tap in ((0, 0), (1, 2)):
+            window = jnp.concatenate([value[n * rows : (n + 1) * rows], tangent[n * rows : (n + 1) * rows]], axis=0)
+            inner = inner + dot(window, conv_ref[layer, tap], ((1,), (0,)))
+        hidden, hslope = gelu_pair(inner[:rows])
+        hslope_ref[layer] = hslope
+        hidden = jnp.concatenate([hidden, hslope * inner[rows:]], axis=0).astype(BF16)
+        point = dot(hidden, point_ref[layer], ((1,), (0,)))
+        if layer == 0:
+            mixed_ref[...] += point[:rows]
+        tan_ref[...] += point[rows:]
+    out_ref[...] = tan_ref[...].astype(BF16)
+    sends = []
+    for k in range(4):
+        sends.append(
+            remote(
+                out_ref.at[pl.ds(64 * k, 64)], tan_out_ref.at[owners.slot], o_send.at[k], o_recv.at[owners.slot], owners.dst(k)
+            )
+        )
+        sends[-1].start()
+    grad_out_ref[...] = curve_ref[...] * tan_ref[...]
+    for layer in (1, 0):
+        dilation = dil_ref[layer]
+        back = dot(grad_out_ref[...].astype(BF16), point_ref[layer], ((1,), (1,)))
+        gpad_ref[DMAX : DMAX + rows, :] = (back * hslope_ref[layer]).astype(BF16)
+        finish = swap(2 + layer, gedge_ref.at[layer], ghalo_ref.at[layer], gpad_ref, width)
+
+        act = dot(gpad_ref[DMAX : DMAX + rows, :], conv_ref[layer, 1], ((1,), (1,)))
+        finish()
+        windows = dot(picker(dilation, rows), gpad_ref[...], ((1,), (0,))).astype(BF16)
+        act = act + dot(windows[:rows], conv_ref[layer, 2], ((1,), (1,)))
+        act = act + dot(windows[rows:], conv_ref[layer, 0], ((1,), (1,)))
+        grad_out_ref[...] += slope_ref[layer] * act
+    final = grad_out_ref[...].astype(BF16)
+    for h in range(HEADS):
+        ga_ref[h] = dot(final, w_out_ref[h * VAL : (h + 1) * VAL, :], ((1,), (1,))).astype(BF16)
+
+    def start(k, carry):
+        i = (j + k) % 8
+        remote(ga_ref.at[i], item_ref.at[j], g_send.at[i], g_recv.at[j], group.dst(i)).start()
+        return carry
+
+    lax.fori_loop(1, 8, start, 0)
+    own = pltpu.make_async_copy(ga_ref.at[j], item_ref.at[j], g_send.at[j])
+    own.start()
+    own.wait()
+
+    def end(k, carry):
+        i = (j + k) % 8
+        remote(ga_ref.at[i], item_ref.at[i], g_send.at[i], g_recv.at[i], group.dst(i)).wait()
+        return carry
+
+    lax.fori_loop(1, 8, end, 0)
+    for k in range(4):
+        sends[k].wait_send()
+        remote(out_ref.at[pl.ds(64 * k, 64)], tan_out_ref.at[k], o_send.at[k], o_recv.at[k], owners.dst(k)).wait_recv()
+
+
+def conv_chain(dilations, attended, x_home, curve, w_out, conv_weight, point_weight, collective_id):
+    rows, features = x_home.shape
+    width = conv_weight.shape[3]
+    vmem = pl.BlockSpec(memory_space=pltpu.VMEM)
+    anywhere = pl.BlockSpec(memory_space=pl.ANY)
+    return pl.pallas_call(
+        conv_kernel,
+        out_shape=[
+            jax.ShapeDtypeStruct((4, 64, features), BF16),
+            jax.ShapeDtypeStruct((rows, features), F32),
+            jax.ShapeDtypeStruct((8, rows, VAL), BF16),
+        ],
+        in_specs=[pl.BlockSpec(memory_space=pltpu.SMEM)] + [vmem] * 6,
+        out_specs=[anywhere, vmem, anywhere],
+        scratch_shapes=[
+            pltpu.VMEM((rows, features), F32),
+            pltpu.VMEM((rows, features), F32),
+            pltpu.VMEM((2, rows, features), F32),
+            pltpu.VMEM((2, rows, width), F32),
+            pltpu.VMEM((2, rows + 2 * DMAX, features), BF16),
+            pltpu.VMEM((rows + 2 * DMAX, width), BF16),
+            pltpu.VMEM((2, 2, 2, DMAX, features), BF16),
+            pltpu.VMEM((2, 2, 2, DMAX, features), BF16),
+            pltpu.VMEM((2, 2, DMAX, width), BF16),
+            pltpu.VMEM((2, 2, DMAX, width), BF16),
+            pltpu.VMEM((rows, features), BF16),
+            pltpu.VMEM((8, rows, VAL), BF16),
+            pltpu.SemaphoreType.DMA((8,)),
+            pltpu.SemaphoreType.DMA((8,)),
+            pltpu.SemaphoreType.DMA((4,)),
+            pltpu.SemaphoreType.DMA((4,)),
+            pltpu.SemaphoreType.DMA((8,)),
+            pltpu.SemaphoreType.DMA((8,)),
+        ],
+        compiler_params=pltpu.CompilerParams(
+            collective_id=collective_id, has_side_effects=True, vmem_limit_bytes=VMEM_LIMIT
+        ),
+    )(dilations, attended, x_home, curve, w_out, conv_weight, point_weight)
+
+
+def final_kernel(
+    x_ref, grad_ref, gain_ref, pair_ref, dv_ref, wq_ref, wk_ref, wv_ref, parts_ref,
+    out_c_ref, gvq_ref, gvk_ref,
+    buf_ref, rows_ref, got_ref, o_send, o_recv, r_send, r_recv,
+):
+    ctx, head = me()
+    owners = owner_stream()
+    rows = rows_stream()
+    barrier = pltpu.get_barrier_semaphore()
+    for k in range(4):
+        signal(barrier, owners.src(k))
+    for k in range(8):
+        signal(barrier, rows.src(k))
+    summed = jnp.sum(parts_ref[...], axis=0) * (1.0 / (32.0 * 2048.0))
+    for k in range(8):
+        rows_ref[k, 0:3, :] = summed[3 * k : 3 * k + 3, :]
+        rows_ref[k, 3:8, :] = jnp.zeros((5, 2 * KEY), F32)
+    pl.semaphore_wait(barrier, 12)
+    for k in range(8):
+        remote(rows_ref.at[k], got_ref.at[rows.slot], r_send.at[k], r_recv.at[rows.slot], rows.dst(k)).start()
+    inputs = x_ref[...].astype(F32)
+    count, features = inputs.shape
+    acc = jnp.zeros((count, features), F32)
+    for h in range(HEADS):
+        w = jnp.concatenate([wq_ref[:, h * KEY : (h + 1) * KEY], wk_ref[:, h * KEY : (h + 1) * KEY]], axis=1)
+        acc = acc + dot(pair_ref[h], w, ((1,), (1,)))
+        acc = acc + dot(dv_ref[h], wv_ref[:, h * VAL : (h + 1) * VAL], ((1,), (1,)))
+    gained = acc * gain_ref[...]
+    spread = jnp.sqrt(jnp.mean(inputs * inputs, axis=-1, keepdims=True) + 1e-06)
+    along = jnp.sum(gained * inputs, axis=-1, keepdims=True)
+    inv = 1.0 / spread
+    buf_ref[...] = (
+        grad_ref[...] + gained * inv - inputs * (along / (features * spread * spread * spread))
+    ).astype(BF16)
+    for k in range(4):
+        remote(
+            buf_ref.at[pl.ds(64 * k, 64)], out_c_ref.at[owners.slot], o_send.at[k], o_recv.at[owners.slot], owners.dst(k)
+        ).start()
+    for k in range(8):
+        remote(rows_ref.at[k], got_ref.at[k], r_send.at[k], r_recv.at[k], rows.dst(k)).wait()
+    for k in range(8):
+        gvq_ref[:, k * KEY : (k + 1) * KEY] = got_ref[k, 0:3, :KEY]
+        gvk_ref[:, k * KEY : (k + 1) * KEY] = got_ref[k, 0:3, KEY:]
+    for k in range(4):
+        remote(
+            buf_ref.at[pl.ds(64 * k, 64)], out_c_ref.at[k], o_send.at[k], o_recv.at[k], owners.dst(k)
+        ).wait()
+
+
+def finish_rows(x_home, gradient, norm_gain, pair, dv, wq, wk, wv, parts, collective_id):
+    rows, features = x_home.shape
+    vmem = pl.BlockSpec(memory_space=pltpu.VMEM)
+    return pl.pallas_call(
+        final_kernel,
+        out_shape=[
+            jax.ShapeDtypeStruct((4, 64, features), BF16),
+            jax.ShapeDtypeStruct((3, HEADS * KEY), F32),
+            jax.ShapeDtypeStruct((3, HEADS * KEY), F32),
+        ],
+        in_specs=[vmem] * 9,
+        out_specs=[pl.BlockSpec(memory_space=pl.ANY), vmem, vmem],
+        scratch_shapes=[
+            pltpu.VMEM((rows, features), BF16),
+            pltpu.VMEM((8, 8, 2 * KEY), F32),
+            pltpu.VMEM((8, 8, 2 * KEY), F32),
+            pltpu.SemaphoreType.DMA((4,)),
+            pltpu.SemaphoreType.DMA((4,)),
+            pltpu.SemaphoreType.DMA((8,)),
+            pltpu.SemaphoreType.DMA((8,)),
+        ],
+        compiler_params=pltpu.CompilerParams(
+            collective_id=collective_id, has_side_effects=True, vmem_limit_bytes=VMEM_LIMIT
+        ),
+    )(x_home, gradient, norm_gain, pair, dv, wq, wk, wv, parts)
 
 
 def per_device(
@@ -377,79 +663,21 @@
     )
     proj = jnp.dot(normed_all, joined, preferred_element_type=F32).astype(BF16)
     out, lse, att, q, k, v = attend_forward(proj)
-    (attended,) = exchange([out.reshape(8, 256, 2 * VAL)], [group_stream], 2)
-    out_weight = w_out.reshape((HEADS, VAL, features))
-    mixed = inputs + jnp.einsum("hlv,hvc->lc", attended[..., :VAL], out_weight, preferred_element_type=F32)
-    tangent_mixed = jnp.einsum("hlv,hvc->lc", attended[..., VAL:], out_weight, preferred_element_type=F32)
-    slopes = []
-    for layer in range(2):
-        dilation = dilations[layer]
-        activated, act_slope = gelu_pair(mixed)
-        stacked = jnp.stack([activated.astype(BF16), (act_slope * tangent_mixed).astype(BF16)])
-        padded = extended(stacked)
-        inner = 0.0
-        for tap in range(3):
-            window = lax.dynamic_slice_in_dim(padded, DMAX + (tap - 1) * dilation, 256, 1)
-            inner = inner + jnp.einsum("slc,cf->slf", window, conv_weight[layer, tap], preferred_element_type=F32)
-        hidden_value, hidden_slope = gelu_pair(inner[0])
-        hidden = jnp.stack([hidden_value.astype(BF16), (hidden_slope * inner[1]).astype(BF16)])
-        pointwise = jnp.einsum("slf,fc->slc", hidden, point_weight[layer], preferred_element_type=F32)
-        mixed = mixed + pointwise[0]
-        tangent_mixed = tangent_mixed + pointwise[1]
-        slopes.append((act_slope, hidden_slope, dilation))
-    output_tangent = tangent_mixed.astype(BF16)
-    gradient = curve * tangent_mixed
-    for layer in (1, 0):
-        act_slope, hidden_slope, dilation = slopes[layer]
-        grad_inner = (
-            jnp.einsum("lc,fc->lf", gradient.astype(BF16), point_weight[layer], preferred_element_type=F32)
-            * hidden_slope
-        ).astype(BF16)
-        padded = extended(grad_inner)
-        grad_act = 0.0
-        for tap in range(3):
-            window = lax.dynamic_slice_in_dim(padded, DMAX - (tap - 1) * dilation, 256, 0)
-            grad_act = grad_act + jnp.einsum("lf,cf->lc", window, conv_weight[layer, tap], preferred_element_type=F32)
-        gradient = gradient + grad_act * act_slope
-    grad_attended = jnp.einsum("lc,hvc->hlv", gradient.astype(BF16), out_weight, preferred_element_type=F32).astype(
-        BF16
+    (attended,) = exchange([out.reshape(2, 8, 256, VAL).transpose(1, 0, 2, 3)], [group_stream], 2)
+    out_t, gradient, grad_item = conv_chain(
+        dilations, attended, x_home.reshape(256, features), curve, w_out, conv_weight, point_weight, 3
     )
-    (grad_item,) = exchange([grad_attended], [group_stream], 3)
     dq, dk, dv = attend_backward(q, k, v, grad_item.reshape(2048, VAL), lse, att)
     pair = jnp.concatenate([dq, dk], axis=1)
     part = lax.dot_general(normed_all, pair, (((0,), (0,)), ((), ())), preferred_element_type=F32)
-    grads, parts = exchange(
-        [jnp.concatenate([pair, dv], axis=1).reshape(8, 256, 2 * KEY + VAL), part.reshape(32, 24, 2 * KEY)],
-        [group_stream, plane_stream],
+    pairs, dvs, parts = exchange(
+        [pair.reshape(8, 256, 2 * KEY), dv.reshape(8, 256, VAL), part.reshape(32, 24, 2 * KEY)],
+        [group_stream, group_stream, plane_stream],
         4,
     )
-    summed = jnp.sum(parts, axis=0) / (32.0 * 2048.0)
-    joined_grad = jnp.concatenate(
-        [
-            w_query.reshape(features, HEADS, KEY),
-            w_key.reshape(features, HEADS, KEY),
-            w_value.reshape(features, HEADS, VAL),
-        ],
-        axis=2,
+    out_c, gv_query, gv_key = finish_rows(
+        x_home.reshape(256, features), gradient, norm_gain[None, :], pairs, dvs, w_query, w_key, w_value, parts, 5
     )
-    grad_normed = jnp.einsum("hld,chd->lc", grads, joined_grad, preferred_element_type=F32)
-    gained = grad_normed * norm_gain
-    input_cotangent = (
-        gradient
-        + gained / spread
-        - inputs * jnp.sum(gained * inputs, axis=-1, keepdims=True) / (features * spread * spread * spread)
-    ).astype(BF16)
-    out_t, out_c, rows = exchange(
-        [
-            output_tangent.reshape(4, 64, features),
-            input_cotangent.reshape(4, 64, features),
-            summed.reshape(8, 3, 2 * KEY),
-        ],
-        [owner_stream, owner_stream, rows_stream],
-        5,
-    )
-    gv_query = rows[:, :, :KEY].transpose(1, 0, 2).reshape(3, HEADS * KEY)
-    gv_key = rows[:, :, KEY:].transpose(1, 0, 2).reshape(3, HEADS * KEY)
     return out_t, out_c, gv_query, gv_key
 
 

time: 269 us -> 226 us (0.84)
  starting transfers between devices: 24.2 us -> 0 us
  Pallas kernels: 161 us -> 182 us
  matrix products: 26.8 us -> 6.94 us
  local copies, waits for them, and re-layouts: 35.3 us -> 25.9 us
  between operations: 7.68 us -> 0.87 us
  other arithmetic: 10.2 us -> 6.95 us
  waiting for transfers between devices: 3.12 us -> 0 us
    pallas_call x0 -> x2, Pallas kernels: none -> 60.6 us  [the longest x1 39.6 us: conv_chain(): pl.pallas_call(conv_kernel, out_shape=[jax.ShapeDtypeStruct((4, 64, featu...]
    pallas_call x5 -> x3, Pallas kernels: 106 us -> 66.6 us  [exchange(): pl.pallas_call(kernel, out_shape=[jax.ShapeDtypeStruct(a.shape, a.dtype)...]
    ppermute x8 -> x0, starting transfers between devices: 24.2 us -> none  [the longest x4 14.4 us: extended(): down = lax.ppermute(cells[..., :DMAX, :], ('ctx', 'head'), neighbours(-1))]
    dot_general x19 -> x0, matrix products: 18.5 us -> none  [the longest x6 7.86 us: per_device(): jnp.einsum('slc,cf->slf', window, conv_weight[layer, tap], preferred_elem...]
    unnamed x32 -> x17, local copies, waits for them, and re-layouts: 11.4 us -> 5.4 us
    ppermute x8 -> x0, waiting for transfers between devices: 3.12 us -> none  [the longest x4 3.11 us: extended(): down = lax.ppermute(cells[..., :DMAX, :], ('ctx', 'head'), neighbours(-1))]
  transfers between devices with their start and end apart: 8 -> 0, of which waited for: 3 -> 0; matrix products, arithmetic and copies ran while one was open for 6% -> 0% of each run, Pallas kernels for 0% -> 0%
where the time goes in v2:
time: 226 us; the launch traced here: 223 us
  Pallas kernels  182 us (81%)
  local copies, waits for them, and re-layouts  25.9 us (11%)
  other arithmetic  6.95 us (3%)
  matrix products  6.94 us (3%)
    pallas_call x3, Pallas kernels, exchange(): pl.pallas_call(kernel, out_shape=[jax.ShapeDtypeStruct(a.shape, a.dtype)...  66.6 us
    pallas_call x1, Pallas kernels, conv_chain(): pl.pallas_call(conv_kernel, out_shape=[jax.ShapeDtypeStruct((4, 64, featu...  39.6 us
    pallas_call x1, Pallas kernels, gather(): pl.pallas_call(kernel, out_shape=jax.ShapeDtypeStruct((8,) + rows.shape,...  23.8 us
    pallas_call x1, Pallas kernels, finish_rows(): pl.pallas_call(final_kernel, out_shape=[jax.ShapeDtypeStruct((4, 64, feat...  21 us
    pallas_call x1, Pallas kernels, attend_forward(): pl.pallas_call(attend_forward_kernel, grid=(length // BLOCK,), out_shape=...  16.5 us
    pallas_call x1, Pallas kernels, attend_backward(): pl.pallas_call(attend_backward_kernel, grid=(length // BLOCK,), out_shape...  14.3 us
    unnamed x17, local copies, waits for them, and re-layouts  5.4 us

profile of v2, /device:TPU:2, one launch (start us, length us, event | category | flops | bytes accessed | tf_op | source)
XLA Modules:
  0.0 222.5 jit_solution(9224294361367508649)
XLA Ops:
  0.7 1.1 constant_dynamic-slice_fusion
  1.8 1.2 constant_dynamic-slice_fusion.1
  3.1 1.2 constant_dynamic-slice_fusion.3
  5.4 18.4 %shard_map.147 = (bf16[4,64,768]{2,1,0:T(8,128)(2,1)}, f32[4,8,128]{2,1,0:T(8,128)}) custom-call(bf16[4,64,768]{2,1,0:T(8,128)(2,1)} %refs_0_.1, f32[4,8,128]{2,1,0:T(8,128)} %pad.5.refs_1_), custom_call_target="tpu_custom_call" | custom-call | tf_op jit(solution)/shard_map/pallas_call | solution.py:160
  23.7 1.2 multiply_reduce_fusion.1
  25.0 1.9 multiply_convert_fusion.x_ref
  26.9 23.8 %shard_map.148 = bf16[8,256,768]{2,1,0:T(8,128)(2,1)} custom-call(bf16[256,768]{1,0:T(8,128)(2,1)} %multiply_convert_fusion.x_ref), custom_call_target="tpu_custom_call" | custom-call | tf_op jit(solution)/shard_map/pallas_call | solution.py:198
  50.8 3.2 %convolution_convert_fusion = bf16[2048,352]{0,1:T(8,128)(2,1)S(1)} fusion(bf16[2048,768]{1,0:T(8,128)(2,1)} %bitcast.24, bf16[768,352]{1,0:T(8,128)(2,1)S(1)} %concatenate.15), kind=kOutput, calls=%fused_computation | convolution fusion | flops 1108017152 | bytes 5128192 | tf_op jit(solution)/shard_map/dot_general | solution.py:664
  54.0 0.8 slice_bitcast_fusion
  54.8 1.0 copy.26.qt_ref
  55.9 1.0 copy.27.q_ref
  56.9 1.0 copy.29.k_ref
  58.2 1.0 concatenate.18.clone.v_ref
  59.3 1.0 copy.28.kt_ref
  60.3 16.5 %shard_map.149 = (bf16[2,2048,96]{2,1,0:T(8,128)(2,1)}, f32[8,2048]{1,0:T(8,128)}, f32[2048,128]{1,0:T(8,128)}) custom-call(bf16[2048,128]{1,0:T(8,128)(2,1)} %copy.26.qt_ref, bf16[2048,64]{1,0:T(8,128)(2,1)} %copy.27.q_ref, bf16[2048,128]{1,0:T(8,128)(2,1)} %copy.28.kt_ref, bf16[2048,64]{1,0:T(8,128)(2,1)} %copy.29.k_ref, ...), custom_call_target="tpu_custom_call" | custom-call | tf_op jit(solution)/shard_map/pallas_call | solution.py:241
  76.8 2.3 %copy.43 = bf16[2,8,256,96]{3,2,0,1:T(8,128)(2,1)} copy(bf16[2,8,256,96]{3,2,1,0:T(8,128)(2,1)} %bitcast.33) | data formatting | bytes 1572864 | tf_op jit(solution)/shard_map/reshape | solution.py:666
  79.0 15.2 %shard_map.150.att_ref = bf16[8,2,256,96]{3,2,1,0:T(8,128)(2,1)} custom-call(bf16[8,2,256,96]{3,2,1,0:T(8,128)(2,1)} %bitcast.30), custom_call_target="tpu_custom_call" | custom-call | tf_op jit(solution)/shard_map/pallas_call | solution.py:160
  94.2 0.7 slice_reduce_fusion
  95.0 0.8 reshape_squeeze.4.curve_ref
  95.8 39.6 %shard_map.151 = (bf16[4,64,768]{2,1,0:T(8,128)(2,1)}, f32[256,768]{1,0:T(8,128)}, bf16[8,256,96]{2,1,0:T(8,128)(2,1)}) custom-call(s32[2]{0:T(128)} %dil_ref.1, bf16[8,2,256,96]{3,2,1,0:T(8,128)(2,1)} %shard_map.150.att_ref, bf16[256,768]{1,0:T(8,128)(2,1)} %bitcast.27, f32[256,1]{1,0:T(8,128)} %reshape_squeeze.4.curve_ref, bf16[768,768]{1,0:T(8,128)(2,1)} %w_out_ref.1, ...), custom_call_target="tpu_custom_call" | custom-call | tf_op jit(solution)/shard_map/pallas_call | solution.py:515
  135.4 1.5 multiply_reduce_fusion
  137.6 14.3 %shard_map.152 = (bf16[64,2048]{1,0:T(8,128)(2,1)}, bf16[2048,64]{1,0:T(8,128)(2,1)}, bf16[2048,96]{1,0:T(8,128)(2,1)}) custom-call(bf16[2048,64]{1,0:T(8,128)(2,1)} %copy.27.q_ref, bf16[2048,64]{1,0:T(8,128)(2,1)} %copy.29.k_ref, bf16[2048,96]{1,0:T(8,128)(2,1)} %copy-done.1, bf16[2048,96]{1,0:T(8,128)(2,1)} %bitcast.31, ...), custom_call_target="tpu_custom_call" | custom-call | tf_op jit(solution)/shard_map/pallas_call | solution.py:292
  151.9 2.0 copy.37
  153.8 2.3 %pad_maximum_fusion.1 = bf16[2048,128]{1,0:T(8,128)(2,1)} fusion(bf16[2048,64]{1,0:T(8,128)(2,1)} %get-tuple-element.30, bf16[2048,64]{1,0:T(8,128)(2,1)} %bitcast.32), kind=kLoop, calls=%fused_computation.6 | loop fusion | flops 1048576 | bytes 1048576 | tf_op jit(solution)/shard_map/concatenate | solution.py:671
  156.1 2.9 %copy.38 = bf16[768,2048]{1,0:T(8,128)(2,1)} copy(bf16[768,2048]{0,1:T(8,128)(2,1)S(1)} %bitcast.25) | data formatting | bytes 6291456 | tf_op jit(solution)/shard_map/dot_general | solution.py:672
  159.0 3.7 %fusion.refs_2_ = f32[32,24,128]{2,1,0:T(8,128)} fusion(bf16[32,24,2048]{2,1,0:T(8,128)(2,1)} %bitcast.26, bf16[2048,128]{1,0:T(8,128)(2,1)} %pad_maximum_fusion.1), kind=kOutput, calls=%fused_computation.7 | convolution fusion | flops 402653184 | bytes 4063232 | tf_op jit(solution)/shard_map/dot_general | solution.py:672
  162.8 33.0 %shard_map.153 = (bf16[8,256,128]{2,1,0:T(8,128)(2,1)}, bf16[8,256,96]{2,1,0:T(8,128)(2,1)}, f32[32,24,128]{2,1,0:T(8,128)}) custom-call(bf16[8,256,128]{2,1,0:T(8,128)(2,1)} %bitcast.29, bf16[8,256,96]{2,1,0:T(8,128)(2,1)} %bitcast.34, f32[32,24,128]{2,1,0:T(8,128)} %fusion.refs_2_), custom_call_target="tpu_custom_call" | custom-call | tf_op jit(solution)/shard_map/pallas_call | solution.py:160
  196.4 21.0 %shard_map.154 = (bf16[4,64,768]{2,1,0:T(8,128)(2,1)}, f32[3,512]{1,0:T(4,128)}, f32[3,512]{1,0:T(4,128)}) custom-call(bf16[256,768]{1,0:T(8,128)(2,1)} %bitcast.28, f32[256,768]{1,0:T(8,128)} %get-tuple-element.25.grad_ref, f32[1,768]{1,0:T(1,128)} %broadcast_in_dim.7.gain_ref, bf16[8,256,128]{2,1,0:T(8,128)(2,1)} %get-tuple-element.32.pair_ref, ...), custom_call_target="tpu_custom_call" | custom-call | tf_op jit(solution)/shard_map/pallas_call | solution.py:602
  217.4 0.7 copy.48
  218.2 1.8 copy.49
  219.9 1.3 copy.50
  221.2 1.3 copy.51
  (22 shorter events, 2.8 us)
Async XLA Ops:
  0.6 4.1 %copy-start.5 = (f32[4,64]{1,0:T(4,128)S(1)}, f32[4,64]{1,0:T(4,128)}, u32[]{:S(2)}) copy-start(f32[4,64]{1,0:T(4,128)} %param.23) | copy-start | bytes 3076
  0.6 24.3 %copy-start.4 = (f32[768]{0:T(1024)S(1)}, f32[768]{0:T(1024)}, u32[]{:S(2)}) copy-start(f32[768]{0:T(1024)} %param.13) | copy-start | bytes 9220
  58.2 20.8 %copy-start.1 = (bf16[2048,96]{1,0:T(8,128)(2,1)}, bf16[2048,96]{1,0:T(8,128)(2,1)S(1)}, u32[]{:S(2)}) copy-start(bf16[2048,96]{1,0:T(8,128)(2,1)S(1)} %copy.41.v_ref) | copy-start | bytes 1179652
  95.8 39.6 %copy-start.2 = (f32[2048,128]{1,0:T(8,128)S(1)}, f32[2048,128]{1,0:T(8,128)}, u32[]{:S(2)}) copy-start(f32[2048,128]{1,0:T(8,128)} %get-tuple-element.28) | copy-start | bytes 3145732
  135.4 20.7 %copy-start = (bf16[8,256,768]{2,1,0:T(8,128)(2,1)S(1)}, bf16[8,256,768]{2,1,0:T(8,128)(2,1)}, u32[]{:S(2)}) copy-start(bf16[8,256,768]{2,1,0:T(8,128)(2,1)} %shard_map.148) | copy-start | bytes 9437188
  162.8 54.6 %copy-start.3 = (bf16[4,64,768]{2,1,0:T(8,128)(2,1)S(1)}, bf16[4,64,768]{2,1,0:T(8,128)(2,1)}, u32[]{:S(2)}) copy-start(bf16[4,64,768]{2,1,0:T(8,128)(2,1)} %get-tuple-element.50) | copy-start | bytes 1179652

commit v3 on v2

--- a/solution.py
+++ b/solution.py
@@ -1,5 +1,3 @@
-import functools
-
 import jax
 import jax.numpy as jnp
 from jax import lax
@@ -108,213 +106,208 @@
     return Stream(8, lambda i: (r, i), src, chunk_of(ctx, head), None)
 
 
-def exchange(arrays, kinds, collective_id):
-    count = len(arrays)
-
-    def kernel(*refs):
-        xs, outs, sems = refs[:count], refs[count : 2 * count], refs[2 * count :]
-        streams = [kind() for kind in kinds]
-        barrier = pltpu.get_barrier_semaphore()
-        total = 0
-        for stream in streams:
-            first = 0 if stream.own is None else 1
-            base = 0 if stream.own is None else stream.own
-
-            def greet(i, carry, stream=stream, base=base):
-                signal(barrier, stream.src((base + i) % stream.count))
-                return carry
-
-            lax.fori_loop(first, stream.count, greet, 0)
-            total += stream.count - first
-        pl.semaphore_wait(barrier, total)
-        for n, stream in enumerate(streams):
-            x_ref, o_ref, send, recv = xs[n], outs[n], sems[2 * n], sems[2 * n + 1]
-            first = 0 if stream.own is None else 1
-            base = stream.slot if stream.own is None else stream.own
-
-            def start(i, carry, stream=stream, base=base, x_ref=x_ref, o_ref=o_ref, send=send, recv=recv):
-                k = (base + i) % stream.count
-                remote(x_ref.at[k], o_ref.at[stream.slot], send.at[k], recv.at[stream.slot], stream.dst(k)).start()
-                return carry
-
-            lax.fori_loop(first, stream.count, start, 0)
-            if first:
-                local = pltpu.make_async_copy(x_ref.at[base], o_ref.at[base], send.at[base])
-                local.start()
-                local.wait()
-        for n, stream in enumerate(streams):
-            x_ref, o_ref, send, recv = xs[n], outs[n], sems[2 * n], sems[2 * n + 1]
-            first = 0 if stream.own is None else 1
-            base = stream.slot if stream.own is None else stream.own
-
-            def finish(i, carry, stream=stream, base=base, x_ref=x_ref, o_ref=o_ref, send=send, recv=recv):
-                k = (base + i) % stream.count
-                remote(x_ref.at[k], o_ref.at[k], send.at[k], recv.at[k], stream.dst(k)).wait()
-                return carry
-
-            lax.fori_loop(first, stream.count, finish, 0)
-
-    scratch = []
-    for array in arrays:
-        scratch += [pltpu.SemaphoreType.DMA((array.shape[0],))] * 2
-    return pl.pallas_call(
-        kernel,
-        out_shape=[jax.ShapeDtypeStruct(a.shape, a.dtype) for a in arrays],
-        in_specs=[pl.BlockSpec(memory_space=pl.ANY)] * count,
-        out_specs=[pl.BlockSpec(memory_space=pl.ANY)] * count,
-        scratch_shapes=scratch,
-        compiler_params=pltpu.CompilerParams(collective_id=collective_id, has_side_effects=True),
-    )(*arrays)
-
-
-def gather(rows, collective_id):
-    def kernel(x_ref, o_ref, send, recv, fsend, frecv, local):
-        ctx, head = me()
-        j = chunk_of(ctx, head)
-        core = j % 2
-        sibling = member(ctx, head, j - core + 1 - core)
-        barrier = pltpu.get_barrier_semaphore()
-        signal(barrier, sibling)
-        for d in range(1, 4):
-            signal(barrier, member(ctx, head, (j + 2 * d) % 8))
-        pl.semaphore_wait(barrier, 4)
-        for d in range(1, 4):
-            remote(x_ref, o_ref.at[j], send.at[d], recv.at[d], member(ctx, head, (j + 2 * d) % 8)).start()
-        remote(x_ref, o_ref.at[j], send.at[0], recv.at[0], sibling).start()
-        own = pltpu.make_async_copy(x_ref, o_ref.at[j], local)
-        own.start()
-        for d in (1, 3, 2):
-            s = (j + 8 - 2 * d) % 8
-            remote(x_ref, o_ref.at[s], send.at[d], recv.at[d], sibling).wait_recv()
-            remote(o_ref.at[s], o_ref.at[s], fsend.at[d], frecv.at[d], sibling).start()
-        own.wait()
-        other = j - core + 1 - core
-        remote(x_ref, o_ref.at[other], send.at[0], recv.at[0], sibling).wait()
-        for d in (1, 3, 2):
-            s = (other + 8 - 2 * d) % 8
-            remote(o_ref.at[s], o_ref.at[s], fsend.at[d], frecv.at[d], sibling).wait()
-            remote(x_ref, o_ref.at[s], send.at[d], recv.at[d], sibling).wait_send()
-
-    return pl.pallas_call(
-        kernel,
-        out_shape=jax.ShapeDtypeStruct((8,) + rows.shape, rows.dtype),
-        in_specs=[pl.BlockSpec(memory_space=pl.ANY)],
-        out_specs=pl.BlockSpec(memory_space=pl.ANY),
-        scratch_shapes=[pltpu.SemaphoreType.DMA((4,))] * 4 + [pltpu.SemaphoreType.DMA],
-        compiler_params=pltpu.CompilerParams(collective_id=collective_id, has_side_effects=True),
-    )(rows)
-
-
 def dot(a, b, contract):
     return lax.dot_general(a, b, ((contract[0], contract[1]), ((), ())), preferred_element_type=F32)
 
 
-def attend_forward_kernel(qt_ref, q_ref, kt_ref, k_ref, v_ref, o_ref, lse_ref, att_ref):
+def front_kernel(
+    x_ref, c_ref, gain_ref, wq_ref, tq_ref, wk_ref, tk_ref, wv_ref,
+    home_ref, curve_ref, all_ref, qt_ref, kt_ref, v_ref,
+    join_ref, x_send, x_recv, c_send, c_recv, send, recv,
+):
+    ctx, head = me()
+    j = chunk_of(ctx, head)
+    core = j % 2
+    homes = home_stream()
+    barrier = pltpu.get_barrier_semaphore()
+    sibling = j + 1 - 2 * core
+    up, down = (j + 2) % 8, (j + 6) % 8
+    for k in range(4):
+        signal(barrier, homes.src(k))
+    for i in (sibling, up, down):
+        signal(barrier, member(ctx, head, i))
+    pl.semaphore_wait(barrier, 7)
+    for k in range(4):
+        remote(x_ref.at[k], home_ref.at[homes.slot], x_send.at[k], x_recv.at[homes.slot], homes.dst(k)).start()
+        remote(c_ref.at[k], curve_ref.at[homes.slot], c_send.at[k], c_recv.at[homes.slot], homes.dst(k)).start()
+
+    def columns(weight, size, at):
+        shape = (weight.shape[1], 384)
+        row = lax.broadcasted_iota(jnp.int32, shape, 0)
+        column = lax.broadcasted_iota(jnp.int32, shape, 1)
+        hit = (row - j * size == column - at) & (column >= at) & (column < at + size)
+        return dot(weight[...], jnp.where(hit, 1.0, 0.0).astype(BF16), ((1,), (0,)))
+
+    joined = columns(tq_ref, KEY, 0) + columns(wq_ref, KEY, KEY)
+    joined = joined + columns(wk_ref, KEY, 2 * KEY) + columns(tk_ref, KEY, 3 * KEY)
+    joined = joined + columns(wv_ref, VAL, 4 * KEY)
+    join_ref[...] = joined.astype(BF16)
+
+    def piece(i, p):
+        return all_ref.at[i, pl.ds(64 * p, 64)]
+
+    def push(i, p, way, to):
+        remote(piece(i, p), piece(i, p), send.at[i, p, way], recv.at[i, p], member(ctx, head, to)).start()
+
+    def arrived(i, p):
+        remote(piece(i, p), piece(i, p), send.at[i, p, 0], recv.at[i, p], member(ctx, head, sibling)).wait_recv()
+
+    def sent(i, p, way, to):
+        remote(piece(i, p), piece(i, p), send.at[i, p, way], recv.at[i, p], member(ctx, head, to)).wait_send()
+
+    for p in range(4):
+        remote(x_ref.at[p], home_ref.at[p], x_send.at[p], x_recv.at[p], homes.dst(p)).wait_recv()
+        inputs = home_ref[p].astype(F32)
+        spread = jnp.sqrt(jnp.mean(inputs * inputs, axis=-1, keepdims=True) + 1e-06)
+        all_ref[j, 64 * p : 64 * p + 64, :] = (inputs / spread * gain_ref[...]).astype(BF16)
+        push(j, p, 1, up)
+        push(j, p, 2, down)
+        push(j, p, 0, sibling)
+
+    def project(i):
+        rows = pl.ds(pl.multiple_of(i * 256, 256), 256)
+        proj = dot(all_ref[i], join_ref[...], ((1,), (0,))).astype(BF16)
+        qt_ref[rows, :] = proj[:, :128]
+        kt_ref[rows, :] = proj[:, 128:256]
+        lane = lax.broadcasted_iota(jnp.int32, (256, 128), 1)
+        v_ref[rows, :] = jnp.where(lane < VAL, proj[:, 256:].astype(F32), 1.0).astype(BF16)
+
+    for p in range(4):
+        arrived(down, p)
+        if p < 2:
+            push(down, p, 1, up)
+        push(down, p, 0, sibling)
+        arrived(up, p)
+        if p >= 2:
+            push(up, p, 2, down)
+        push(up, p, 0, sibling)
+    project(j)
+    project(down)
+    project(up)
+    far = (j + 4) % 8
+    for p in (0, 2, 1, 3):
+        arrived(far, p)
+        push(far, p, 0, sibling)
+    project(far)
+    for d in (0, 2, 6, 4):
+        i = (sibling + d) % 8
+        for p in range(4):
+            arrived(i, p)
+        project(i)
+    for k in range(4):
+        remote(x_ref.at[k], home_ref.at[k], x_send.at[k], x_recv.at[k], homes.dst(k)).wait_send()
+        remote(c_ref.at[k], curve_ref.at[k], c_send.at[k], c_recv.at[k], homes.dst(k)).wait()
+    for p in range(4):
+        sent(j, p, 1, up)
+        sent(j, p, 2, down)
+        for i in (j, up, down, far):
+            sent(i, p, 0, sibling)
+        if p < 2:
+            sent(down, p, 1, up)
+        else:
+            sent(up, p, 2, down)
+
+
+def front(window_input, curves, gain, wq, tq, wk, tk, wv, collective_id):
+    features = window_input.shape[2]
+    vmem = pl.BlockSpec(memory_space=pltpu.VMEM)
+    length = 2048
+    return pl.pallas_call(
+        front_kernel,
+        out_shape=[
+            jax.ShapeDtypeStruct((4, 64, features), BF16),
+            jax.ShapeDtypeStruct(curves.shape, F32),
+            jax.ShapeDtypeStruct((8, 256, features), BF16),
+            jax.ShapeDtypeStruct((length, 128), BF16),
+            jax.ShapeDtypeStruct((length, 128), BF16),
+            jax.ShapeDtypeStruct((length, 128), BF16),
+        ],
+        in_specs=[vmem] * 8,
+        out_specs=[vmem] * 6,
+        scratch_shapes=[
+            pltpu.VMEM((features, 384), BF16),
+            pltpu.SemaphoreType.DMA((4,)),
+            pltpu.SemaphoreType.DMA((4,)),
+            pltpu.SemaphoreType.DMA((4,)),
+            pltpu.SemaphoreType.DMA((4,)),
+            pltpu.SemaphoreType.DMA((8, 4, 3)),
+            pltpu.SemaphoreType.DMA((8, 4)),
+        ],
+        compiler_params=pltpu.CompilerParams(
+            collective_id=collective_id, has_side_effects=True, vmem_limit_bytes=VMEM_LIMIT
+        ),
+    )(window_input, curves, gain, wq, tq, wk, tk, wv)
+
+
+def forward_kernel(qt_ref, kt_ref, v_ref, out_ref, lse_ref, att_ref, buf_ref, send, recv):
+    ctx, head = me()
+    j = chunk_of(ctx, head)
     scale = KEY**-0.5
-    s = dot(q_ref[...], k_ref[...], ((1,), (1,))) * scale
-    top = jnp.max(s, axis=1, keepdims=True)
-    p = jnp.exp(s - top)
-    ext = dot(p.astype(BF16), v_ref[...], ((1,), (0,)))
-    total = ext[:, VAL : VAL + 1]
-    inv = 1.0 / total
-    ts = dot(qt_ref[...], kt_ref[...], ((1,), (1,))) * scale
-    mean = jnp.sum(p * ts, axis=1, keepdims=True) / jnp.sum(p, axis=1, keepdims=True)
-    tw = p * (ts - mean)
-    tan = dot(tw.astype(BF16), v_ref[...], ((1,), (0,))) * inv
-    att = ext * inv
-    o_ref[0] = att[:, :VAL].astype(BF16)
-    o_ref[1] = tan[:, :VAL].astype(BF16)
-    att_ref[...] = att
-    lse = jnp.broadcast_to(top + jnp.log(total), (BLOCK, 128))
-    lse_ref[...] = lse.T[:8]
-
-
-def attend_forward(proj):
-    length = proj.shape[0]
-    q, tq = proj[:, :KEY], proj[:, KEY : 2 * KEY]
-    k, tk = proj[:, 2 * KEY : 3 * KEY], proj[:, 3 * KEY : 4 * KEY]
-    qt = jnp.concatenate([tq, q], axis=1)
-    kt = jnp.concatenate([k, tk], axis=1)
-    v = jnp.concatenate([proj[:, 4 * KEY :], jnp.ones((length, 128 - VAL), BF16)], axis=1)
-    whole = lambda a: pl.BlockSpec(a.shape, lambda i: (0, 0))
-    part = lambda a: pl.BlockSpec((BLOCK, a.shape[1]), lambda i: (i, 0))
-    out, lse, att = pl.pallas_call(
-        attend_forward_kernel,
-        grid=(length // BLOCK,),
+    barrier = pltpu.get_barrier_semaphore()
+    for d in range(1, 8):
+        signal(barrier, member(ctx, head, (j + d) % 8))
+    pl.semaphore_wait(barrier, 7)
+
+    def block(t, carry):
+        i = (j + 1 + t) % 8
+        rows = pl.ds(pl.multiple_of(i * BLOCK, BLOCK), BLOCK)
+        qt = qt_ref[rows, :]
+        s = dot(qt[:, KEY:], kt_ref[:, :KEY], ((1,), (1,))) * scale
+        top = jnp.max(s, axis=1, keepdims=True)
+        p = jnp.exp(s - top)
+        ext = dot(p.astype(BF16), v_ref[...], ((1,), (0,)))
+        total = ext[:, VAL : VAL + 1]
+        inv = 1.0 / total
+        ts = dot(qt, kt_ref[...], ((1,), (1,))) * scale
+        mean = jnp.sum(p * ts, axis=1, keepdims=True) / jnp.sum(p, axis=1, keepdims=True)
+        tw = p * (ts - mean)
+        tan = dot(tw.astype(BF16), v_ref[...], ((1,), (0,))) * inv
+        att = ext * inv
+        buf_ref[i, 0] = att[:, :VAL].astype(BF16)
+        buf_ref[i, 1] = tan[:, :VAL].astype(BF16)
+
+        @pl.when(t < 7)
+        def _():
+            remote(buf_ref.at[i], out_ref.at[j], send.at[i], recv.at[j], member(ctx, head, i)).start()
+
+        att_ref[rows, :] = att
+        lse_ref[:, rows] = jnp.broadcast_to(top + jnp.log(total), (BLOCK, 128)).T[:8]
+        return carry
+
+    lax.fori_loop(0, 8, block, 0)
+    own = pltpu.make_async_copy(buf_ref.at[j], out_ref.at[j], send.at[j])
+    own.start()
+    own.wait()
+
+    def end(t, carry):
+        i = (j + 1 + t) % 8
+        remote(buf_ref.at[i], out_ref.at[i], send.at[i], recv.at[i], member(ctx, head, i)).wait()
+        return carry
+
+    lax.fori_loop(0, 7, end, 0)
+
+
+def attend_forward(qt, kt, v, collective_id):
+    length = qt.shape[0]
+    vmem = pl.BlockSpec(memory_space=pltpu.VMEM)
+    return pl.pallas_call(
+        forward_kernel,
         out_shape=[
-            jax.ShapeDtypeStruct((2, length, VAL), BF16),
+            jax.ShapeDtypeStruct((8, 2, BLOCK, VAL), BF16),
             jax.ShapeDtypeStruct((8, length), F32),
             jax.ShapeDtypeStruct((length, 128), F32),
         ],
-        in_specs=[part(qt), part(q), whole(kt), whole(k), whole(v)],
-        out_specs=[
-            pl.BlockSpec((2, BLOCK, VAL), lambda i: (0, i, 0)),
-            pl.BlockSpec((8, BLOCK), lambda i: (0, i)),
-            pl.BlockSpec((BLOCK, 128), lambda i: (i, 0)),
+        in_specs=[vmem] * 3,
+        out_specs=[vmem] * 3,
+        scratch_shapes=[
+            pltpu.VMEM((8, 2, BLOCK, VAL), BF16),
+            pltpu.SemaphoreType.DMA((8,)),
+            pltpu.SemaphoreType.DMA((8,)),
         ],
-        compiler_params=pltpu.CompilerParams(vmem_limit_bytes=VMEM_LIMIT),
-    )(qt, q, kt, k, v)
-    return out, lse, att, q, k, v
-
-
-def attend_backward_kernel(q_ref, k_ref, v_ref, g_ref, kT_ref, lse_ref, delta_ref, dqT_ref, dk_ref, dv_ref, acc_ref):
-    i = pl.program_id(0)
-    scale = KEY**-0.5
-    s = dot(k_ref[...], q_ref[...], ((1,), (1,))) * scale
-    w = jnp.exp(s - lse_ref[0:1, :])
-    dp = dot(v_ref[...], g_ref[...], ((1,), (1,)))
-    ds = (w * (dp - delta_ref[0:1, :]) * scale).astype(BF16)
-    dk_ref[...] = dot(ds, q_ref[...], ((1,), (0,))).astype(BF16)
-    dv_ref[...] = dot(w.astype(BF16), g_ref[...], ((1,), (0,))).astype(BF16)
-    dq = dot(kT_ref[...], ds, ((1,), (0,)))
-
-    @pl.when(i == 0)
-    def _():
-        acc_ref[...] = dq
-
-    @pl.when(i > 0)
-    def _():
-        acc_ref[...] += dq
-
-    @pl.when(i == pl.num_programs(0) - 1)
-    def _():
-        dqT_ref[...] = acc_ref[...].astype(BF16)
-
-
-def attend_backward(q, k, v, grad, lse, att):
-    length = q.shape[0]
-    delta = jnp.sum(grad.astype(F32) * att[:, :VAL], axis=1)
-    delta = jnp.broadcast_to(delta[None, :], (8, length))
-    kT = k.T
-    v = v[:, :VAL]
-    whole = lambda a: pl.BlockSpec(a.shape, lambda i: (0, 0))
-    part = lambda a: pl.BlockSpec((BLOCK, a.shape[1]), lambda i: (i, 0))
-    dqT, dk, dv = pl.pallas_call(
-        attend_backward_kernel,
-        grid=(length // BLOCK,),
-        out_shape=[
-            jax.ShapeDtypeStruct((KEY, length), BF16),
-            jax.ShapeDtypeStruct((length, KEY), BF16),
-            jax.ShapeDtypeStruct((length, VAL), BF16),
-        ],
-        in_specs=[
-            whole(q),
-            part(k),
-            part(v),
-            whole(grad),
-            pl.BlockSpec((KEY, BLOCK), lambda i: (0, i)),
-            whole(lse),
-            whole(delta),
-        ],
-        out_specs=[
-            pl.BlockSpec((KEY, length), lambda i: (0, 0)),
-            pl.BlockSpec((BLOCK, KEY), lambda i: (i, 0)),
-            pl.BlockSpec((BLOCK, VAL), lambda i: (i, 0)),
-        ],
-        scratch_shapes=[pltpu.VMEM((KEY, length), F32)],
-        compiler_params=pltpu.CompilerParams(vmem_limit_bytes=VMEM_LIMIT),
-    )(q, k, v, grad, kT, lse, delta)
-    return dqT.T, dk, dv
+        compiler_params=pltpu.CompilerParams(
+            collective_id=collective_id, has_side_effects=True, vmem_limit_bytes=VMEM_LIMIT
+        ),
+    )(qt, kt, v)
 
 
 def gelu_pair(v):
@@ -547,26 +540,106 @@
     )(dilations, attended, x_home, curve, w_out, conv_weight, point_weight)
 
 
-def final_kernel(
-    x_ref, grad_ref, gain_ref, pair_ref, dv_ref, wq_ref, wk_ref, wv_ref, parts_ref,
+def back_kernel(
+    qt_ref, kt_ref, v_ref, g_ref, lse_ref, att_ref, normed_ref,
+    x_ref, grad_ref, gain_ref, wq_ref, wk_ref, wv_ref,
     out_c_ref, gvq_ref, gvk_ref,
-    buf_ref, rows_ref, got_ref, o_send, o_recv, r_send, r_recv,
+    q_ref, kT_ref, delta_ref, acc_ref, pairT_ref,
+    dv_buf, dv_ref, pair_buf, pair_ref, part_buf, part_ref,
+    buf_ref, rows_ref, got_ref,
+    v_send, v_recv, p_send, p_recv, e_send, e_recv, o_send, o_recv, r_send, r_recv,
 ):
     ctx, head = me()
+    j = chunk_of(ctx, head)
+    scale = KEY**-0.5
     owners = owner_stream()
     rows = rows_stream()
+    plane = plane_stream()
     barrier = pltpu.get_barrier_semaphore()
+    for d in range(1, 8):
+        signal(barrier, member(ctx, head, (j + d) % 8))
     for k in range(4):
         signal(barrier, owners.src(k))
     for k in range(8):
         signal(barrier, rows.src(k))
-    summed = jnp.sum(parts_ref[...], axis=0) * (1.0 / (32.0 * 2048.0))
-    for k in range(8):
-        rows_ref[k, 0:3, :] = summed[3 * k : 3 * k + 3, :]
-        rows_ref[k, 3:8, :] = jnp.zeros((5, 2 * KEY), F32)
-    pl.semaphore_wait(barrier, 12)
-    for k in range(8):
-        remote(rows_ref.at[k], got_ref.at[rows.slot], r_send.at[k], r_recv.at[rows.slot], rows.dst(k)).start()
+
+    def greet(d, carry):
+        signal(barrier, plane.src((plane.own + d) % 32))
+        return carry
+
+    lax.fori_loop(1, 32, greet, 0)
+    for c in range(8):
+        at = slice(c * BLOCK, (c + 1) * BLOCK)
+        prod = g_ref[at, :].astype(F32) * att_ref[at, :VAL]
+        prod = jnp.concatenate([prod, jnp.zeros((BLOCK, 128 - VAL), F32)], axis=1)
+        delta_ref[:, at] = jnp.broadcast_to(jnp.sum(prod.T, axis=0, keepdims=True), (8, BLOCK))
+        kT_ref[:, at] = kt_ref[at, :].astype(F32).T[:KEY].astype(BF16)
+    q_ref[...] = qt_ref[:, KEY:]
+    acc_ref[...] = jnp.zeros(acc_ref.shape, F32)
+    pl.semaphore_wait(barrier, 50)
+
+    def block(t, carry):
+        i = (j + 1 + t) % 8
+        at = pl.ds(pl.multiple_of(i * BLOCK, BLOCK), BLOCK)
+        s = dot(kt_ref[at, :KEY], q_ref[...], ((1,), (1,))) * scale
+        w = jnp.exp(s - lse_ref[0:1, :])
+        dp = dot(v_ref[at, :VAL], g_ref[...], ((1,), (1,)))
+        ds = (w * (dp - delta_ref[0:1, :]) * scale).astype(BF16)
+        dv = dot(w.astype(BF16), g_ref[...], ((1,), (0,))).astype(BF16)
+
+        @pl.when(t < 7)
+        def _():
+            dv_buf[i] = dv
+            remote(dv_buf.at[i], dv_ref.at[j], v_send.at[i], v_recv.at[j], member(ctx, head, i)).start()
+
+        @pl.when(t == 7)
+        def _():
+            dv_ref[j] = dv
+
+        dk = dot(ds, q_ref[...], ((1,), (0,)))
+        dk = jnp.concatenate([jnp.zeros((BLOCK, KEY), F32), dk], axis=1)
+        pairT_ref[KEY:, at] = dk.T[KEY:].astype(BF16)
+        acc_ref[...] += dot(kT_ref[:, at], ds, ((1,), (0,)))
+        return carry
+
+    lax.fori_loop(0, 8, block, 0)
+    pairT_ref[:KEY, :] = acc_ref[...].astype(BF16)
+
+    def pair_out(t, carry):
+        i = (j + 1 + t) % 8
+        at = pl.ds(pl.multiple_of(i * BLOCK, BLOCK), BLOCK)
+        pair = pairT_ref[:, at].astype(F32).T.astype(BF16)
+
+        @pl.when(t < 7)
+        def _():
+            pair_buf[i] = pair
+            remote(pair_buf.at[i], pair_ref.at[j], p_send.at[i], p_recv.at[j], member(ctx, head, i)).start()
+
+        @pl.when(t == 7)
+        def _():
+            pair_ref[j] = pair
+
+        return carry
+
+    lax.fori_loop(0, 8, pair_out, 0)
+    part = dot(pairT_ref[...], normed_ref[...], ((1,), (0,)))
+    part_buf[...] = part.T.reshape(part_buf.shape)
+    part_ref[plane.own] = part_buf[plane.own]
+
+    def part_out(d, carry):
+        k = (plane.own + d) % 32
+        remote(part_buf.at[k], part_ref.at[plane.slot], e_send.at[k], e_recv.at[plane.slot], plane.dst(k)).start()
+        return carry
+
+    lax.fori_loop(1, 32, part_out, 0)
+
+    def group_end(t, carry):
+        i = (j + 1 + t) % 8
+        remote(dv_buf.at[i], dv_ref.at[i], v_send.at[i], v_recv.at[i], member(ctx, head, i)).wait()
+        remote(pair_buf.at[i], pair_ref.at[i], p_send.at[i], p_recv.at[i], member(ctx, head, i)).wait()
+        return carry
+
+    lax.fori_loop(0, 7, group_end, 0)
     inputs = x_ref[...].astype(F32)
     count, features = inputs.shape
     acc = jnp.zeros((count, features), F32)
@@ -585,6 +658,19 @@
         remote(
             buf_ref.at[pl.ds(64 * k, 64)], out_c_ref.at[owners.slot], o_send.at[k], o_recv.at[owners.slot], owners.dst(k)
         ).start()
+
+    def part_end(d, carry):
+        k = (plane.own + d) % 32
+        remote(part_buf.at[k], part_ref.at[k], e_send.at[k], e_recv.at[k], plane.dst(k)).wait()
+        return carry
+
+    lax.fori_loop(1, 32, part_end, 0)
+    summed = jnp.sum(part_ref[...], axis=0) * (1.0 / (32.0 * 2048.0))
+    for k in range(8):
+        rows_ref[k, 0:3, :] = summed[3 * k : 3 * k + 3, :]
+        rows_ref[k, 3:8, :] = jnp.zeros((5, 2 * KEY), F32)
+    for k in range(8):
+        remote(rows_ref.at[k], got_ref.at[rows.slot], r_send.at[k], r_recv.at[rows.slot], rows.dst(k)).start()
     for k in range(8):
         remote(rows_ref.at[k], got_ref.at[k], r_send.at[k], r_recv.at[k], rows.dst(k)).wait()
     for k in range(8):
@@ -596,31 +682,50 @@
         ).wait()
 
 
-def finish_rows(x_home, gradient, norm_gain, pair, dv, wq, wk, wv, parts, collective_id):
+def back(qt, kt, v, grad_item, lse, att, normed_all, x_home, gradient, gain, wq, wk, wv, collective_id):
     rows, features = x_home.shape
+    length = qt.shape[0]
     vmem = pl.BlockSpec(memory_space=pltpu.VMEM)
+    dma = pltpu.SemaphoreType.DMA
     return pl.pallas_call(
-        final_kernel,
+        back_kernel,
         out_shape=[
             jax.ShapeDtypeStruct((4, 64, features), BF16),
             jax.ShapeDtypeStruct((3, HEADS * KEY), F32),
             jax.ShapeDtypeStruct((3, HEADS * KEY), F32),
         ],
-        in_specs=[vmem] * 9,
+        in_specs=[vmem] * 13,
         out_specs=[pl.BlockSpec(memory_space=pl.ANY), vmem, vmem],
         scratch_shapes=[
+            pltpu.VMEM((length, KEY), BF16),
+            pltpu.VMEM((KEY, length), BF16),
+            pltpu.VMEM((8, length), F32),
+            pltpu.VMEM((KEY, length), F32),
+            pltpu.VMEM((2 * KEY, length), BF16),
+            pltpu.VMEM((8, rows, VAL), BF16),
+            pltpu.VMEM((8, rows, VAL), BF16),
+            pltpu.VMEM((8, rows, 2 * KEY), BF16),
+            pltpu.VMEM((8, rows, 2 * KEY), BF16),
+            pltpu.VMEM((32, features // 32, 2 * KEY), F32),
+            pltpu.VMEM((32, features // 32, 2 * KEY), F32),
             pltpu.VMEM((rows, features), BF16),
             pltpu.VMEM((8, 8, 2 * KEY), F32),
             pltpu.VMEM((8, 8, 2 * KEY), F32),
-            pltpu.SemaphoreType.DMA((4,)),
-            pltpu.SemaphoreType.DMA((4,)),
-            pltpu.SemaphoreType.DMA((8,)),
-            pltpu.SemaphoreType.DMA((8,)),
+            dma((8,)),
+            dma((8,)),
+            dma((8,)),
+            dma((8,)),
+            dma((32,)),
+            dma((32,)),
+            dma((4,)),
+            dma((4,)),
+            dma((8,)),
+            dma((8,)),
         ],
         compiler_params=pltpu.CompilerParams(
             collective_id=collective_id, has_side_effects=True, vmem_limit_bytes=VMEM_LIMIT
         ),
-    )(x_home, gradient, norm_gain, pair, dv, wq, wk, wv, parts)
+    )(qt, kt, v, grad_item, lse, att, normed_all, x_home, gradient, gain, wq, wk, wv)
 
 
 def per_device(
@@ -638,45 +743,32 @@
     curvature,
 ):
     features = window_input.shape[2]
-    ctx, head = me()
-    j = chunk_of(ctx, head)
     curves = jnp.pad(curvature[:, None, :], ((0, 0), (0, 7), (0, 64)))
-    x_home, c_home = exchange([window_input, curves], [home_stream, home_stream], 0)
-    inputs = x_home.reshape(256, features).astype(F32)
+    gain = norm_gain[None, :]
+    x_home, c_home, normed_all, qt, kt, v = front(
+        window_input, curves, gain, w_query, tangent_query, w_key, tangent_key, w_value, 0
+    )
+    x_home = x_home.reshape(256, features)
     curve = c_home[:, 0, :64].reshape(256, 1)
-    spread = jnp.sqrt(jnp.mean(inputs * inputs, axis=-1, keepdims=True) + 1e-06)
-    normed = (inputs / spread * norm_gain).astype(BF16)
-    normed_all = gather(normed, 1).reshape(2048, features)
-
-    def columns(weight, size):
-        return lax.dynamic_slice_in_dim(weight, j * size, size, 1)
-
-    joined = jnp.concatenate(
-        [
-            columns(w_query, KEY),
-            columns(tangent_query, KEY),
-            columns(w_key, KEY),
-            columns(tangent_key, KEY),
-            columns(w_value, VAL),
-        ],
-        axis=1,
+    attended, lse, att = attend_forward(qt, kt, v, 1)
+    out_t, gradient, grad_item = conv_chain(
+        dilations, attended, x_home, curve, w_out, conv_weight, point_weight, 2
     )
-    proj = jnp.dot(normed_all, joined, preferred_element_type=F32).astype(BF16)
-    out, lse, att, q, k, v = attend_forward(proj)
-    (attended,) = exchange([out.reshape(2, 8, 256, VAL).transpose(1, 0, 2, 3)], [group_stream], 2)
-    out_t, gradient, grad_item = conv_chain(
-        dilations, attended, x_home.reshape(256, features), curve, w_out, conv_weight, point_weight, 3
-    )
-    dq, dk, dv = attend_backward(q, k, v, grad_item.reshape(2048, VAL), lse, att)
-    pair = jnp.concatenate([dq, dk], axis=1)
-    part = lax.dot_general(normed_all, pair, (((0,), (0,)), ((), ())), preferred_element_type=F32)
-    pairs, dvs, parts = exchange(
-        [pair.reshape(8, 256, 2 * KEY), dv.reshape(8, 256, VAL), part.reshape(32, 24, 2 * KEY)],
-        [group_stream, group_stream, plane_stream],
-        4,
-    )
-    out_c, gv_query, gv_key = finish_rows(
-        x_home.reshape(256, features), gradient, norm_gain[None, :], pairs, dvs, w_query, w_key, w_value, parts, 5
+    out_c, gv_query, gv_key = back(
+        qt,
+        kt,
+        v,
+        grad_item.reshape(2048, VAL),
+        lse,
+        att,
+        normed_all.reshape(2048, features),
+        x_home,
+        gradient,
+        gain,
+        w_query,
+        w_key,
+        w_value,
+        3,
     )
     return out_t, out_c, gv_query, gv_key
 

time: 226 us -> 175 us (0.77)
  local copies, waits for them, and re-layouts: 25.9 us -> 7.82 us
  Pallas kernels: 182 us -> 164 us
  other arithmetic: 6.95 us -> 0 us
  matrix products: 6.94 us -> 0 us
    pallas_call x7 -> x3, Pallas kernels: 142 us -> 119 us  [the longest x1 58.7 us: back(): pl.pallas_call(back_kernel, out_shape=[jax.ShapeDtypeStruct((4, 64, featu...]
    dot_general x2 -> x0, matrix products: 6.94 us -> none  [the longest x1 3.72 us: per_device(): lax.dot_general(normed_all, pair, (((0,), (0,)), ((), ())), preferred_ele...]
    pallas_call x1, Pallas kernels: 39.6 us -> 45.4 us  [conv_chain(): pl.pallas_call(conv_kernel, out_shape=[jax.ShapeDtypeStruct((4, 64, featu...]
    dynamic_slice x3 -> x0, local copies, waits for them, and re-layouts: 3.54 us -> none  [columns(): return lax.dynamic_slice_in_dim(weight, j * size, size, 1)]
    concatenate x5 -> x0, local copies, waits for them, and re-layouts: 3.51 us -> none  [the longest x2 1.04 us: attend_forward(): kt = jnp.concatenate([k, tk], axis=1)]
    dot_general x1 -> x0, local copies, waits for them, and re-layouts: 2.92 us -> none  [per_device(): lax.dot_general(normed_all, pair, (((0,), (0,)), ((), ())), preferred_ele...]
    reduce_sum x2 -> x0, other arithmetic: 2.69 us -> none  [the longest x1 1.54 us: attend_backward(): delta = jnp.sum(grad.astype(F32) * att[:, :VAL], axis=1)]
    concatenate x2 -> x0, other arithmetic: 2.33 us -> none  [the longest x1 2.29 us: per_device(): pair = jnp.concatenate([dq, dk], axis=1)]
where the time goes in v3:
time: 175 us; the launch traced here: 173 us
  Pallas kernels  164 us (94%)
  local copies, waits for them, and re-layouts  7.82 us (4%)
    pallas_call x1, Pallas kernels, back(): pl.pallas_call(back_kernel, out_shape=[jax.ShapeDtypeStruct((4, 64, featu...  58.7 us
    pallas_call x1, Pallas kernels, conv_chain(): pl.pallas_call(conv_kernel, out_shape=[jax.ShapeDtypeStruct((4, 64, featu...  45.4 us
    pallas_call x1, Pallas kernels, front(): pl.pallas_call(front_kernel, out_shape=[jax.ShapeDtypeStruct((4, 64, feat...  37.8 us
    pallas_call x1, Pallas kernels, attend_forward(): pl.pallas_call(forward_kernel, out_shape=[jax.ShapeDtypeStruct((8, 2, BLO...  22.1 us
    unnamed x10, local copies, waits for them, and re-layouts  3.72 us

profile of v3, /device:TPU:2, one launch (start us, length us, event | category | flops | bytes accessed | tf_op | source)
XLA Modules:
  0.0 172.6 jit_solution(5041626878358472682)
XLA Ops:
  0.6 1.3 broadcast_in_dim.7.gain_ref
  1.9 1.3 pad.4.c_ref
  3.2 37.8 %shard_map.147 = (bf16[4,64,768]{2,1,0:T(8,128)(2,1)}, f32[4,8,128]{2,1,0:T(8,128)}, bf16[8,256,768]{2,1,0:T(8,128)(2,1)}, bf16[2048,128]{1,0:T(8,128)(2,1)}, bf...) custom-call(bf16[4,64,768]{2,1,0:T(8,128)(2,1)} %x_ref.1, f32[4,8,128]{2,1,0:T(8,128)} %pad.4.c_ref, ...), custom_call_target="tpu_custom_call" | custom-call | tf_op jit(solution)/shard_map/pallas_call | solution.py:215
  41.0 0.7 slice_reduce_fusion
  41.8 0.8 reshape_squeeze.4.curve_ref
  42.6 22.1 %shard_map.148 = (bf16[8,2,256,96]{3,2,1,0:T(8,128)(2,1)}, f32[8,2048]{1,0:T(8,128)}, f32[2048,128]{1,0:T(8,128)}) custom-call(bf16[2048,128]{1,0:T(8,128)(2,1)} %get-tuple-element.19.qt_ref, bf16[2048,128]{1,0:T(8,128)(2,1)} %get-tuple-element.20.kt_ref, bf16[2048,128]{1,0:T(8,128)(2,1)} %get-tuple-element.21.v_ref), custom_call_target="tpu_custom_call" | custom-call | tf_op jit(solution)/shard_map/pallas_call | solution.py:293
  64.7 45.4 %shard_map.149 = (bf16[4,64,768]{2,1,0:T(8,128)(2,1)}, f32[256,768]{1,0:T(8,128)}, bf16[8,256,96]{2,1,0:T(8,128)(2,1)}) custom-call(s32[2]{0:T(128)} %dil_ref.1, bf16[8,2,256,96]{3,2,1,0:T(8,128)(2,1)} %get-tuple-element.22.att_ref, bf16[256,768]{1,0:T(8,128)(2,1)} %bitcast.5, f32[256,1]{1,0:T(8,128)} %reshape_squeeze.4.curve_ref, ...), custom_call_target="tpu_custom_call" | custom-call | tf_op jit(solution)/shard_map/pallas_call | solution.py:508
  110.1 0.0 copy-start
  110.1 58.7 %shard_map.150 = (bf16[4,64,768]{2,1,0:T(8,128)(2,1)}, f32[3,512]{1,0:T(4,128)}, f32[3,512]{1,0:T(4,128)}) custom-call(bf16[2048,128]{1,0:T(8,128)(2,1)} %get-tuple-element.19.qt_ref, bf16[2048,128]{1,0:T(8,128)(2,1)} %get-tuple-element.20.kt_ref, bf16[2048,128]{1,0:T(8,128)(2,1)} %get-tuple-element.21.v_ref, bf16[2048,96]{1,0:T(8,128)(2,1)} %bitcast.7, ...), custom_call_target="tpu_custom_call" | custom-call | tf_op jit(solution)/shard_map/pallas_call | solution.py:690
  168.8 0.0 copy-start.2
  168.8 0.0 copy-start.1
  168.8 0.0 copy-done
  168.8 0.7 copy.21
  169.6 1.8 %copy.22 = bf16[4,64,768]{2,1,0:T(8,128)(2,1)} copy(bf16[4,64,768]{2,1,0:T(8,128)(2,1)} %get-tuple-element.39) | data formatting | bytes 786432
  171.4 0.0 copy-done.2
  171.4 0.6 copy.23
  172.0 0.0 copy-done.1
  172.0 0.6 copy.24
Async XLA Ops:
  110.1 58.8 %copy-start = (bf16[4,64,768]{2,1,0:T(8,128)(2,1)S(1)}, bf16[4,64,768]{2,1,0:T(8,128)(2,1)}, u32[]{:S(2)}) copy-start(bf16[4,64,768]{2,1,0:T(8,128)(2,1)} %get-tuple-element.38) | copy-start | bytes 1179652
  168.8 2.5 %copy-start.2 = (f32[3,512]{1,0:T(4,128)S(1)}, f32[3,512]{1,0:T(4,128)}, u32[]{:S(2)}) copy-start(f32[3,512]{1,0:T(4,128)} %get-tuple-element.40) | copy-start | bytes 18436
  168.8 3.1 %copy-start.1 = (f32[3,512]{1,0:T(4,128)S(1)}, f32[3,512]{1,0:T(4,128)}, u32[]{:S(2)}) copy-start(f32[3,512]{1,0:T(4,128)} %get-tuple-element.41) | copy-start | bytes 18436

commit v4 on v3

v4 whole, which is shorter than its diff:
```python
import functools

import jax
import jax.numpy as jnp
from jax import lax
from jax.experimental import pallas as pl
from jax.experimental.pallas import tpu as pltpu
from jax.sharding import PartitionSpec as P

HEADS = 8
KEY = 64
VAL = 96
DMAX = 16
MESH = pl.DeviceIdType.MESH
VMEM_LIMIT = 56 * 2**20
F32 = jnp.float32
BF16 = jnp.bfloat16
BLOCK = 256
SCALE = KEY**-0.5


def place(ctx, head):
    return ctx // 8, (ctx // 4) % 2 * 4 + head // 2, ctx % 4, head % 2


def device(y, z, x, core):
    return y * 8 + z // 4 * 4 + x, z % 4 * 2 + core


def chunk_of(ctx, head):
    return ctx // 8 * 2 + head % 2


def member(ctx, head, j):
    _, z, x, _ = place(ctx, head)
    return device(j // 2, z, x, j % 2)


def home_of(ctx, head, b):
    y, z, _, core = place(ctx, head)
    return device(y, core * 4 + (z % 4 + 2) % 4, b, z // 4)


def owner_of(ctx, head, x0):
    y, z, _, core = place(ctx, head)
    return device(y, core * 4 + (z % 4 + 2) % 4, x0, z // 4)


def me():
    return lax.axis_index("ctx"), lax.axis_index("head")


def signal(barrier, target):
    pl.semaphore_signal(barrier, inc=1, device_id=target, device_id_type=MESH)


def remote(src, dst, send, recv, target):
    return pltpu.make_async_remote_copy(
        src_ref=src, dst_ref=dst, send_sem=send, recv_sem=recv, device_id=target, device_id_type=MESH
    )


class Stream:
    def __init__(self, count, dst, src, slot, own):
        self.count, self.dst, self.src, self.slot, self.own = count, dst, src, slot, own


def home_stream():
    ctx, head = me()
    return Stream(4, lambda i: home_of(ctx, head, i), lambda k: owner_of(ctx, head, k), ctx % 4, None)


def owner_stream():
    ctx, head = me()
    return Stream(4, lambda i: owner_of(ctx, head, i), lambda k: home_of(ctx, head, k), ctx % 4, None)


def group_stream():
    ctx, head = me()
    return Stream(
        8, lambda i: member(ctx, head, i), lambda k: member(ctx, head, k), chunk_of(ctx, head), chunk_of(ctx, head)
    )


def plane_stream():
    ctx, head = me()
    y, z, x, core = place(ctx, head)

    def at(r):
        return device(y, r // 4 % 2 * 4 + r // 8, (r + 3) % 4, core)

    rank = z % 4 * 8 + z // 4 * 4 + (x + 1) % 4
    return Stream(32, at, at, rank, rank)


def rows_stream():
    ctx, head = me()
    _, z, x, _ = place(ctx, head)
    r = z % 4 * 8 + z // 4 * 4 + (x + 1) % 4

    def src(k):
        return device(k // 2, ctx // 4 % 2 * 4 + ctx // 8, (ctx + 3) % 4, k % 2)

    return Stream(8, lambda i: (r, i), src, chunk_of(ctx, head), None)


def dot(a, b, contract):
    return lax.dot_general(a, b, ((contract[0], contract[1]), ((), ())), preferred_element_type=F32)


class Refs:
    def __init__(self, names, refs):
        for name, ref in zip(names, refs, strict=True):
            setattr(self, name, ref)


def greet_all(r, barrier):
    ctx, head = me()
    j = chunk_of(ctx, head)
    homes, owners, rows, plane = home_stream(), owner_stream(), rows_stream(), plane_stream()
    for k in range(4):
        signal(barrier, homes.src(k))
        signal(barrier, owners.src(k))
    for d in range(1, 8):
        signal(barrier, member(ctx, head, (j + d) % 8))
    for k in range(8):
        signal(barrier, rows.src(k))

    def greet(d, carry):
        signal(barrier, plane.src((plane.own + d) % 32))
        return carry

    lax.fori_loop(1, 32, greet, 0)


def front(r):
    ctx, head = me()
    j = chunk_of(ctx, head)
    core = j % 2
    homes = home_stream()
    sibling = j + 1 - 2 * core
    up, down, far = (j + 2) % 8, (j + 6) % 8, (j + 4) % 8
    for k in range(4):
        remote(r.x.at[k], r.home.at[homes.slot], r.x_send.at[k], r.x_recv.at[homes.slot], homes.dst(k)).start()
    for k in range(4):
        r.c_buf[k] = jnp.zeros((8, 128), F32)
        r.c_buf[k, 0:1, 0:64] = r.curvature[k : k + 1, :]
        remote(r.c_buf.at[k], r.c_home.at[homes.slot], r.c_send.at[k], r.c_recv.at[homes.slot], homes.dst(k)).start()

    def columns(weight, size, at, factor):
        shape = (weight.shape[1], 384)
        row = lax.broadcasted_iota(jnp.int32, shape, 0)
        column = lax.broadcasted_iota(jnp.int32, shape, 1)
        hit = (row - j * size == column - at) & (column >= at) & (column < at + size)
        return dot(weight[...], jnp.where(hit, factor, 0.0).astype(BF16), ((1,), (0,)))

    joined = None
    for name, size, at, factor in (
        ("tq", KEY, 0, SCALE),
        ("wq", KEY, KEY, SCALE),
        ("wk", KEY, 2 * KEY, 1.0),
        ("tk", KEY, 3 * KEY, 1.0),
        ("wv", VAL, 4 * KEY, 1.0),
    ):
        fetch(r, name).wait()
        part = columns(getattr(r, name), size, at, factor)
        joined = part if joined is None else joined + part
    r.joined[...] = joined.astype(BF16)

    def piece(i, p):
        return r.normed.at[i, pl.ds(64 * p, 64)]

    def push(i, p, way, to):
        remote(piece(i, p), piece(i, p), r.n_send.at[i, p, way], r.n_recv.at[i, p], member(ctx, head, to)).start()

    def arrived(i, p):
        remote(
            piece(i, p), piece(i, p), r.n_send.at[i, p, 0], r.n_recv.at[i, p], member(ctx, head, sibling)
        ).wait_recv()

    def sent(i, p, way, to):
        remote(piece(i, p), piece(i, p), r.n_send.at[i, p, way], r.n_recv.at[i, p], member(ctx, head, to)).wait_send()

    gain = r.gain[...].reshape(1, -1)
    for p in range(4):
        remote(r.x.at[p], r.home.at[p], r.x_send.at[p], r.x_recv.at[p], homes.dst(p)).wait_recv()
        inputs = r.home[p].astype(F32)
        spread = jnp.sqrt(jnp.mean(inputs * inputs, axis=-1, keepdims=True) + 1e-06)
        r.normed[j, 64 * p : 64 * p + 64, :] = (inputs / spread * gain).astype(BF16)
        push(j, p, 1, up)
        push(j, p, 2, down)
        push(j, p, 0, sibling)

    def project(i):
        rows = pl.ds(pl.multiple_of(i * BLOCK, BLOCK), BLOCK)
        proj = dot(r.normed[i], r.joined[...], ((1,), (0,))).astype(BF16)
        r.qt[rows, :] = proj[:, :128]
        r.kt[rows, :] = proj[:, 128:256]
        lane = lax.broadcasted_iota(jnp.int32, (BLOCK, 128), 1)
        r.v[rows, :] = jnp.where(lane < VAL, proj[:, 256:].astype(F32), 1.0).astype(BF16)

    for p in range(4):
        arrived(down, p)
        if p < 2:
            push(down, p, 1, up)
        push(down, p, 0, sibling)
        arrived(up, p)
        if p >= 2:
            push(up, p, 2, down)
        push(up, p, 0, sibling)
    project(j)
    project(down)
    project(up)
    for p in (0, 2, 1, 3):
        arrived(far, p)
        push(far, p, 0, sibling)
    project(far)
    for d in (0, 2, 6, 4):
        i = (sibling + d) % 8
        for p in range(4):
            arrived(i, p)
        project(i)
    for k in range(4):
        remote(r.x.at[k], r.home.at[k], r.x_send.at[k], r.x_recv.at[k], homes.dst(k)).wait_send()
        remote(r.c_buf.at[k], r.c_home.at[k], r.c_send.at[k], r.c_recv.at[k], homes.dst(k)).wait()
    for p in range(4):
        sent(j, p, 1, up)
        sent(j, p, 2, down)
        for i in (j, up, down, far):
            sent(i, p, 0, sibling)
        if p < 2:
            sent(down, p, 1, up)
        else:
            sent(up, p, 2, down)


def attend_forward(r):
    ctx, head = me()
    j = chunk_of(ctx, head)

    def block(t, carry):
        i = (j + 1 + t) % 8
        rows = pl.ds(pl.multiple_of(i * BLOCK, BLOCK), BLOCK)
        qt = r.qt[rows, :]
        s = dot(qt[:, KEY:], r.kt[:, :KEY], ((1,), (1,)))
        top = jnp.max(s, axis=1, keepdims=True)
        p = jnp.exp(s - top)
        ext = dot(p.astype(BF16), r.v[...], ((1,), (0,)))
        total = ext[:, VAL : VAL + 1]
        inv = 1.0 / total
        ts = dot(qt, r.kt[...], ((1,), (1,)))
        mean = jnp.sum(p * ts, axis=1, keepdims=True) / jnp.sum(p, axis=1, keepdims=True)
        tw = p * (ts - mean)
        tan = dot(tw.astype(BF16), r.v[...], ((1,), (0,))) * inv
        att = ext * inv

        @pl.when(t < 7)
        def _():
            r.att_buf[i, 0] = att[:, :VAL].astype(BF16)
            r.att_buf[i, 1] = tan[:, :VAL].astype(BF16)
            remote(
                r.att_buf.at[i], r.attended.at[j], r.a_send.at[i], r.a_recv.at[j], member(ctx, head, i)
            ).start()

        @pl.when(t == 7)
        def _():
            r.attended[j, 0] = att[:, :VAL].astype(BF16)
            r.attended[j, 1] = tan[:, :VAL].astype(BF16)

        r.att[rows, :] = att
        r.lse[:, rows] = jnp.broadcast_to(top + jnp.log(total), (BLOCK, 128)).T[:8]
        return carry

    lax.fori_loop(0, 8, block, 0)

    def end(t, carry):
        i = (j + 1 + t) % 8
        remote(r.att_buf.at[i], r.attended.at[i], r.a_send.at[i], r.a_recv.at[i], member(ctx, head, i)).wait()
        return carry

    lax.fori_loop(0, 7, end, 0)


def gelu_pair(v):
    root = 0.7978845608028654
    square = v * v
    t = jnp.tanh(root * (v + 0.044715 * v * square))
    half = 0.5 * (1.0 + t)
    return v * half, half + 0.5 * v * (1.0 - t * t) * (root + (3.0 * 0.044715 * root) * square)


def picker(dilation, rows):
    shape = (2 * rows, rows + 2 * DMAX)
    row = lax.broadcasted_iota(jnp.int32, shape, 0)
    column = lax.broadcasted_iota(jnp.int32, shape, 1)
    wanted = jnp.where(row < rows, row + DMAX - dilation, row - rows + DMAX + dilation)
    return jnp.where(column == wanted, 1.0, 0.0).astype(BF16)


def conv_chain(r):
    ctx, head = me()
    j = chunk_of(ctx, head)
    rows, features, width = BLOCK, r.w_out.shape[1], r.conv.shape[3]
    owners = owner_stream()

    def beside(step):
        return member(ctx, head, (j + step + 8) % 8)

    def swap(n, edge, halo, pad, width):
        lead = pad.shape[:-2]
        edge[0] = pad[..., DMAX : 2 * DMAX, :]
        edge[1] = pad[..., rows : rows + DMAX, :]
        down = remote(edge.at[0], halo.at[1], r.h_send.at[2 * n], r.h_recv.at[2 * n], beside(-1))
        up = remote(edge.at[1], halo.at[0], r.h_send.at[2 * n + 1], r.h_recv.at[2 * n + 1], beside(1))

        @pl.when(j > 0)
        def _():
            down.start()

        @pl.when(j < 7)
        def _():
            up.start()

        def finish():
            @pl.when(j > 0)
            def _():
                up.wait_recv()
                pad[..., 0:DMAX, :] = halo[0]
                down.wait_send()

            @pl.when(j == 0)
            def _():
                pad[..., 0:DMAX, :] = jnp.zeros(lead + (DMAX, width), BF16)

            @pl.when(j < 7)
            def _():
                down.wait_recv()
                pad[..., rows + DMAX : rows + 2 * DMAX, :] = halo[1]
                up.wait_send()

            @pl.when(j == 7)
            def _():
                pad[..., rows + DMAX : rows + 2 * DMAX, :] = jnp.zeros(lead + (DMAX, width), BF16)

        return finish

    for name in ("w_out", "conv", "point"):
        fetch(r, name).wait()
    both = jnp.zeros((2 * rows, features), F32)
    for h in range(HEADS):
        both = both + dot(r.attended[h].reshape(2 * rows, VAL), r.w_out[h * VAL : (h + 1) * VAL, :], ((1,), (0,)))
    r.mixed[...] = r.home[...].reshape(rows, features).astype(F32) + both[:rows]
    r.tan[...] = both[rows:]
    for layer in range(2):
        dilation = r.dilations[layer]
        act, slope = gelu_pair(r.mixed[...])
        r.slope[layer] = slope
        r.pad[0, DMAX : DMAX + rows, :] = act.astype(BF16)
        r.pad[1, DMAX : DMAX + rows, :] = (slope * r.tan[...]).astype(BF16)
        finish = swap(layer, r.edge.at[layer], r.halo.at[layer], r.pad, features)
        inner = dot(r.pad[:, DMAX : DMAX + rows, :].reshape(2 * rows, features), r.conv[layer, 1], ((1,), (0,)))
        pick = picker(dilation, rows)
        finish()
        value = dot(pick, r.pad[0], ((1,), (0,))).astype(BF16)
        tangent = dot(pick, r.pad[1], ((1,), (0,))).astype(BF16)
        for n, tap in ((0, 0), (1, 2)):
            window = jnp.concatenate([value[n * rows : (n + 1) * rows], tangent[n * rows : (n + 1) * rows]], axis=0)
            inner = inner + dot(window, r.conv[layer, tap], ((1,), (0,)))
        hidden, hslope = gelu_pair(inner[:rows])
        r.hslope[layer] = hslope
        hidden = jnp.concatenate([hidden, hslope * inner[rows:]], axis=0).astype(BF16)
        point = dot(hidden, r.point[layer], ((1,), (0,)))
        if layer == 0:
            r.mixed[...] += point[:rows]
        r.tan[...] += point[rows:]
    r.out_buf[0] = r.tan[...].astype(BF16)
    for k in range(4):
        out_copy(r, 0, k, owners.slot, owners.dst(k)).start()
    for k in range(4):
        curve = r.c_home[k].T[:64, 0:1]
        at = slice(64 * k, 64 * k + 64)
        r.grad[at, :] = curve * r.tan[at, :]
    for layer in (1, 0):
        dilation = r.dilations[layer]
        back = dot(r.grad[...].astype(BF16), r.point[layer], ((1,), (1,)))
        r.gpad[DMAX : DMAX + rows, :] = (back * r.hslope[layer]).astype(BF16)
        finish = swap(2 + layer, r.gedge.at[layer], r.ghalo.at[layer], r.gpad, width)
        act = dot(r.gpad[DMAX : DMAX + rows, :], r.conv[layer, 1], ((1,), (1,)))
        pick = picker(dilation, rows)
        finish()
        windows = dot(pick, r.gpad[...], ((1,), (0,))).astype(BF16)
        act = act + dot(windows[:rows], r.conv[layer, 2], ((1,), (1,)))
        act = act + dot(windows[rows:], r.conv[layer, 0], ((1,), (1,)))
        r.grad[...] += r.slope[layer] * act
    final = r.grad[...].astype(BF16)

    def send(t, carry):
        i = (j + 1 + t) % 8
        part = r.w_out[pl.ds(pl.multiple_of(i * VAL, 32), VAL), :]
        ga = dot(final, part, ((1,), (1,))).astype(BF16)

        @pl.when(t < 7)
        def _():
            r.ga_buf[i] = ga
            remote(r.ga_buf.at[i], r.item.at[j], r.g_send.at[i], r.g_recv.at[j], member(ctx, head, i)).start()

        @pl.when(t == 7)
        def _():
            r.item[j] = ga

        return carry

    lax.fori_loop(0, 8, send, 0)


def out_copy(r, n, k, slot, target):
    out = (r.out_t, r.out_c)[n]
    return remote(
        r.out_buf.at[n, pl.ds(64 * k, 64)], out.at[slot], r.o_send.at[n, k], r.o_recv.at[n, slot], target
    )


def back(r):
    ctx, head = me()
    j = chunk_of(ctx, head)
    owners, rows, plane = owner_stream(), rows_stream(), plane_stream()
    length = 8 * BLOCK
    r.q[...] = r.qt[:, KEY:]
    r.acc[...] = jnp.zeros(r.acc.shape, F32)
    for c in range(8):
        at = slice(c * BLOCK, (c + 1) * BLOCK)
        r.kT[:, at] = (r.kt[at, :].astype(F32).T[:KEY] * SCALE).astype(BF16)

    def ga_end(t, carry):
        i = (j + 1 + t) % 8
        remote(r.ga_buf.at[i], r.item.at[i], r.g_send.at[i], r.g_recv.at[i], member(ctx, head, i)).wait()
        return carry

    lax.fori_loop(0, 7, ga_end, 0)
    for c in range(8):
        at = slice(c * BLOCK, (c + 1) * BLOCK)
        prod = r.item[c].astype(F32) * r.att[at, :VAL]
        prod = jnp.concatenate([prod, jnp.zeros((BLOCK, 128 - VAL), F32)], axis=1)
        r.delta[:, at] = jnp.broadcast_to(jnp.sum(prod.T, axis=0, keepdims=True), (8, BLOCK))

    def packed(a):
        return jnp.concatenate([a[: BLOCK // 2], a[BLOCK // 2 :]], axis=1)

    def deliver(buf, ref, send, recv, i, t, value):
        @pl.when(t < 7)
        def _():
            buf[i] = value
            remote(buf.at[i], ref.at[j], send.at[i], recv.at[j], member(ctx, head, i)).start()

        @pl.when(t == 7)
        def _():
            ref[j] = value

    def block(t, carry):
        i = (j + 1 + t) % 8
        at = pl.ds(pl.multiple_of(i * BLOCK, BLOCK), BLOCK)
        g = r.item[...].reshape(length, VAL)
        s = dot(r.kt[at, :KEY], r.q[...], ((1,), (1,)))
        w = jnp.exp(s - r.lse[0:1, :])
        dp = dot(r.v[at, :VAL], g, ((1,), (1,)))
        ds = (w * (dp - r.delta[0:1, :])).astype(BF16)
        dv = dot(w.astype(BF16), g, ((1,), (0,))).astype(BF16)
        deliver(r.dv_buf, r.dv, r.v_send, r.v_recv, i, t, dv)
        dk = packed(dot(ds, r.q[...], ((1,), (0,))))
        deliver(r.dk_buf, r.dk, r.k_send, r.k_recv, i, t, dk.astype(BF16))
        dkT = dk.T
        r.pairT[KEY:, at] = jnp.concatenate([dkT[:KEY], dkT[KEY:]], axis=1).astype(BF16)
        r.acc[...] += dot(r.kT[:, at], ds, ((1,), (0,)))
        return carry

    lax.fori_loop(0, 8, block, 0)

    def dq_out(t, carry):
        i = (j + 1 + t) % 8
        at = pl.ds(pl.multiple_of(i * BLOCK, BLOCK), BLOCK)
        part = r.acc[:, at]
        dq = jnp.concatenate([part[:, : BLOCK // 2], part[:, BLOCK // 2 :]], axis=0).T.astype(BF16)
        deliver(r.dq_buf, r.dq, r.q_send, r.q_recv, i, t, dq)
        return carry

    lax.fori_loop(0, 8, dq_out, 0)
    r.pairT[:KEY, :] = r.acc[...].astype(BF16)
    part = dot(r.pairT[...], r.normed[...].reshape(length, -1), ((1,), (0,)))
    r.part_buf[...] = part.T.reshape(r.part_buf.shape)
    r.part[plane.own] = r.part_buf[plane.own]

    def part_out(d, carry):
        k = (plane.own + d) % 32
        remote(r.part_buf.at[k], r.part.at[plane.slot], r.e_send.at[k], r.e_recv.at[plane.slot], plane.dst(k)).start()
        return carry

    lax.fori_loop(1, 32, part_out, 0)

    def group_end(t, carry):
        i = (j + 1 + t) % 8
        to = member(ctx, head, i)
        remote(r.dv_buf.at[i], r.dv.at[i], r.v_send.at[i], r.v_recv.at[i], to).wait()
        remote(r.dk_buf.at[i], r.dk.at[i], r.k_send.at[i], r.k_recv.at[i], to).wait()
        remote(r.dq_buf.at[i], r.dq.at[i], r.q_send.at[i], r.q_recv.at[i], to).wait()
        return carry

    lax.fori_loop(0, 7, group_end, 0)
    inputs = r.home[...].reshape(BLOCK, -1).astype(F32)
    count, features = inputs.shape
    acc = jnp.zeros((count, features), F32)
    for h in range(HEADS):
        w = jnp.concatenate([r.wq[:, h * KEY : (h + 1) * KEY], r.wk[:, h * KEY : (h + 1) * KEY]], axis=1)
        dq, dk = r.dq[h], r.dk[h]
        pair = jnp.concatenate(
            [
                jnp.concatenate([dq[:, :KEY], dk[:, :KEY]], axis=1),
                jnp.concatenate([dq[:, KEY:], dk[:, KEY:]], axis=1),
            ],
            axis=0,
        )
        acc = acc + dot(pair, w, ((1,), (1,)))
        acc = acc + dot(r.dv[h], r.wv[:, h * VAL : (h + 1) * VAL], ((1,), (1,)))
    gained = acc * r.gain[...].reshape(1, -1)
    spread = jnp.sqrt(jnp.mean(inputs * inputs, axis=-1, keepdims=True) + 1e-06)
    along = jnp.sum(gained * inputs, axis=-1, keepdims=True)
    inv = 1.0 / spread
    r.out_buf[1] = (
        r.grad[...] + gained * inv - inputs * (along / (features * spread * spread * spread))
    ).astype(BF16)
    for k in range(4):
        out_copy(r, 1, k, owners.slot, owners.dst(k)).start()

    def part_end(d, carry):
        k = (plane.own + d) % 32
        remote(r.part_buf.at[k], r.part.at[k], r.e_send.at[k], r.e_recv.at[k], plane.dst(k)).wait()
        return carry

    lax.fori_loop(1, 32, part_end, 0)
    summed = jnp.sum(r.part[...], axis=0) * (1.0 / (32.0 * 2048.0))
    for k in range(8):
        r.rows[k, 0:3, :] = summed[3 * k : 3 * k + 3, :]
        r.rows[k, 3:8, :] = jnp.zeros((5, 2 * KEY), F32)
    for k in range(8):
        remote(r.rows.at[k], r.got.at[rows.slot], r.r_send.at[k], r.r_recv.at[rows.slot], rows.dst(k)).start()
    for k in range(8):
        remote(r.rows.at[k], r.got.at[k], r.r_send.at[k], r.r_recv.at[k], rows.dst(k)).wait()
    for k in range(8):
        r.gvq[:, k * KEY : (k + 1) * KEY] = r.got[k, 0:3, :KEY]
        r.gvk[:, k * KEY : (k + 1) * KEY] = r.got[k, 0:3, KEY:]
    for n in range(2):
        for k in range(4):
            out_copy(r, n, k, k, owners.dst(k)).wait()


WEIGHTS = ("tq", "wq", "wk", "tk", "wv", "w_out", "conv", "point")


def fetch(r, name):
    n = WEIGHTS.index(name)
    return pltpu.make_async_copy(getattr(r, name + "_hbm"), getattr(r, name), r.w_sem.at[n])


def whole_kernel(names, *refs):
    r = Refs(names, refs)
    barrier = pltpu.get_barrier_semaphore()
    greet_all(r, barrier)
    for name in WEIGHTS:
        fetch(r, name).start()
    pl.semaphore_wait(barrier, 54)
    front(r)
    attend_forward(r)
    conv_chain(r)
    back(r)


def run(inputs, collective_id):
    by_name = {name: array for name, array, _ in inputs}
    features = by_name["x"].shape[2]
    width = by_name["conv_hbm"].shape[3]
    length = 8 * BLOCK
    rows = BLOCK
    vmem, dma = pltpu.VMEM, pltpu.SemaphoreType.DMA
    scratch = {name: vmem(by_name[name + "_hbm"].shape, BF16) for name in WEIGHTS}
    scratch.update(
        w_sem=dma((len(WEIGHTS),)),
        home=vmem((4, 64, features), BF16),
        c_buf=vmem((4, 8, 128), F32),
        c_home=vmem((4, 8, 128), F32),
        joined=vmem((features, 384), BF16),
        normed=vmem((8, rows, features), BF16),
        qt=vmem((length, 128), BF16),
        kt=vmem((length, 128), BF16),
        v=vmem((length, 128), BF16),
        att_buf=vmem((8, 2, rows, VAL), BF16),
        attended=vmem((8, 2, rows, VAL), BF16),
        att=vmem((length, 128), F32),
        lse=vmem((8, length), F32),
        mixed=vmem((rows, features), F32),
        tan=vmem((rows, features), F32),
        grad=vmem((rows, features), F32),
        slope=vmem((2, rows, features), F32),
        hslope=vmem((2, rows, width), F32),
        pad=vmem((2, rows + 2 * DMAX, features), BF16),
        gpad=vmem((rows + 2 * DMAX, width), BF16),
        edge=vmem((2, 2, 2, DMAX, features), BF16),
        halo=vmem((2, 2, 2, DMAX, features), BF16),
        gedge=vmem((2, 2, DMAX, width), BF16),
        ghalo=vmem((2, 2, DMAX, width), BF16),
        out_buf=vmem((2, rows, features), BF16),
        ga_buf=vmem((8, rows, VAL), BF16),
        item=vmem((8, rows, VAL), BF16),
        q=vmem((length, KEY), BF16),
        kT=vmem((KEY, length), BF16),
        delta=vmem((8, length), F32),
        acc=vmem((KEY, length), F32),
        pairT=vmem((2 * KEY, length), BF16),
        dv_buf=vmem((8, rows, VAL), BF16),
        dv=vmem((8, rows, VAL), BF16),
        dk_buf=vmem((8, rows // 2, 2 * KEY), BF16),
        dk=vmem((8, rows // 2, 2 * KEY), BF16),
        dq_buf=vmem((8, rows // 2, 2 * KEY), BF16),
        dq=vmem((8, rows // 2, 2 * KEY), BF16),
        part_buf=vmem((32, features // 32, 2 * KEY), F32),
        part=vmem((32, features // 32, 2 * KEY), F32),
        rows=vmem((8, 8, 2 * KEY), F32),
        got=vmem((8, 8, 2 * KEY), F32),
    )
    for name, shape in (
        ("x", (4,)),
        ("c", (4,)),
        ("n", (8, 4)),
        ("a", (8,)),
        ("h", (8,)),
        ("o", (2, 4)),
        ("g", (8,)),
        ("v", (8,)),
        ("k", (8,)),
        ("q", (8,)),
        ("e", (32,)),
        ("r", (8,)),
    ):
        scratch[name + "_send"] = dma(shape + (3,)) if name == "n" else dma(shape)
        scratch[name + "_recv"] = dma(shape)
    outs = ("out_t", "out_c", "gvq", "gvk")
    names = [name for name, _, _ in inputs] + list(outs) + list(scratch)
    return pl.pallas_call(
        functools.partial(whole_kernel, names),
        out_shape=[
            jax.ShapeDtypeStruct((4, 64, features), BF16),
            jax.ShapeDtypeStruct((4, 64, features), BF16),
            jax.ShapeDtypeStruct((3, HEADS * KEY), F32),
            jax.ShapeDtypeStruct((3, HEADS * KEY), F32),
        ],
        in_specs=[pl.BlockSpec(memory_space=space) for _, _, space in inputs],
        out_specs=[pl.BlockSpec(memory_space=space) for space in (pl.ANY, pl.ANY, vmem, vmem)],
        scratch_shapes=list(scratch.values()),
        compiler_params=pltpu.CompilerParams(
            collective_id=collective_id, has_side_effects=True, vmem_limit_bytes=VMEM_LIMIT
        ),
    )(*[array for _, array, _ in inputs])


def per_device(
    window_input,
    norm_gain,
    w_query,
    w_key,
    w_value,
    w_out,
    conv_weight,
    point_weight,
    dilations,
    tangent_query,
    tangent_key,
    curvature,
):
    return run(
        (
            ("dilations", dilations, pltpu.SMEM),
            ("x", window_input, pl.ANY),
            ("curvature", curvature, pltpu.VMEM),
            ("gain", norm_gain, pltpu.VMEM),
            ("tq_hbm", tangent_query, pl.ANY),
            ("wq_hbm", w_query, pl.ANY),
            ("wk_hbm", w_key, pl.ANY),
            ("tk_hbm", tangent_key, pl.ANY),
            ("wv_hbm", w_value, pl.ANY),
            ("w_out_hbm", w_out, pl.ANY),
            ("conv_hbm", conv_weight, pl.ANY),
            ("point_hbm", point_weight, pl.ANY),
        ),
        0,
    )


def solution(mesh):
    in_specs = (P("head", "ctx", None),) + (P(),) * 10 + (P("head", "ctx"),)
    out_specs = (
        P("head", "ctx", None),
        P("head", "ctx", None),
        P(("ctx", "head"), None),
        P(("ctx", "head"), None),
    )
    return jax.shard_map(per_device, mesh=mesh, in_specs=in_specs, out_specs=out_specs, check_vma=False)
```

time: 175 us -> 139 us (0.79)
  the two profiles are of different devices: /device:TPU:2 before, /device:TPU:17 now
where the time goes in v4:
time: 139 us
  Pallas kernels  134 us (96%)
  local copies, waits for them, and re-layouts  4.75 us (3%)
    pallas_call x1, Pallas kernels, run(): pl.pallas_call(functools.partial(whole_kernel, names), out_shape=[jax.Sha...  134 us
    unnamed x8, local copies, waits for them, and re-layouts  4.75 us

profile of v4, /device:TPU:17, one launch (start us, length us, event | category | flops | bytes accessed | tf_op | source)
XLA Modules:
  0.0 138.9 jit_solution(260662720484184658)
XLA Ops:
  0.6 133.5 %shard_map.147 = (bf16[4,64,768]{2,1,0:T(8,128)(2,1)}, bf16[4,64,768]{2,1,0:T(8,128)(2,1)}, f32[3,512]{1,0:T(4,128)}, f32[3,512]{1,0:T(4,128)}) custom-call(s32[2]{0:T(128)} %refs_0_.1, bf16[4,64,768]{2,1,0:T(8,128)(2,1)} %refs_1_.1, f32[4,64]{1,0:T(4,128)} %refs_2_.1, f32[768]{0:T(1024)} %refs_3_.1, bf16[768,512]{1,0:T(8,128)(2,1)} %refs_4_.1, ...), custom_call_target="tpu_custom_call" | custom-call | tf_op jit(solution)/shard_map/pallas_call | solution.py:646
  134.2 0.0 copy-start.1
  134.2 0.0 copy-start
  134.2 1.8 %copy.20 = bf16[4,64,768]{2,1,0:T(8,128)(2,1)} copy(bf16[4,64,768]{2,1,0:T(8,128)(2,1)} %get-tuple-element.8) | data formatting | bytes 786432
  136.0 1.8 %copy.21 = bf16[4,64,768]{2,1,0:T(8,128)(2,1)} copy(bf16[4,64,768]{2,1,0:T(8,128)(2,1)} %get-tuple-element.9) | data formatting | bytes 786432
  137.7 0.0 copy-done.1
  137.7 0.6 copy.22
  138.3 0.0 copy-done
  138.3 0.6 copy.23
Async XLA Ops:
  134.2 3.6 %copy-start.1 = (f32[3,512]{1,0:T(4,128)S(1)}, f32[3,512]{1,0:T(4,128)}, u32[]{:S(2)}) copy-start(f32[3,512]{1,0:T(4,128)} %get-tuple-element.10) | copy-start | bytes 18436
  134.2 4.2 %copy-start = (f32[3,512]{1,0:T(4,128)S(1)}, f32[3,512]{1,0:T(4,128)}, u32[]{:S(2)}) copy-start(f32[3,512]{1,0:T(4,128)} %get-tuple-element.11) | copy-start | bytes 18436

commit v5 on v4

--- a/solution.py
+++ b/solution.py
@@ -140,8 +140,15 @@
     homes = home_stream()
     sibling = j + 1 - 2 * core
     up, down, far = (j + 2) % 8, (j + 6) % 8, (j + 4) % 8
+
+    def block_copy(k, half, slot):
+        part = pl.ds(32 * half, 32)
+        return remote(
+            r.x.at[k, part], r.home.at[slot, part], r.x_send.at[half, k], r.x_recv.at[half, slot], homes.dst(k)
+        )
+
     for k in range(4):
-        remote(r.x.at[k], r.home.at[homes.slot], r.x_send.at[k], r.x_recv.at[homes.slot], homes.dst(k)).start()
+        block_copy(k, 0, homes.slot).start()
     for k in range(4):
         r.c_buf[k] = jnp.zeros((8, 128), F32)
         r.c_buf[k, 0:1, 0:64] = r.curvature[k : k + 1, :]
@@ -154,21 +161,15 @@
         hit = (row - j * size == column - at) & (column >= at) & (column < at + size)
         return dot(weight[...], jnp.where(hit, factor, 0.0).astype(BF16), ((1,), (0,)))
 
-    joined = None
-    for name, size, at, factor in (
-        ("tq", KEY, 0, SCALE),
-        ("wq", KEY, KEY, SCALE),
-        ("wk", KEY, 2 * KEY, 1.0),
-        ("tk", KEY, 3 * KEY, 1.0),
-        ("wv", VAL, 4 * KEY, 1.0),
-    ):
-        fetch(r, name).wait()
-        part = columns(getattr(r, name), size, at, factor)
-        joined = part if joined is None else joined + part
-    r.joined[...] = joined.astype(BF16)
+    def join(joined, names):
+        for name, size, at, factor in names:
+            fetch(r, name).wait()
+            part = columns(getattr(r, name), size, at, factor)
+            joined = part if joined is None else joined + part
+        return joined
 
     def piece(i, p):
-        return r.normed.at[i, pl.ds(64 * p, 64)]
+        return r.normed.at[i, pl.ds(p % 4 * 64 + p // 4 * 32, 32)]
 
     def push(i, p, way, to):
         remote(piece(i, p), piece(i, p), r.n_send.at[i, p, way], r.n_recv.at[i, p], member(ctx, head, to)).start()
@@ -182,14 +183,27 @@
         remote(piece(i, p), piece(i, p), r.n_send.at[i, p, way], r.n_recv.at[i, p], member(ctx, head, to)).wait_send()
 
     gain = r.gain[...].reshape(1, -1)
-    for p in range(4):
-        remote(r.x.at[p], r.home.at[p], r.x_send.at[p], r.x_recv.at[p], homes.dst(p)).wait_recv()
-        inputs = r.home[p].astype(F32)
+    def norm(p):
+        k, half = p % 4, p // 4
+        block_copy(k, half, k).wait_recv()
+        inputs = r.home[k, 32 * half : 32 * half + 32, :].astype(F32)
         spread = jnp.sqrt(jnp.mean(inputs * inputs, axis=-1, keepdims=True) + 1e-06)
-        r.normed[j, 64 * p : 64 * p + 64, :] = (inputs / spread * gain).astype(BF16)
+        at = 64 * k + 32 * half
+        r.normed[j, at : at + 32, :] = (inputs / spread * gain).astype(BF16)
         push(j, p, 1, up)
         push(j, p, 2, down)
         push(j, p, 0, sibling)
+
+    joined = join(None, (("tq", KEY, 0, SCALE), ("wq", KEY, KEY, SCALE)))
+    for k in range(4):
+        block_copy(k, 0, homes.slot).wait_send()
+        block_copy(k, 1, homes.slot).start()
+    for p in range(4):
+        norm(p)
+    joined = join(joined, (("wk", KEY, 2 * KEY, 1.0), ("tk", KEY, 3 * KEY, 1.0), ("wv", VAL, 4 * KEY, 1.0)))
+    r.joined[...] = joined.astype(BF16)
+    for p in range(4, 8):
+        norm(p)
 
     def project(i):
         rows = pl.ds(pl.multiple_of(i * BLOCK, BLOCK), BLOCK)
@@ -199,36 +213,41 @@
         lane = lax.broadcasted_iota(jnp.int32, (BLOCK, 128), 1)
         r.v[rows, :] = jnp.where(lane < VAL, proj[:, 256:].astype(F32), 1.0).astype(BF16)
 
-    for p in range(4):
+    project(j)
+    for p in range(8):
         arrived(down, p)
-        if p < 2:
+        if p % 2 == 0:
             push(down, p, 1, up)
         push(down, p, 0, sibling)
         arrived(up, p)
-        if p >= 2:
+        if p % 2 == 1:
             push(up, p, 2, down)
         push(up, p, 0, sibling)
-    project(j)
-    project(down)
-    project(up)
-    for p in (0, 2, 1, 3):
+    for p in range(8):
         arrived(far, p)
         push(far, p, 0, sibling)
+        if p == 3:
+            project(down)
+        if p == 5:
+            project(up)
+    for p in range(8):
+        arrived(sibling, p)
+    project(sibling)
     project(far)
-    for d in (0, 2, 6, 4):
+    for d in (2, 6, 4):
         i = (sibling + d) % 8
-        for p in range(4):
+        for p in range(8):
             arrived(i, p)
         project(i)
     for k in range(4):
-        remote(r.x.at[k], r.home.at[k], r.x_send.at[k], r.x_recv.at[k], homes.dst(k)).wait_send()
+        block_copy(k, 1, k).wait_send()
         remote(r.c_buf.at[k], r.c_home.at[k], r.c_send.at[k], r.c_recv.at[k], homes.dst(k)).wait()
-    for p in range(4):
+    for p in range(8):
         sent(j, p, 1, up)
         sent(j, p, 2, down)
         for i in (j, up, down, far):
             sent(i, p, 0, sibling)
-        if p < 2:
+        if p % 2 == 0:
             sent(down, p, 1, up)
         else:
             sent(up, p, 2, down)
@@ -289,12 +308,17 @@
     return v * half, half + 0.5 * v * (1.0 - t * t) * (root + (3.0 * 0.044715 * root) * square)
 
 
-def picker(dilation, rows):
-    shape = (2 * rows, rows + 2 * DMAX)
+def one_hot(shape, wanted):
+    column = lax.broadcasted_iota(jnp.int32, shape, 1)
+    return jnp.where(column == wanted, 1.0, 0.0).astype(BF16)
+
+
+def pickers(dilation, rows):
+    shape = (2 * rows, rows)
     row = lax.broadcasted_iota(jnp.int32, shape, 0)
-    column = lax.broadcasted_iota(jnp.int32, shape, 1)
-    wanted = jnp.where(row < rows, row + DMAX - dilation, row - rows + DMAX + dilation)
-    return jnp.where(column == wanted, 1.0, 0.0).astype(BF16)
+    own = one_hot(shape, jnp.where(row < rows, row - dilation, row - rows + dilation))
+    edge = lax.broadcasted_iota(jnp.int32, (DMAX, DMAX), 0)
+    return own, one_hot((DMAX, DMAX), edge + DMAX - dilation), one_hot((DMAX, DMAX), edge + dilation - DMAX)
 
 
 def conv_chain(r):
@@ -306,12 +330,12 @@
     def beside(step):
         return member(ctx, head, (j + step + 8) % 8)
 
-    def swap(n, edge, halo, pad, width):
-        lead = pad.shape[:-2]
-        edge[0] = pad[..., DMAX : 2 * DMAX, :]
-        edge[1] = pad[..., rows : rows + DMAX, :]
-        down = remote(edge.at[0], halo.at[1], r.h_send.at[2 * n], r.h_recv.at[2 * n], beside(-1))
-        up = remote(edge.at[1], halo.at[0], r.h_send.at[2 * n + 1], r.h_recv.at[2 * n + 1], beside(1))
+    def swap(n, cells, halo):
+        lead = (slice(None),) * (len(cells.shape) - 2)
+        first = cells.at[lead + (pl.ds(0, DMAX), slice(None))]
+        last = cells.at[lead + (pl.ds(rows - DMAX, DMAX), slice(None))]
+        down = remote(first, halo.at[1], r.h_send.at[2 * n], r.h_recv.at[2 * n], beside(-1))
+        up = remote(last, halo.at[0], r.h_send.at[2 * n + 1], r.h_recv.at[2 * n + 1], beside(1))
 
         @pl.when(j > 0)
         def _():
@@ -325,22 +349,20 @@
             @pl.when(j > 0)
             def _():
                 up.wait_recv()
-                pad[..., 0:DMAX, :] = halo[0]
                 down.wait_send()
 
             @pl.when(j == 0)
             def _():
-                pad[..., 0:DMAX, :] = jnp.zeros(lead + (DMAX, width), BF16)
+                halo[0] = jnp.zeros(halo.shape[1:], BF16)
 
             @pl.when(j < 7)
             def _():
                 down.wait_recv()
-                pad[..., rows + DMAX : rows + 2 * DMAX, :] = halo[1]
                 up.wait_send()
 
             @pl.when(j == 7)
             def _():
-                pad[..., rows + DMAX : rows + 2 * DMAX, :] = jnp.zeros(lead + (DMAX, width), BF16)
+                halo[1] = jnp.zeros(halo.shape[1:], BF16)
 
         return finish
 
@@ -355,20 +377,25 @@
         dilation = r.dilations[layer]
         act, slope = gelu_pair(r.mixed[...])
         r.slope[layer] = slope
-        r.pad[0, DMAX : DMAX + rows, :] = act.astype(BF16)
-        r.pad[1, DMAX : DMAX + rows, :] = (slope * r.tan[...]).astype(BF16)
-        finish = swap(layer, r.edge.at[layer], r.halo.at[layer], r.pad, features)
-        inner = dot(r.pad[:, DMAX : DMAX + rows, :].reshape(2 * rows, features), r.conv[layer, 1], ((1,), (0,)))
-        pick = picker(dilation, rows)
-        finish()
-        value = dot(pick, r.pad[0], ((1,), (0,))).astype(BF16)
-        tangent = dot(pick, r.pad[1], ((1,), (0,))).astype(BF16)
+        cells, halo, conv = r.act.at[layer], r.halo.at[layer], r.conv.at[layer]
+        cells[0] = act.astype(BF16)
+        cells[1] = (slope * r.tan[...]).astype(BF16)
+        finish = swap(layer, cells, halo)
+        inner = dot(cells[...].reshape(2 * rows, features), conv[1], ((1,), (0,)))
+        pick, pick_low, pick_high = pickers(dilation, rows)
+        value = dot(pick, cells[0], ((1,), (0,))).astype(BF16)
+        tangent = dot(pick, cells[1], ((1,), (0,))).astype(BF16)
         for n, tap in ((0, 0), (1, 2)):
             window = jnp.concatenate([value[n * rows : (n + 1) * rows], tangent[n * rows : (n + 1) * rows]], axis=0)
-            inner = inner + dot(window, r.conv[layer, tap], ((1,), (0,)))
-        hidden, hslope = gelu_pair(inner[:rows])
+            inner = inner + dot(window, conv[tap], ((1,), (0,)))
+        r.inner[...] = inner.reshape(2, rows, width)
+        finish()
+        for n, tap, pick, at in ((0, 0, pick_low, 0), (1, 2, pick_high, rows - DMAX)):
+            window = jnp.concatenate([dot(pick, halo[n, m], ((1,), (0,))).astype(BF16) for m in range(2)], axis=0)
+            r.inner[:, at : at + DMAX, :] += dot(window, conv[tap], ((1,), (0,))).reshape(2, DMAX, width)
+        hidden, hslope = gelu_pair(r.inner[0])
         r.hslope[layer] = hslope
-        hidden = jnp.concatenate([hidden, hslope * inner[rows:]], axis=0).astype(BF16)
+        hidden = jnp.concatenate([hidden, hslope * r.inner[1]], axis=0).astype(BF16)
         point = dot(hidden, r.point[layer], ((1,), (0,)))
         if layer == 0:
             r.mixed[...] += point[:rows]
@@ -383,15 +410,20 @@
     for layer in (1, 0):
         dilation = r.dilations[layer]
         back = dot(r.grad[...].astype(BF16), r.point[layer], ((1,), (1,)))
-        r.gpad[DMAX : DMAX + rows, :] = (back * r.hslope[layer]).astype(BF16)
-        finish = swap(2 + layer, r.gedge.at[layer], r.ghalo.at[layer], r.gpad, width)
-        act = dot(r.gpad[DMAX : DMAX + rows, :], r.conv[layer, 1], ((1,), (1,)))
-        pick = picker(dilation, rows)
+        cells, halo, conv = r.gact.at[layer], r.ghalo.at[layer], r.conv.at[layer]
+        cells[...] = (back * r.hslope[layer]).astype(BF16)
+        finish = swap(2 + layer, cells, halo)
+        act = dot(cells[...], conv[1], ((1,), (1,)))
+        pick, pick_low, pick_high = pickers(dilation, rows)
+        windows = dot(pick, cells[...], ((1,), (0,))).astype(BF16)
+        act = act + dot(windows[:rows], conv[2], ((1,), (1,)))
+        act = act + dot(windows[rows:], conv[0], ((1,), (1,)))
+        r.grad[...] += r.slope[layer] * act
         finish()
-        windows = dot(pick, r.gpad[...], ((1,), (0,))).astype(BF16)
-        act = act + dot(windows[:rows], r.conv[layer, 2], ((1,), (1,)))
-        act = act + dot(windows[rows:], r.conv[layer, 0], ((1,), (1,)))
-        r.grad[...] += r.slope[layer] * act
+        for n, tap, pick, at in ((0, 2, pick_low, 0), (1, 0, pick_high, rows - DMAX)):
+            window = dot(pick, halo[n], ((1,), (0,))).astype(BF16)
+            at = slice(at, at + DMAX)
+            r.grad[at, :] += r.slope[layer, at, :] * dot(window, conv[tap], ((1,), (1,)))
     final = r.grad[...].astype(BF16)
 
     def send(t, carry):
@@ -496,30 +528,35 @@
 
     lax.fori_loop(1, 32, part_out, 0)
 
-    def group_end(t, carry):
+    def early_end(t, carry):
         i = (j + 1 + t) % 8
         to = member(ctx, head, i)
         remote(r.dv_buf.at[i], r.dv.at[i], r.v_send.at[i], r.v_recv.at[i], to).wait()
         remote(r.dk_buf.at[i], r.dk.at[i], r.k_send.at[i], r.k_recv.at[i], to).wait()
-        remote(r.dq_buf.at[i], r.dq.at[i], r.q_send.at[i], r.q_recv.at[i], to).wait()
-        return carry
-
-    lax.fori_loop(0, 7, group_end, 0)
+        return carry
+
+    lax.fori_loop(0, 7, early_end, 0)
     inputs = r.home[...].reshape(BLOCK, -1).astype(F32)
     count, features = inputs.shape
+
+    def unpacked(a, b):
+        top = jnp.concatenate([a[:, :KEY], b[:, :KEY]], axis=1)
+        return jnp.concatenate([top, jnp.concatenate([a[:, KEY:], b[:, KEY:]], axis=1)], axis=0)
+
     acc = jnp.zeros((count, features), F32)
     for h in range(HEADS):
-        w = jnp.concatenate([r.wq[:, h * KEY : (h + 1) * KEY], r.wk[:, h * KEY : (h + 1) * KEY]], axis=1)
-        dq, dk = r.dq[h], r.dk[h]
-        pair = jnp.concatenate(
-            [
-                jnp.concatenate([dq[:, :KEY], dk[:, :KEY]], axis=1),
-                jnp.concatenate([dq[:, KEY:], dk[:, KEY:]], axis=1),
-            ],
-            axis=0,
-        )
-        acc = acc + dot(pair, w, ((1,), (1,)))
         acc = acc + dot(r.dv[h], r.wv[:, h * VAL : (h + 1) * VAL], ((1,), (1,)))
+    for h in range(0, HEADS, 2):
+        acc = acc + dot(unpacked(r.dk[h], r.dk[h + 1]), r.wk[:, h * KEY : (h + 2) * KEY], ((1,), (1,)))
+
+    def late_end(t, carry):
+        i = (j + 1 + t) % 8
+        remote(r.dq_buf.at[i], r.dq.at[i], r.q_send.at[i], r.q_recv.at[i], member(ctx, head, i)).wait()
+        return carry
+
+    lax.fori_loop(0, 7, late_end, 0)
+    for h in range(0, HEADS, 2):
+        acc = acc + dot(unpacked(r.dq[h], r.dq[h + 1]), r.wq[:, h * KEY : (h + 2) * KEY], ((1,), (1,)))
     gained = acc * r.gain[...].reshape(1, -1)
     spread = jnp.sqrt(jnp.mean(inputs * inputs, axis=-1, keepdims=True) + 1e-06)
     along = jnp.sum(gained * inputs, axis=-1, keepdims=True)
@@ -600,11 +637,10 @@
         grad=vmem((rows, features), F32),
         slope=vmem((2, rows, features), F32),
         hslope=vmem((2, rows, width), F32),
-        pad=vmem((2, rows + 2 * DMAX, features), BF16),
-        gpad=vmem((rows + 2 * DMAX, width), BF16),
-        edge=vmem((2, 2, 2, DMAX, features), BF16),
+        act=vmem((2, 2, rows, features), BF16),
+        inner=vmem((2, rows, width), F32),
         halo=vmem((2, 2, 2, DMAX, features), BF16),
-        gedge=vmem((2, 2, DMAX, width), BF16),
+        gact=vmem((2, rows, width), BF16),
         ghalo=vmem((2, 2, DMAX, width), BF16),
         out_buf=vmem((2, rows, features), BF16),
         ga_buf=vmem((8, rows, VAL), BF16),
@@ -626,9 +662,9 @@
         got=vmem((8, 8, 2 * KEY), F32),
     )
     for name, shape in (
-        ("x", (4,)),
+        ("x", (2, 4)),
         ("c", (4,)),
-        ("n", (8, 4)),
+        ("n", (8, 8)),
         ("a", (8,)),
         ("h", (8,)),
         ("o", (2, 4)),
@@ -660,6 +696,21 @@
     )(*[array for _, array, _ in inputs])
 
 
+def deliver_kernel(*refs):
+    count = len(refs) // 2
+    for n in range(count):
+        refs[count + n][...] = refs[n][...]
+
+
+def deliver_all(arrays):
+    return pl.pallas_call(
+        deliver_kernel,
+        out_shape=[jax.ShapeDtypeStruct(a.shape, a.dtype) for a in arrays],
+        in_specs=[pl.BlockSpec(memory_space=pltpu.VMEM)] * len(arrays),
+        out_specs=[pl.BlockSpec(memory_space=pltpu.VMEM)] * len(arrays),
+    )(*arrays)
+
+
 def per_device(
     window_input,
     norm_gain,
@@ -674,7 +725,7 @@
     tangent_key,
     curvature,
 ):
-    return run(
+    outs = run(
         (
             ("dilations", dilations, pltpu.SMEM),
             ("x", window_input, pl.ANY),
@@ -691,6 +742,7 @@
         ),
         0,
     )
+    return tuple(deliver_all(outs))
 
 
 def solution(mesh):

time: 139 us -> 130 us (0.935)
  the two profiles are of different devices: /device:TPU:17 before, /device:TPU:25 now
where the time goes in v5:
time: 130 us
  Pallas kernels  129 us (99%)
    pallas_call x1, Pallas kernels, run(): pl.pallas_call(functools.partial(whole_kernel, names), out_shape=[jax.Sha...  127 us

profile of v5, /device:TPU:25, one launch (start us, length us, event | category | flops | bytes accessed | tf_op | source)
XLA Modules:
  0.0 129.9 jit_solution(1488126490452701333)
XLA Ops:
  0.6 127.2 %shard_map.147 = (bf16[4,64,768]{2,1,0:T(8,128)(2,1)}, bf16[4,64,768]{2,1,0:T(8,128)(2,1)}, f32[3,512]{1,0:T(4,128)}, f32[3,512]{1,0:T(4,128)}) custom-call(s32[2]{0:T(128)} %refs_0_.1, bf16[4,64,768]{2,1,0:T(8,128)(2,1)} %refs_1_.1, f32[4,64]{1,0:T(4,128)} %refs_2_.1, f32[768]{0:T(1024)} %refs_3_.1, bf16[768,512]{1,0:T(8,128)(2,1)} %refs_4_.1, ...), custom_call_target="tpu_custom_call" | custom-call | tf_op jit(solution)/shard_map/pallas_call | solution.py:682
  127.8 2.0 %shard_map.148 = (bf16[4,64,768]{2,1,0:T(8,128)(2,1)}, bf16[4,64,768]{2,1,0:T(8,128)(2,1)}, f32[3,512]{1,0:T(4,128)}, f32[3,512]{1,0:T(4,128)}) custom-call(bf16[4,64,768]{2,1,0:T(8,128)(2,1)} %get-tuple-element.8.refs_0_, bf16[4,64,768]{2,1,0:T(8,128)(2,1)} %get-tuple-element.9.refs_1_, f32[3,512]{1,0:T(4,128)} %get-tuple-element.10.refs_2_, ...), custom_call_target="tpu_custom_call" | custom-call | tf_op jit(solution)/shard_map/pallas_call | solution.py:706

commit v6 on v5

--- a/solution.py
+++ b/solution.py
@@ -82,15 +82,25 @@
     )
 
 
-def plane_stream():
+def line_stream():
     ctx, head = me()
     y, z, x, core = place(ctx, head)
 
-    def at(r):
-        return device(y, r // 4 % 2 * 4 + r // 8, (r + 3) % 4, core)
-
-    rank = z % 4 * 8 + z // 4 * 4 + (x + 1) % 4
-    return Stream(32, at, at, rank, rank)
+    def at(i):
+        return device(y, z, (i + 3) % 4, core)
+
+    return Stream(4, at, at, (x + 1) % 4, (x + 1) % 4)
+
+
+def column_stream():
+    ctx, head = me()
+    y, z, x, core = place(ctx, head)
+
+    def at(m):
+        return device(y, m % 2 * 4 + m // 2, x, core)
+
+    rank = z % 4 * 2 + z // 4
+    return Stream(8, at, at, rank, rank)
 
 
 def rows_stream():
@@ -117,20 +127,18 @@
 def greet_all(r, barrier):
     ctx, head = me()
     j = chunk_of(ctx, head)
-    homes, owners, rows, plane = home_stream(), owner_stream(), rows_stream(), plane_stream()
+    homes, owners, rows = home_stream(), owner_stream(), rows_stream()
+    line, column = line_stream(), column_stream()
     for k in range(4):
         signal(barrier, homes.src(k))
         signal(barrier, owners.src(k))
     for d in range(1, 8):
         signal(barrier, member(ctx, head, (j + d) % 8))
+        signal(barrier, column.src((column.own + d) % 8))
+    for d in range(1, 4):
+        signal(barrier, line.src((line.own + d) % 4))
     for k in range(8):
         signal(barrier, rows.src(k))
-
-    def greet(d, carry):
-        signal(barrier, plane.src((plane.own + d) % 32))
-        return carry
-
-    lax.fori_loop(1, 32, greet, 0)
 
 
 def front(r):
@@ -202,6 +210,8 @@
         norm(p)
     joined = join(joined, (("wk", KEY, 2 * KEY, 1.0), ("tk", KEY, 3 * KEY, 1.0), ("wv", VAL, 4 * KEY, 1.0)))
     r.joined[...] = joined.astype(BF16)
+    for name in WEIGHTS[5:]:
+        fetch(r, name).start()
     for p in range(4, 8):
         norm(p)
 
@@ -455,7 +465,7 @@
 def back(r):
     ctx, head = me()
     j = chunk_of(ctx, head)
-    owners, rows, plane = owner_stream(), rows_stream(), plane_stream()
+    owners, rows, line, column = owner_stream(), rows_stream(), line_stream(), column_stream()
     length = 8 * BLOCK
     r.q[...] = r.qt[:, KEY:]
     r.acc[...] = jnp.zeros(r.acc.shape, F32)
@@ -518,15 +528,30 @@
     lax.fori_loop(0, 8, dq_out, 0)
     r.pairT[:KEY, :] = r.acc[...].astype(BF16)
     part = dot(r.pairT[...], r.normed[...].reshape(length, -1), ((1,), (0,)))
-    r.part_buf[...] = part.T.reshape(r.part_buf.shape)
-    r.part[plane.own] = r.part_buf[plane.own]
-
-    def part_out(d, carry):
-        k = (plane.own + d) % 32
-        remote(r.part_buf.at[k], r.part.at[plane.slot], r.e_send.at[k], r.e_recv.at[plane.slot], plane.dst(k)).start()
-        return carry
-
-    lax.fori_loop(1, 32, part_out, 0)
+    part = part.T
+    size = part.shape[0] // 32
+    for m in range(8):
+        for i in range(4):
+            n = 4 * m + i
+            r.part_buf[i, m] = part[n * size : (n + 1) * size]
+    r.part[line.own] = r.part_buf[line.own]
+
+    def line_copy(d, slot):
+        i = (line.own + d) % 4
+        return remote(
+            r.part_buf.at[i], r.part.at[i if slot is None else slot], r.e_send.at[i], r.e_recv.at[i if slot is None else slot],
+            line.dst(i),
+        )
+
+    def column_copy(d, slot):
+        m = (column.own + d) % 8
+        return remote(
+            r.half_buf.at[m], r.half.at[m if slot is None else slot], r.f_send.at[m], r.f_recv.at[m if slot is None else slot],
+            column.dst(m),
+        )
+
+    for d in range(1, 4):
+        line_copy(d, line.own).start()
 
     def early_end(t, carry):
         i = (j + 1 + t) % 8
@@ -557,23 +582,26 @@
     lax.fori_loop(0, 7, late_end, 0)
     for h in range(0, HEADS, 2):
         acc = acc + dot(unpacked(r.dq[h], r.dq[h + 1]), r.wq[:, h * KEY : (h + 2) * KEY], ((1,), (1,)))
-    gained = acc * r.gain[...].reshape(1, -1)
-    spread = jnp.sqrt(jnp.mean(inputs * inputs, axis=-1, keepdims=True) + 1e-06)
-    along = jnp.sum(gained * inputs, axis=-1, keepdims=True)
-    inv = 1.0 / spread
-    r.out_buf[1] = (
-        r.grad[...] + gained * inv - inputs * (along / (features * spread * spread * spread))
-    ).astype(BF16)
+    for d in range(1, 4):
+        line_copy(d, None).wait()
+    r.half_buf[...] = jnp.sum(r.part[...], axis=0)
+    for d in range(1, 8):
+        column_copy(d, column.own).start()
+    r.half[column.own] = r.half_buf[column.own]
+    gain = r.gain[...].reshape(1, -1)
     for k in range(4):
+        at = slice(64 * k, 64 * k + 64)
+        part_in = inputs[at]
+        gained = acc[at] * gain
+        spread = jnp.sqrt(jnp.mean(part_in * part_in, axis=-1, keepdims=True) + 1e-06)
+        along = jnp.sum(gained * part_in, axis=-1, keepdims=True)
+        r.out_buf[1, at, :] = (
+            r.grad[at, :] + gained * (1.0 / spread) - part_in * (along / (features * spread * spread * spread))
+        ).astype(BF16)
         out_copy(r, 1, k, owners.slot, owners.dst(k)).start()
-
-    def part_end(d, carry):
-        k = (plane.own + d) % 32
-        remote(r.part_buf.at[k], r.part.at[k], r.e_send.at[k], r.e_recv.at[k], plane.dst(k)).wait()
-        return carry
-
-    lax.fori_loop(1, 32, part_end, 0)
-    summed = jnp.sum(r.part[...], axis=0) * (1.0 / (32.0 * 2048.0))
+    for d in range(1, 8):
+        column_copy(d, None).wait()
+    summed = jnp.sum(r.half[...], axis=0) * (1.0 / (32.0 * 2048.0))
     for k in range(8):
         r.rows[k, 0:3, :] = summed[3 * k : 3 * k + 3, :]
         r.rows[k, 3:8, :] = jnp.zeros((5, 2 * KEY), F32)
@@ -601,9 +629,9 @@
     r = Refs(names, refs)
     barrier = pltpu.get_barrier_semaphore()
     greet_all(r, barrier)
-    for name in WEIGHTS:
+    for name in WEIGHTS[:5]:
         fetch(r, name).start()
-    pl.semaphore_wait(barrier, 54)
+    pl.semaphore_wait(barrier, 33)
     front(r)
     attend_forward(r)
     conv_chain(r)
@@ -656,8 +684,10 @@
         dk=vmem((8, rows // 2, 2 * KEY), BF16),
         dq_buf=vmem((8, rows // 2, 2 * KEY), BF16),
         dq=vmem((8, rows // 2, 2 * KEY), BF16),
-        part_buf=vmem((32, features // 32, 2 * KEY), F32),
-        part=vmem((32, features // 32, 2 * KEY), F32),
+        part_buf=vmem((4, 8, features // 32, 2 * KEY), F32),
+        part=vmem((4, 8, features // 32, 2 * KEY), F32),
+        half_buf=vmem((8, features // 32, 2 * KEY), F32),
+        half=vmem((8, features // 32, 2 * KEY), F32),
         rows=vmem((8, 8, 2 * KEY), F32),
         got=vmem((8, 8, 2 * KEY), F32),
     )
@@ -672,7 +702,8 @@
         ("v", (8,)),
         ("k", (8,)),
         ("q", (8,)),
-        ("e", (32,)),
+        ("e", (4,)),
+        ("f", (8,)),
         ("r", (8,)),
     ):
         scratch[name + "_send"] = dma(shape + (3,)) if name == "n" else dma(shape)

time: 130 us -> 128 us (0.985)
  the two profiles are of different devices: /device:TPU:25 before, /device:TPU:2 now
where the time goes in v6:
time: 128 us; the launch traced here: 125 us
  Pallas kernels  125 us (98%)
    pallas_call x1, Pallas kernels, run(): pl.pallas_call(functools.partial(whole_kernel, names), out_shape=[jax.Sha...  123 us

profile of v6, /device:TPU:2, one launch (start us, length us, event | category | flops | bytes accessed | tf_op | source)
XLA Modules:
  0.0 125.4 jit_solution(8317472140500649034)
XLA Ops:
  0.6 122.7 %shard_map.147 = (bf16[4,64,768]{2,1,0:T(8,128)(2,1)}, bf16[4,64,768]{2,1,0:T(8,128)(2,1)}, f32[3,512]{1,0:T(4,128)}, f32[3,512]{1,0:T(4,128)}) custom-call(s32[2]{0:T(128)} %refs_0_.1, bf16[4,64,768]{2,1,0:T(8,128)(2,1)} %refs_1_.1, f32[4,64]{1,0:T(4,128)} %refs_2_.1, f32[768]{0:T(1024)} %refs_3_.1, bf16[768,512]{1,0:T(8,128)(2,1)} %refs_4_.1, ...), custom_call_target="tpu_custom_call" | custom-call | tf_op jit(solution)/shard_map/pallas_call | solution.py:713
  123.4 2.0 %shard_map.148 = (bf16[4,64,768]{2,1,0:T(8,128)(2,1)}, bf16[4,64,768]{2,1,0:T(8,128)(2,1)}, f32[3,512]{1,0:T(4,128)}, f32[3,512]{1,0:T(4,128)}) custom-call(bf16[4,64,768]{2,1,0:T(8,128)(2,1)} %get-tuple-element.8.refs_0_, bf16[4,64,768]{2,1,0:T(8,128)(2,1)} %get-tuple-element.9.refs_1_, f32[3,512]{1,0:T(4,128)} %get-tuple-element.10.refs_2_, ...), custom_call_target="tpu_custom_call" | custom-call | tf_op jit(solution)/shard_map/pallas_call | solution.py:737
